TPU v7x, 256 devices: a whole 4x4x8 slice. The times are simulated.
256 devices in a mesh: seq: 32 (over x, y, core), clip: 8 (over z).
Axes of the slice: x: 4, y: 4, z: 8, core: 2. Of those that a mesh axis runs over, the one named last changes fastest.
Arguments:
- tokens: bfloat16 [32, 128, 64, 192], P('clip', None, 'seq'), may hold values from -6 to 6
- conv_one: bfloat16 [3, 3, 3, 192, 192], replicated, may hold values from -0.078125 to 0.078125
- conv_two: bfloat16 [3, 3, 3, 192, 96], replicated, may hold values from -0.078125 to 0.078125
- pixel_grad: bfloat16 [32, 256, 128, 96], P('clip', 'seq'), may hold values from -6 to 6
Outputs:
- decoded: bfloat16 [32, 256, 128, 96], P('clip', 'seq')
- token_grad: bfloat16 [32, 128, 64, 192], P('clip', None, 'seq')
All inputs are finite; a program needn't handle non-finite values.
Results may differ from a plain program's by a relative error of at most 0.0052.
Values may be sent and summed in bfloat16 or wider, within the bound.
No kernel may reach another device: no remote copies, remote signals or barrier semaphores. Data moves between devices by JAX's collectives and lax.ppermute only.
A program may use at most 64 MiB of HBM per device.

v0:
```python
import jax
import jax.numpy as jnp
from jax import lax
from jax.sharding import PartitionSpec as P

GROUPS = 32


def shifted(block, axis, distance):
    devices = range(lax.axis_size(axis))
    route = [(i - distance, i) for i in devices if i - distance in devices]
    return lax.ppermute(block, axis, route)


def padded_2(array, sides, width):
    for axis, dim in sides:
        peers, length = (lax.axis_size(axis), array.shape[dim])
        up = [(i, (i + 1) % peers) for i in range(peers - 1)]
        down = [(j, i) for i, j in up]
        last = lax.slice_in_dim(array, length - width, length, axis=dim)
        initial = lax.slice_in_dim(array, 0, width, axis=dim)
        before = lax.ppermute(last, axis, up)
        after = lax.ppermute(initial, axis, down)
        array = jnp.concatenate([before, array, after], axis=dim)
    return array


def causal_conv(padded, kernel, frames):
    rows = padded.shape[1] - 2
    cols = padded.shape[2] - 2
    chans = padded.shape[3]
    outs = kernel.shape[4]
    flat_kernel = kernel.reshape(3, 3, 3 * chans, outs)

    def one_frame(start):
        window = lax.dynamic_slice_in_dim(padded, start, 3, 0)
        stacked = jnp.concatenate(
            [window[:, :, 0:cols], window[:, :, 1 : cols + 1], window[:, :, 2 : cols + 2]], axis=-1
        )
        running = jnp.zeros((rows * cols, outs), jnp.float32)
        for tap_time in range(3):
            for tap_row in range(3):
                piece = stacked[tap_time, tap_row : tap_row + rows].reshape(rows * cols, 3 * chans)
                running = running + jnp.dot(
                    piece, flat_kernel[tap_time, tap_row], preferred_element_type=jnp.float32
                )
        return running.reshape(rows, cols, outs)

    return lax.map(one_frame, jnp.arange(frames, dtype=jnp.int32))


def flipped(kernel):
    return jnp.swapaxes(kernel[::-1, ::-1, ::-1], 3, 4)


def grouped(field):
    shape = field.shape
    return field.reshape(shape[0], shape[1], shape[2], GROUPS, shape[3] // GROUPS)


def pad_columns(field):
    return jnp.pad(field, ((0, 0), (0, 0), (1, 1), (0, 0)))


def body(tokens, conv_one, conv_two, pixel_grad):
    frames = tokens.shape[0]
    tile = lax.all_to_all(tokens, "seq", split_axis=1, concat_axis=2, tiled=True)
    values = grouped(tile.astype(jnp.float32))
    count = float(
        values.shape[0]
        * values.shape[1]
        * values.shape[2]
        * values.shape[4]
        * lax.axis_size("seq")
        * lax.axis_size("clip")
    )
    mean = lax.psum(jnp.sum(values, axis=(0, 1, 2, 4), keepdims=True), ("seq", "clip")) / count
    spread = lax.psum(
        jnp.sum((values - mean) ** 2, axis=(0, 1, 2, 4), keepdims=True), ("seq", "clip")
    )
    var = spread / count
    rscale = lax.rsqrt(var + 1e-06)
    normed = (values - mean) * rscale
    act = jax.nn.silu(normed).reshape(tile.shape).astype(jnp.bfloat16)
    earlier = shifted(act[-2:], "clip", 1)
    widened = padded_2(jnp.concatenate([earlier, act], axis=0), (("seq", 1),), 1)
    mid = (tile.astype(jnp.float32) + causal_conv(pad_columns(widened), conv_one, frames)).astype(
        jnp.bfloat16
    )
    upper = jnp.repeat(jnp.repeat(mid, 2, axis=1), 2, axis=2)
    earlier_up = shifted(upper[-2:], "clip", 1)
    padded_up = padded_2(jnp.concatenate([earlier_up, upper], axis=0), (("seq", 1),), 1)
    decoded = causal_conv(pad_columns(padded_up), conv_two, frames).astype(jnp.bfloat16)
    later = shifted(pixel_grad[:2], "clip", -1)
    grad_wide = padded_2(jnp.concatenate([pixel_grad, later], axis=0), (("seq", 1),), 1)
    up_grad = causal_conv(pad_columns(grad_wide), flipped(conv_two), frames)
    shape = mid.shape
    mid_grad = (
        up_grad.reshape(shape[0], shape[1], 2, shape[2], 2, shape[3])
        .sum(axis=(2, 4))
        .astype(jnp.bfloat16)
    )
    later_mid = shifted(mid_grad[:2], "clip", -1)
    mid_grad_wide = padded_2(jnp.concatenate([mid_grad, later_mid], axis=0), (("seq", 1),), 1)
    act_grad = grouped(causal_conv(pad_columns(mid_grad_wide), flipped(conv_one), frames))
    sigmoid = jax.nn.sigmoid(normed)
    norm_grad = act_grad * sigmoid * (1.0 + normed * (1.0 - sigmoid))
    first_sum, second_sum = lax.psum(
        (
            jnp.sum(norm_grad, axis=(0, 1, 2, 4), keepdims=True),
            jnp.sum(norm_grad * normed, axis=(0, 1, 2, 4), keepdims=True),
        ),
        ("seq", "clip"),
    )
    back = ((norm_grad - first_sum / count - normed * (second_sum / count)) * rscale).reshape(
        tile.shape
    )
    tile_grad = (mid_grad.astype(jnp.float32) + back).astype(jnp.bfloat16)
    token_grad = lax.all_to_all(tile_grad, "seq", split_axis=2, concat_axis=1, tiled=True)
    return (decoded, token_grad)


def solution(mesh):
    return jax.shard_map(
        body,
        mesh=mesh,
        in_specs=(P("clip", None, "seq", None), P(), P(), P("clip", "seq", None, None)),
        out_specs=(P("clip", "seq", None, None), P("clip", None, "seq", None)),
        check_vma=False,
    )
```

profile of v0, /device:TPU:1, one launch (start us, length us, event | category | flops | bytes accessed | tf_op | source)
XLA Modules:
  0.0 589.4 jit_solution(16142029270963551795)
XLA Ops:
  2.9 8.6 %all-to-all-start = ((bf16[4,128,2,192]{3,0,2,1:T(4,128)(2,1)}), bf16[4,128,2,192]{3,0,2,1:T(4,128)(2,1)S(1)}, u32[]{:S(2)}, u32[]{:S(2)}) async-start(bf16[4,128,2,192]{3,0,2,1:T(4,128)(2,1)} %copy.88), calls=%async_computation | async-start | bytes 1048576 | tf_op jit(solution)/shard_map/all_to_all | solution.py:67
  22.5 5.8 copy.105
  28.8 82.6 %psum.28 = f32[1,1,1,32,1]{3,4,2,1,0:T(1,128)S(1)} all-reduce(f32[1,1,1,32,1]{3,4,2,1,0:T(1,128)S(1)} %bitcast.525), channel_id=1, replica_groups=mesh['seq'=32,'clip'=8] {'seq','clip'}, use_global_device_ids=true, to_apply=%region_2.0 | all-reduce | flops 32 | bytes 256 | tf_op jit(solution)/shard_map/psum | solution.py:77
  121.4 2.9 select_maximum_fusion
  124.3 44.4 %while.42 = (s32[]{:T(128)}, f32[4,8,128,192]{2,1,3,0:T(8,128)}, s32[4]{0:T(128)S(1)}, bf16[6,10,130,96]{3,2,1,0:T(8,128)(2,1)S(1)}, bf16[3,3,288,192]{3,2,1,0:T...) while((s32[]{:T(128)}, f32[4,8,128,192]{2,1,3,0:T(8,128)}, s32[4]{0:T(128)S(1)}, ...), condition=%wide.region_11.12_spmd, body=%wide.region_10.11_spmd.sunk | while | flops 1027424256 | bytes 44384952 | solution.py:49
  168.7 4.2 copy.103
  172.9 3.6 reduce_sum.66
  178.9 77.8 %psum.29 = f32[1,1,1,32,1]{3,4,2,1,0:T(1,128)S(1)} all-reduce(f32[1,1,1,32,1]{3,4,2,1,0:T(1,128)S(1)} %bitcast.526), channel_id=1, replica_groups=mesh['seq'=32,'clip'=8] {'seq','clip'}, use_global_device_ids=true, to_apply=%region_5.6 | all-reduce | flops 32 | bytes 256 | tf_op jit(solution)/shard_map/psum | solution.py:78
  259.9 3.1 collective-permute-start.11
  267.2 2.8 select_maximum_fusion.2
  270.0 39.0 %while.43 = (s32[]{:T(128)}, f32[4,4,64,192]{3,2,1,0:T(8,128)}, s32[4]{0:T(128)S(1)}, bf16[6,6,66,192]{3,2,1,0:T(8,128)(2,1)}, bf16[3,3,576,192]{3,2,1,0:T(8,128...) while((s32[]{:T(128)}, f32[4,4,64,192]{3,2,1,0:T(8,128)}, s32[4]{0:T(128)S(1)}, ...), condition=%wide.region_14.15_spmd, body=%wide.region_13.14_spmd.sunk | while | flops 513982464 | bytes 20415160 | solution.py:49
  311.7 76.1 %all-reduce.4 = (f32[1,1,1,32,1]{3,4,2,1,0:T(1,128)S(1)}, f32[1,1,1,32,1]{3,4,2,1,0:T(1,128)S(1)}) all-reduce(f32[1,1,1,32,1]{3,4,2,1,0:T(1,128)S(1)} %bitcast.524, f32[1,1,1,32,1]{3,4,2,1,0:T(1,128)S(1)} %bitcast.523), channel_id=1, replica_groups=mesh['seq'=32,'clip'=8] {'seq','clip'}, use_global_device_ids=true, to_apply=%region_20.21 | all-reduce | flops 64 | bytes 512 | tf_op jit(solution)/shard_map/psum | solution.py:108
  390.9 3.8 collective-permute-start
  394.7 4.9 collective-permute-done
  400.4 3.9 collective-permute-start.1
  407.2 4.4 collective-permute-done.2
  411.6 2.8 select_maximum_fusion.5
  414.4 39.6 %while.40 = (s32[]{:T(128)}, f32[4,4,64,192]{3,1,2,0:T(4,128)}, s32[4]{0:T(128)S(1)}, bf16[6,6,66,192]{3,2,1,0:T(8,128)(2,1)}, bf16[3,3,576,192]{3,2,1,0:T(8,128...) while((s32[]{:T(128)}, f32[4,4,64,192]{3,1,2,0:T(4,128)}, s32[4]{0:T(128)S(1)}, ...), condition=%wide.region_7.8_spmd, body=%wide.region_6.7_spmd.sunk | while | flops 513982464 | bytes 20415160 | solution.py:49
  457.9 5.1 collective-permute-start.3
  464.2 8.5 %all-to-all-start.1 = ((bf16[4,4,64,192]{3,1,0,2:T(4,128)(2,1)}), bf16[4,4,64,192]{3,1,0,2:T(4,128)(2,1)}, u32[]{:S(2)}, u32[]{:S(2)}) async-start(bf16[4,4,64,192]{3,1,0,2:T(4,128)(2,1)} %copy.106), calls=%async_computation.1 | async-start | bytes 1048576 | tf_op jit(solution)/shard_map/all_to_all | solution.py:119
  479.4 2.9 fusion.87
  482.3 2.8 copy.95
  485.1 5.6 collective-permute-start.4
  490.7 2.8 copy.96
  502.0 4.8 copy.97
  509.0 3.6 copy.124
  512.6 6.6 %pad.16.clone = bf16[6,10,130,192]{3,2,1,0:T(8,128)(2,1)} pad(bf16[6,10,128,192]{3,2,1,0:T(8,128)(2,1)} %copy.124, bf16[]{:T(256)} %constant.59.clone.1), padding=0_0x0_0x1_1x0_0 | pad | bytes 5944322 | tf_op jit(solution)/shard_map/jit(_pad)/pad | solution.py:62
  519.2 69.1 %while.41 = (s32[]{:T(128)}, bf16[4,8,128,96]{2,3,1,0:T(8,128)(2,1)S(1)}, s32[4]{0:T(128)S(1)}, bf16[6,10,130,192]{3,2,1,0:T(8,128)(2,1)}, bf16[3,3,576,96]{3,2,...) while((s32[]{:T(128)}, bf16[4,8,128,96]{2,3,1,0:T(8,128)(2,1)S(1)}, ...), condition=%wide.region_9.10_spmd, body=%wide.region_8.9_spmd.sunk | while | flops 1033371648 | bytes 59326652 | solution.py:49
  521.7 5.2 constant_dynamic-slice_fusion.17
  539.0 5.2 constant_dynamic-slice_fusion.17
  556.3 5.2 constant_dynamic-slice_fusion.17
  573.6 5.2 constant_dynamic-slice_fusion.17
  (347 shorter events, 205.4 us)
Async XLA Ops:
  0.6 10.9 %copy-start.12 = (bf16[4,8,128,96]{2,3,1,0:T(8,128)(2,1)S(1)}, bf16[4,8,128,96]{2,3,1,0:T(8,128)(2,1)}, u32[]{:S(2)}) copy-start(bf16[4,8,128,96]{2,3,1,0:T(8,128)(2,1)} %param.15) | copy-start | bytes 2359300
  2.9 25.4 %all-to-all-start = ((bf16[4,128,2,192]{3,0,2,1:T(4,128)(2,1)}), bf16[4,128,2,192]{3,0,2,1:T(4,128)(2,1)S(1)}, u32[]{:S(2)}, u32[]{:S(2)}) async-start(bf16[4,128,2,192]{3,0,2,1:T(4,128)(2,1)} %copy.88), calls=%async_computation | async-start | bytes 1048576 | tf_op jit(solution)/shard_map/all_to_all | solution.py:67
  12.2 1.0 copy-start.6
  14.0 6.7 %copy-start = (bf16[3,3,3,192,192]{4,3,2,1,0:T(8,128)(2,1)S(1)}, bf16[3,3,3,192,192]{4,3,2,1,0:T(8,128)(2,1)}, u32[]{:S(2)}) copy-start(bf16[3,3,3,192,192]{4,3,2,1,0:T(8,128)(2,1)} %param.13) | copy-start | bytes 5971972
  14.0 97.3 %collective-permute-start.6 = (bf16[2,8,128,96]{3,2,1,0:T(8,128)(2,1)}, bf16[2,8,128,96]{3,2,1,0:T(8,128)(2,1)}, u32[]{:S(2)}, u32[]{:S(2)}) collective-permute-start(bf16[2,8,128,96]{3,2,1,0:T(8,128)(2,1)} %slice.352), channel_id=1, source_target_pairs={{1,0},{2,1},{3,2},{4,3},{5,4},{6,5},{7,6},{9,8},{10,9},{11,10},{12... | collective-permute-start | bytes 1179656 | tf_op jit(solution)/shard_map/ppermute | solution.py:12
  22.5 88.9 %copy-start.7 = (bf16[4,8,128,96]{3,2,1,0:T(8,128)(2,1)S(1)}, bf16[4,8,128,96]{3,2,1,0:T(8,128)(2,1)}, u32[]{:S(2)}) copy-start(bf16[4,8,128,96]{3,2,1,0:T(8,128)(2,1)} %copy-done.6) | copy-start | bytes 2359300
  112.3 6.2 %collective-permute-start.7 = (bf16[6,1,128,96]{3,2,1,0:T(8,128)(2,1)S(1)}, bf16[6,1,128,96]{3,2,1,0:T(8,128)(2,1)S(1)}, u32[]{:S(2)}, u32[]{:S(2)}) collective-permute-start(bf16[6,1,128,96]{3,2,1,0:T(8,128)(2,1)S(1)} %get-tuple-element.276), channel_id=1, source_target_pairs={{0,8},{8,16},{16,24},{24,32},{32,40},{40,48},{48,56},{56,64},{64,7... | collective-permute-start | bytes 442376 | tf_op jit(solution)/shard_map/ppermute | solution.py:22
  114.3 7.1 %collective-permute-start.8 = (bf16[6,1,128,96]{3,2,1,0:T(8,128)(2,1)S(1)}, bf16[6,1,128,96]{3,2,1,0:T(8,128)(2,1)}, u32[]{:S(2)}, u32[]{:S(2)}) collective-permute-start(bf16[6,1,128,96]{3,2,1,0:T(8,128)(2,1)S(1)} %get-tuple-element.277), channel_id=1, source_target_pairs={{8,0},{16,8},{24,16},{32,24},{40,32},{48,40},{56,48},{64,56},{72,6... | collective-permute-start | bytes 442376 | tf_op jit(solution)/shard_map/ppermute | solution.py:23
  118.5 5.8 copy-start.4
  118.6 0.7 copy-start.13
  172.9 5.0 copy-start.8
  176.5 86.6 %copy-start.9 = (bf16[4,4,64,192]{3,0,2,1:T(4,128)(2,1)}, bf16[4,4,64,192]{3,0,2,1:T(4,128)(2,1)S(1)}, u32[]{:S(2)}) copy-start(bf16[4,4,64,192]{3,0,2,1:T(4,128)(2,1)S(1)} %reduce_sum.66) | copy-start | bytes 1179652
  176.6 80.0 %collective-permute-start.9 = (bf16[2,4,64,192]{3,2,1,0:T(8,128)(2,1)S(1)}, bf16[2,4,64,192]{3,2,1,0:T(8,128)(2,1)S(1)}, u32[]{:S(2)}, u32[]{:S(2)}) collective-permute-start(bf16[2,4,64,192]{3,2,1,0:T(8,128)(2,1)S(1)} %slice.353), channel_id=1, source_target_pairs={{1,0},{2,1},{3,2},{4,3},{5,4},{6,5},{7,6},{9,8},{10,9},{11,10},{12... | collective-permute-start | bytes 589832 | tf_op jit(solution)/shard_map/ppermute | solution.py:12
  257.5 8.3 %collective-permute-start.10 = (bf16[6,1,64,192]{3,2,1,0:T(8,128)(2,1)}, bf16[6,1,64,192]{3,2,1,0:T(8,128)(2,1)}, u32[]{:S(2)}, u32[]{:S(2)}) collective-permute-start(bf16[6,1,64,192]{3,2,1,0:T(8,128)(2,1)} %get-tuple-element.280), channel_id=1, source_target_pairs={{0,8},{8,16},{16,24},{24,32},{32,40},{40,48},{48,56},{56,64},{64,7... | collective-permute-start | bytes 442376 | tf_op jit(solution)/shard_map/ppermute | solution.py:22
  259.9 7.3 %collective-permute-start.11 = (bf16[6,1,64,192]{3,2,1,0:T(8,128)(2,1)}, bf16[6,1,64,192]{3,2,1,0:T(8,128)(2,1)}, u32[]{:S(2)}, u32[]{:S(2)}) collective-permute-start(bf16[6,1,64,192]{3,2,1,0:T(8,128)(2,1)} %get-tuple-element.281), channel_id=1, source_target_pairs={{8,0},{16,8},{24,16},{32,24},{40,32},{48,40},{56,48},{64,56},{72,6... | collective-permute-start | bytes 442376 | tf_op jit(solution)/shard_map/ppermute | solution.py:23
  263.2 6.8 %copy-start.2 = (bf16[3,3,3,192,192]{4,3,2,1,0:T(8,128)(2,1)S(1)}, bf16[3,3,3,192,192]{4,3,2,1,0:T(8,128)(2,1)}, u32[]{:S(2)}) copy-start(bf16[3,3,3,192,192]{4,3,2,1,0:T(8,128)(2,1)} %copy.105) | copy-start | bytes 5971972
  309.0 79.2 %copy-start.5 = (f32[4,4,32,2,192]{4,1,3,2,0:T(4,128)S(1)}, f32[4,4,32,2,192]{4,1,3,2,0:T(4,128)}, u32[]{:S(2)}) copy-start(f32[4,4,32,2,192]{4,1,3,2,0:T(4,128)} %copy.90) | copy-start | bytes 2359300
  309.0 79.2 %copy-start.10 = (bf16[4,4,64,192]{3,0,2,1:T(4,128)(2,1)S(1)}, bf16[4,4,64,192]{3,0,2,1:T(4,128)(2,1)}, u32[]{:S(2)}) copy-start(bf16[4,4,64,192]{3,0,2,1:T(4,128)(2,1)} %copy-done.9) | copy-start | bytes 1179652
  390.8 23.6 %copy-start.1 = (bf16[3,3,3,192,192]{4,3,2,1,0:T(8,128)(2,1)S(1)}, bf16[3,3,3,192,192]{4,3,2,1,0:T(8,128)(2,1)}, u32[]{:S(2)}) copy-start(bf16[3,3,3,192,192]{4,3,2,1,0:T(8,128)(2,1)} %param.13) | copy-start | bytes 5971972
  390.9 8.8 %collective-permute-start = (bf16[2,4,64,192]{3,2,1,0:T(8,128)(2,1)S(1)}, bf16[2,4,64,192]{3,2,1,0:T(8,128)(2,1)S(1)}, u32[]{:S(2)}, u32[]{:S(2)}) collective-permute-start(bf16[2,4,64,192]{3,2,1,0:T(8,128)(2,1)S(1)} %slice.346), channel_id=1, source_target_pairs={{0,1},{1,2},{2,3},{3,4},{4,5},{5,6},{6,7},{8,9},{9,10},{10,11},{11... | collective-permute-start | bytes 589832 | tf_op jit(solution)/shard_map/ppermute | solution.py:12
  400.4 6.8 %collective-permute-start.1 = (bf16[6,1,64,192]{3,2,1,0:T(8,128)(2,1)}, bf16[6,1,64,192]{3,2,1,0:T(8,128)(2,1)}, u32[]{:S(2)}, u32[]{:S(2)}) collective-permute-start(bf16[6,1,64,192]{3,2,1,0:T(8,128)(2,1)} %get-tuple-element.282), channel_id=1, source_target_pairs={{0,8},{8,16},{16,24},{24,32},{32,40},{40,48},{48,56},{56,64},{64,7... | collective-permute-start | bytes 442376 | tf_op jit(solution)/shard_map/ppermute | solution.py:22
  404.3 7.3 %collective-permute-start.2 = (bf16[6,1,64,192]{3,2,1,0:T(8,128)(2,1)}, bf16[6,1,64,192]{3,2,1,0:T(8,128)(2,1)}, u32[]{:S(2)}, u32[]{:S(2)}) collective-permute-start(bf16[6,1,64,192]{3,2,1,0:T(8,128)(2,1)} %get-tuple-element.283), channel_id=1, source_target_pairs={{8,0},{16,8},{24,16},{32,24},{40,32},{48,40},{56,48},{64,56},{72,6... | collective-permute-start | bytes 442376 | tf_op jit(solution)/shard_map/ppermute | solution.py:23
  456.3 6.6 %copy-start.11 = (bf16[4,4,64,192]{3,2,1,0:T(8,128)(2,1)S(1)}, bf16[4,4,64,192]{3,2,1,0:T(8,128)(2,1)}, u32[]{:S(2)}) copy-start(bf16[4,4,64,192]{3,2,1,0:T(8,128)(2,1)} %get-tuple-element.278) | copy-start | bytes 1179652
  457.9 18.3 %collective-permute-start.3 = (bf16[2,8,128,192]{2,3,1,0:T(8,128)(2,1)S(1)}, bf16[2,8,128,192]{2,3,1,0:T(8,128)(2,1)}, u32[]{:S(2)}, u32[]{:S(2)}) collective-permute-start(bf16[2,8,128,192]{2,3,1,0:T(8,128)(2,1)S(1)} %copy.93), channel_id=1, source_target_pairs={{0,1},{1,2},{2,3},{3,4},{4,5},{5,6},{6,7},{8,9},{9,10},{10,11},{11... | collective-permute-start | bytes 2359304 | tf_op jit(solution)/shard_map/ppermute | solution.py:12
  464.2 31.4 %all-to-all-start.1 = ((bf16[4,4,64,192]{3,1,0,2:T(4,128)(2,1)}), bf16[4,4,64,192]{3,1,0,2:T(4,128)(2,1)}, u32[]{:S(2)}, u32[]{:S(2)}) async-start(bf16[4,4,64,192]{3,1,0,2:T(4,128)(2,1)} %copy.106), calls=%async_computation.1 | async-start | bytes 1048576 | tf_op jit(solution)/shard_map/all_to_all | solution.py:119
  485.1 21.7 %collective-permute-start.4 = (bf16[6,1,128,192]{2,3,1,0:T(8,128)(2,1)}, bf16[6,1,128,192]{2,3,1,0:T(8,128)(2,1)S(1)}, u32[]{:S(2)}, u32[]{:S(2)}) collective-permute-start(bf16[6,1,128,192]{2,3,1,0:T(8,128)(2,1)} %copy.95), channel_id=1, source_target_pairs={{0,8},{8,16},{16,24},{24,32},{32,40},{40,48},{48,56},{56,64},{64,7... | collective-permute-start | bytes 884744 | tf_op jit(solution)/shard_map/ppermute | solution.py:22
  493.5 13.3 %collective-permute-start.5 = (bf16[6,1,128,192]{2,3,1,0:T(8,128)(2,1)}, bf16[6,1,128,192]{2,3,1,0:T(8,128)(2,1)}, u32[]{:S(2)}, u32[]{:S(2)}) collective-permute-start(bf16[6,1,128,192]{2,3,1,0:T(8,128)(2,1)} %copy.96), channel_id=1, source_target_pairs={{8,0},{16,8},{24,16},{32,24},{40,32},{48,40},{56,48},{64,56},{72,6... | collective-permute-start | bytes 884744 | tf_op jit(solution)/shard_map/ppermute | solution.py:23
  512.6 6.6 %copy-start.3 = (bf16[3,3,3,192,96]{4,3,2,1,0:T(8,128)(2,1)S(1)}, bf16[3,3,3,192,96]{4,3,2,1,0:T(8,128)(2,1)}, u32[]{:S(2)}) copy-start(bf16[3,3,3,192,96]{4,3,2,1,0:T(8,128)(2,1)} %param.14) | copy-start | bytes 2985988
  512.6 6.6 %copy-start.14 = (bf16[4,8,128,96]{2,3,1,0:T(8,128)(2,1)S(1)}, bf16[4,8,128,96]{2,3,1,0:T(8,128)(2,1)}, u32[]{:S(2)}) copy-start(bf16[4,8,128,96]{2,3,1,0:T(8,128)(2,1)} %custom-call.1) | copy-start | bytes 2359300
  588.3 0.9 copy-start.15
where the time goes:
time: 596 us; the launch traced here: 589 us
  blocking collectives  236 us (40%)
  local copies, waits for them, and re-layouts  141 us (24%)
  matrix products  60.5 us (10%)
  starting transfers between devices  52.6 us (9%)
  other arithmetic  50.7 us (9%)
  loops' own time  32 us (5%)
  waiting for transfers between devices  14.6 us (2%)
    psum x1, blocking collectives, body(): lax.psum(jnp.sum(values, axis=(0, 1, 2, 4), keepdims=True), ('seq', 'clip'))  82.6 us
    psum x1, blocking collectives, body(): lax.psum(jnp.sum((values - mean) ** 2, axis=(0, 1, 2, 4), keepdims=True),...  77.8 us
    psum x1, blocking collectives, body(): lax.psum((jnp.sum(norm_grad, axis=(0, 1, 2, 4), keepdims=True), jnp.sum(n...  76.1 us
    dot_general x144, matrix products, one_frame(): jnp.dot(piece, flat_kernel[tap_time, tap_row], preferred_element_type=jnp...  60.5 us
    slice x16, local copies, waits for them, and re-layouts, one_frame(): window[:, :, 0:cols]  41.4 us
    another operation x4, loops' own time, causal_conv(): return lax.map(one_frame, jnp.arange(frames, dtype=jnp.int32))  32 us
    concatenate x16, other arithmetic, one_frame(): jnp.concatenate([window[:, :, 0:cols], window[:, :, 1:cols + 1], window[:...  20.7 us
    slice x16, local copies, waits for them, and re-layouts, one_frame(): stacked[tap_time, tap_row:tap_row + rows].reshape(rows * cols, 3 * chans)  15.9 us
  transfers between devices with their start and end apart: 14, of which 6 were waited for; matrix products, arithmetic and copies ran while one was open for 8% of the time, Pallas kernels for 0%

commit v1 on v0

v1 whole, which is shorter than its diff:
```python
import functools

import jax
import jax.numpy as jnp
from jax import lax
from jax.experimental import pallas as pl
from jax.experimental.pallas import tpu as pltpu
from jax.sharding import PartitionSpec as P

GROUPS = 32
F32 = jnp.float32
BF16 = jnp.bfloat16
VMEM_LIMIT = 48 * 2**20
TAPS = ((2,), (1, 2), (0, 1), (0,))


def vmem(count):
    return [pl.BlockSpec(memory_space=pltpu.VMEM)] * count


def smem():
    return pl.BlockSpec(memory_space=pltpu.SMEM)


def call(kernel, name, outs, in_specs, scratch, flops):
    return pl.pallas_call(
        kernel,
        name=name,
        out_shape=outs,
        in_specs=in_specs,
        out_specs=jax.tree.map(lambda _: pl.BlockSpec(memory_space=pltpu.VMEM), outs),
        scratch_shapes=scratch,
        compiler_params=pltpu.CompilerParams(vmem_limit_bytes=VMEM_LIMIT),
        cost_estimate=pl.CostEstimate(flops=flops, bytes_accessed=4 * 2**20, transcendentals=0),
    )


def combine_kernel(w_ref, out_ref):
    ins, outs = w_ref.shape[3], w_ref.shape[4]

    def one_time(a, carry):
        w = [[w_ref[a, b, d].astype(F32) for d in range(3)] for b in range(3)]
        for p in range(4):
            rows = [functools.reduce(jnp.add, [w[b][d] for b in TAPS[p]]) for d in range(3)]
            for q in range(4):
                value = functools.reduce(jnp.add, [rows[d] for d in TAPS[q]])
                out_ref[a, p, q] = jnp.pad(value, ((0, 0), (0, 128 - outs))).astype(BF16)
        return carry

    lax.fori_loop(0, 3, one_time, 0)


def combined_weights(conv_two):
    ins = conv_two.shape[3]
    return call(
        combine_kernel,
        "combine_weights",
        jax.ShapeDtypeStruct((3, 4, 4, ins, 128), BF16),
        vmem(1),
        [],
        10**6,
    )(conv_two)


def spread_columns(value, buffer, t, r, chans):
    cols = value.shape[0]
    index = lax.broadcasted_iota(jnp.int32, value.shape, 0)
    left = jnp.where(index == 0, 0.0, pltpu.roll(value, 1, 0))
    right = jnp.where(index == cols - 1, 0.0, pltpu.roll(value, cols - 1, 0))
    buffer[t, r, :, 0:chans] = left.astype(BF16)
    buffer[t, r, :, 256 : 256 + chans] = value.astype(BF16)
    buffer[t, r, :, 512 : 512 + chans] = right.astype(BF16)


def fill(buffer, pieces, chans, transform):
    for ref, source, count, t0, r0, keep in pieces:
        rows = ref.shape[1]

        def one_frame(i, carry):
            for r in range(rows):
                value = transform(ref[source + i, r].astype(F32), keep)
                spread_columns(value, buffer, t0 + i, r0 + r, chans)
            return carry

        lax.fori_loop(0, count, one_frame, 0)


def nt_dot(lhs, rhs):
    return lax.dot_general(lhs, rhs, (((1,), (1,)), ((), ())), preferred_element_type=F32)


def down_kernel(layout, frames, rows, flags, weights, *refs):
    sources = refs[: len(layout)]
    out_ref, buffer, wide = refs[len(layout) :]
    cols = out_ref.shape[2]
    outs = out_ref.shape[3]
    chans = sources[0].shape[3]
    wide[...] = jnp.zeros_like(wide)
    for ref, (source, count, t0, r0) in zip(sources, layout):
        lines = ref.shape[1]

        def one_frame(i, carry):
            for r in range(lines):
                wide[r, 8 : 8 + 2 * cols, 0:chans] = ref[source + i, r].astype(F32)
            for r in range(lines):
                line = r0 + r
                for j in range(4):
                    part = wide[r, pl.ds(7 + j, cols, stride=2), :]
                    buffer[t0 + i, line % 2, line // 2, :, 128 * j : 128 * (j + 1)] = part.astype(BF16)
            return carry

        lax.fori_loop(0, count, one_frame, 0)

    def one_out(t, carry):
        total = jnp.zeros((rows * cols, outs), F32)
        for dt in range(3):
            for p in range(4):
                lhs = buffer[t + dt, p % 2, p // 2 : p // 2 + rows].reshape(rows * cols, 512)
                rhs = jnp.concatenate([weights[2 - dt, p, q] for q in range(4)], axis=-1)
                total = total + nt_dot(lhs, rhs)
        total = total.reshape(rows, cols, outs)
        out_ref[t, 0] = (total[0] * flags[0]).astype(BF16)
        out_ref[t, 1 : rows - 1] = total[1 : rows - 1].astype(BF16)
        out_ref[t, rows - 1] = (total[rows - 1] * flags[1]).astype(BF16)
        return carry

    lax.fori_loop(0, frames, one_out, 0)


def down(name, flags, weights, pieces, frames, rows, cols, outs):
    layout = tuple((s, n, t0, r0) for _, s, n, t0, r0 in pieces)
    lines = max(a.shape[1] for a, *_ in pieces)
    return call(
        functools.partial(down_kernel, layout, frames, rows),
        name,
        jax.ShapeDtypeStruct((frames, rows, cols, outs), BF16),
        [smem()] + vmem(1 + len(pieces)),
        [
            pltpu.VMEM((frames + 2, 2, rows + 1, cols, 512), BF16),
            pltpu.VMEM((lines, 2 * cols + 16, 128), F32),
        ],
        2 * frames * rows * cols * 24 * 65536,
    )(flags, weights, *[a for a, *_ in pieces])


def back_kernel(layout, frames, first, flags, stats, weights, tile_ref, *refs):
    sources = refs[: len(layout)]
    out_ref, sums_ref, buffer = refs[len(layout) :]
    rows, cols, chans = out_ref.shape[1:]
    fill(
        buffer,
        [(ref, s, n, t0, 0, None) for ref, (s, n, t0) in zip(sources, layout)],
        chans,
        lambda value, keep: value,
    )
    mean = stats[0:1]
    scale = stats[1:2]
    sums_ref[...] = jnp.zeros_like(sums_ref)

    def one_out(t, carry):
        total = jnp.zeros((rows * cols, chans), F32)
        for dt in range(3):
            for dr in range(3):
                for dc in range(3):
                    lhs = buffer[t + dt, dr : dr + rows, :, 256 * dc : 256 * dc + chans]
                    lhs = lhs.reshape(rows * cols, chans)
                    total = total + nt_dot(lhs, weights[2 - dt, 2 - dr, 2 - dc])
        normed = (tile_ref[first + t].reshape(rows * cols, chans).astype(F32) - mean) * scale
        sigmoid = 1.0 / (1.0 + jnp.exp(-normed))
        grad = total * sigmoid * (1.0 + normed * (1.0 - sigmoid))
        sums_ref[0:1] += jnp.sum(grad, axis=0, keepdims=True)
        sums_ref[1:2] += jnp.sum(grad * normed, axis=0, keepdims=True)
        own = buffer[t, 1 : 1 + rows, :, 256 : 256 + chans].reshape(rows * cols, chans)
        base = own.astype(F32) + grad * scale
        out_ref[t] = base.astype(BF16).reshape(rows, cols, chans)
        return carry

    lax.fori_loop(0, frames, one_out, 0)


def back(name, flags, stats, weights, tile, pieces, frames, first):
    layout = tuple((s, n, t0) for _, s, n, t0 in pieces)
    _, rows, cols, chans = tile.shape
    return call(
        functools.partial(back_kernel, layout, frames, first),
        name,
        (
            jax.ShapeDtypeStruct((frames, rows, cols, chans), BF16),
            jax.ShapeDtypeStruct((2, chans), F32),
        ),
        [smem()] + vmem(3 + len(pieces)),
        [pltpu.VMEM((frames + 2, rows + 2, cols, 768), BF16)],
        2 * frames * rows * cols * 27 * 65536,
    )(flags, stats, weights, tile, *[a for a, *_ in pieces])


def mid_kernel(layout, frames, rows, first, flags, stats, weights, *refs):
    sources = refs[: len(layout)]
    out_ref, buffer = refs[len(layout) :]
    cols, chans = out_ref.shape[2:]
    mean = stats[0:1]
    scale = stats[1:2]

    def activate(value, keep):
        normed = (value - mean) * scale
        act = normed / (1.0 + jnp.exp(-normed))
        for flag in keep:
            act = act * flags[flag]
        return act

    fill(
        buffer,
        [(ref, *where) for ref, where in zip(sources, layout)],
        chans,
        activate,
    )
    own, up, down_ref = sources[:3]

    def one_out(t, carry):
        total = jnp.zeros((rows * cols, chans), F32)
        for dt in range(3):
            for dr in range(3):
                for dc in range(3):
                    lhs = buffer[t + dt, dr : dr + rows, :, 256 * dc : 256 * dc + chans]
                    lhs = lhs.reshape(rows * cols, chans)
                    total = total + jnp.dot(lhs, weights[dt, dr, dc], preferred_element_type=F32)
        total = total.reshape(rows, cols, chans)
        at = first + t
        out_ref[t, 0] = ((total[0] + up[at, 1].astype(F32)) * flags[0]).astype(BF16)
        out_ref[t, 1 : rows - 1] = (total[1 : rows - 1] + own[at].astype(F32)).astype(BF16)
        out_ref[t, rows - 1] = (
            (total[rows - 1] + down_ref[at, 0].astype(F32)) * flags[1]
        ).astype(BF16)
        return carry

    lax.fori_loop(0, frames, one_out, 0)


def middle(name, flags, stats, weights, pieces, frames, rows, first):
    layout = tuple(tuple(where) for _, *where in pieces)
    _, _, cols, chans = pieces[0][0].shape
    return call(
        functools.partial(mid_kernel, layout, frames, rows, first),
        name,
        jax.ShapeDtypeStruct((frames, rows, cols, chans), BF16),
        [smem()] + vmem(2 + len(pieces)),
        [pltpu.VMEM((frames + 2, rows + 2, cols, 768), BF16)],
        2 * frames * rows * cols * 27 * 65536,
    )(flags, stats, weights, *[a for a, *_ in pieces])


def decode_kernel(layout, frames, weights, *refs):
    sources = refs[: len(layout)]
    out_ref, buffer, wide = refs[len(layout) :]
    chans = sources[0].shape[3]
    cols = sources[0].shape[2]
    rows = out_ref.shape[1] // 2
    outs = out_ref.shape[3]
    fill(
        buffer,
        [(ref, s, n, t0, 0, None) for ref, (s, n, t0) in zip(sources, layout)],
        chans,
        lambda value, keep: value,
    )
    zero = jnp.zeros((chans, 128), BF16)

    def one_out(t, carry):
        for i, taps in enumerate((((0, 3), (1, 1)), ((1, 2), (2, 0)))):
            total = jnp.zeros((rows * cols, 256), F32)
            for dt in range(3):
                for dr, p in taps:
                    w = weights.at[dt, p]
                    pairs = ((w[3], zero), (w[1], w[2]), (zero, w[0]))
                    for dc, pair in enumerate(pairs):
                        lhs = buffer[t + dt, dr : dr + rows, :, 256 * dc : 256 * dc + chans]
                        lhs = lhs.reshape(rows * cols, chans)
                        rhs = jnp.concatenate(pair, axis=-1)
                        total = total + jnp.dot(lhs, rhs, preferred_element_type=F32)
            total = total.reshape(rows, cols, 256)
            for r in range(rows):
                wide[2 * r + i, pl.ds(0, cols, stride=2), :] = total[r, :, 0:128]
                wide[2 * r + i, pl.ds(1, cols, stride=2), :] = total[r, :, 128:256]
        out_ref[t] = wide[:, :, 0:outs].astype(BF16)
        return carry

    lax.fori_loop(0, frames, one_out, 0)


def decode(name, weights, pieces, frames, outs):
    layout = tuple((s, n, t0) for _, s, n, t0 in pieces)
    _, ext, cols, _ = pieces[0][0].shape
    rows = ext - 2
    return call(
        functools.partial(decode_kernel, layout, frames),
        name,
        jax.ShapeDtypeStruct((frames, 2 * rows, 2 * cols, outs), BF16),
        vmem(1 + len(pieces)),
        [
            pltpu.VMEM((frames + 2, rows + 2, cols, 768), BF16),
            pltpu.VMEM((2 * rows, 2 * cols, 128), F32),
        ],
        2 * frames * rows * cols * 36 * 65536,
    )(weights, *[a for a, *_ in pieces])


def moved(block, clip_step, seq_step):
    clips, seqs = lax.axis_size("clip"), lax.axis_size("seq")
    if clip_step == 0:
        route = [(i - seq_step, i) for i in range(seqs) if 0 <= i - seq_step < seqs]
        return lax.ppermute(block, "seq", route)
    if seq_step == 0:
        route = [(i - clip_step, i) for i in range(clips) if 0 <= i - clip_step < clips]
        return lax.ppermute(block, "clip", route)
    route = [
        ((s - seq_step) * clips + c - clip_step, s * clips + c)
        for s in range(seqs)
        for c in range(clips)
        if 0 <= c - clip_step < clips and 0 <= s - seq_step < seqs
    ]
    return lax.ppermute(block, ("seq", "clip"), route)


def from_all(values):
    everyone = lax.axis_size("clip") * lax.axis_size("seq")
    rows = jnp.broadcast_to(values[None], (everyone, values.shape[0]))
    return lax.all_to_all(rows, ("seq", "clip"), 0, 0, tiled=True)


def per_group(channels):
    return channels.reshape(GROUPS, -1).sum(axis=1)


def per_channel(groups, chans):
    return jnp.repeat(groups, chans // GROUPS)


def body(tokens, conv_one, conv_two, pixel_grad):
    frames, height, stripe, chans = tokens.shape
    lines, wide, outs = pixel_grad.shape[1:]
    rows, cols = lines // 2, wide // 2
    clips, seqs = lax.axis_size("clip"), lax.axis_size("seq")
    clip, seq = lax.axis_index("clip"), lax.axis_index("seq")
    flags = jnp.stack([seq != 0, seq != seqs - 1, clip != 0]).astype(F32)

    px_up = moved(pixel_grad[:, lines - 3 :], 0, 1)
    px_down = moved(pixel_grad[:, :3], 0, -1)
    px_z = moved(pixel_grad[:2], -1, 0)
    px_zup = moved(pixel_grad[:2, lines - 3 :], -1, 1)
    px_zdown = moved(pixel_grad[:2, :3], -1, -1)

    own_count = frames * height * stripe * (chans // GROUPS)
    field = tokens.astype(F32)
    own_mean = per_group(jnp.sum(field, axis=(0, 1, 2))) / own_count
    own_spread = per_group(jnp.sum((field - per_channel(own_mean, chans)) ** 2, axis=(0, 1, 2)))
    gathered = from_all(jnp.concatenate([own_mean, own_spread]))
    tile = lax.all_to_all(tokens, "seq", split_axis=1, concat_axis=2, tiled=True)
    means, spreads = gathered[:, :GROUPS], gathered[:, GROUPS:]
    mean = jnp.mean(means, axis=0)
    var = jnp.mean(spreads, axis=0) / own_count + jnp.mean((means - mean) ** 2, axis=0)
    scale = lax.rsqrt(var + 1e-06)
    mean_c, scale_c = per_channel(mean, chans), per_channel(scale, chans)
    stats = jnp.stack([mean_c, scale_c])

    tile_up = moved(tile[:, rows - 2 :], 0, 1)
    tile_down = moved(tile[:, :2], 0, -1)
    tile_z = moved(tile[frames - 2 :], 1, 0)
    tile_zup = moved(tile[frames - 2 :, rows - 2 :], 1, 1)
    tile_zdown = moved(tile[frames - 2 :, :2], 1, -1)

    both = combined_weights(conv_two)

    pieces = [(pixel_grad, 0, 4, 0, 3), (px_up, 0, 4, 0, 0), (px_down, 0, 4, 0, 3 + lines)]
    grad_a = down("down_a", flags, both, pieces, 2, rows + 2, cols, chans)
    grad_z = moved(grad_a, -1, 0)
    pieces = [
        (pixel_grad, 2, 2, 0, 3),
        (px_up, 2, 2, 0, 0),
        (px_down, 2, 2, 0, 3 + lines),
        (px_z, 0, 2, 2, 3),
        (px_zup, 0, 2, 2, 0),
        (px_zdown, 0, 2, 2, 3 + lines),
    ]
    grad_b = down("down_b", flags, both, pieces, 2, rows + 2, cols, chans)
    pieces = [(grad_a, 0, 2, 0), (grad_b, 0, 2, 2), (grad_z, 0, 2, 4)]
    base, sums = back("back", flags, stats, conv_one, tile, pieces, frames, 0)
    spread = lax.all_to_all(base, "seq", split_axis=2, concat_axis=1, tiled=True)
    sums = from_all(jnp.concatenate([per_group(sums[0]), per_group(sums[1])]))

    pieces = [
        (tile, 0, 4, 0, 2, ()),
        (tile_up, 0, 4, 0, 0, (0,)),
        (tile_down, 0, 4, 0, 2 + rows, (1,)),
    ]
    mid_b = middle("mid_b", flags, stats, conv_one, pieces, 2, rows + 2, 2)
    mid_z = moved(mid_b, 1, 0)
    pieces = [
        (tile, 0, 2, 2, 2, ()),
        (tile_up, 0, 2, 2, 0, (0,)),
        (tile_down, 0, 2, 2, 2 + rows, (1,)),
        (tile_z, 0, 2, 0, 2, (2,)),
        (tile_zup, 0, 2, 0, 0, (0, 2)),
        (tile_zdown, 0, 2, 0, 2 + rows, (1, 2)),
    ]
    mid_a = middle("mid_a", flags, stats, conv_one, pieces, 2, rows + 2, 0)
    decoded = decode(
        "decode", both, [(mid_z, 0, 2, 0), (mid_a, 0, 2, 2), (mid_b, 0, 2, 4)], frames, outs
    )

    count = float(own_count * clips * seqs)
    total = jnp.sum(sums, axis=0) / count
    first = per_channel(total[:GROUPS], chans)
    second = per_channel(total[GROUPS:], chans)
    normed = (field - mean_c) * scale_c
    token_grad = (spread.astype(F32) - (first + normed * second) * scale_c).astype(BF16)
    return (decoded, token_grad)


def solution(mesh):
    return jax.shard_map(
        body,
        mesh=mesh,
        in_specs=(P("clip", None, "seq", None), P(), P(), P("clip", "seq", None, None)),
        out_specs=(P("clip", "seq", None, None), P("clip", None, "seq", None)),
        check_vma=False,
    )
```

time: 596 us -> 150 us (0.25)
  blocking collectives: 236 us -> 0 us
  local copies, waits for them, and re-layouts: 141 us -> 24.8 us
  matrix products: 60.5 us -> 0 us
  other arithmetic: 50.7 us -> 5.33 us
  Pallas kernels: 0 us -> 33.4 us
  loops' own time: 32 us -> 0 us
  starting transfers between devices: 52.6 us -> 77.4 us
  waiting for transfers between devices: 14.6 us -> 7.06 us
    psum x3 -> x0, blocking collectives: 236 us -> none  [the longest x1 82.6 us: body(): lax.psum(jnp.sum(values, axis=(0, 1, 2, 4), keepdims=True), ('seq', 'clip'))]
    slice x40 -> x10, local copies, waits for them, and re-layouts: 65.4 us -> 3.31 us  [the longest x1 0.94 us: body(): px_down = moved(pixel_grad[:, :3], 0, -1)]
    dot_general x144 -> x0, matrix products: 60.5 us -> none  [one_frame(): jnp.dot(piece, flat_kernel[tap_time, tap_row], preferred_element_type=jnp...]
    concatenate x22 -> x2, other arithmetic: 36.4 us -> 0.15 us  [the longest x1 0.08 us: body(): gathered = from_all(jnp.concatenate([own_mean, own_spread]))]
    pallas_call x0 -> x7, Pallas kernels: none -> 33.4 us  [the longest x2 10.8 us: down(): call(functools.partial(down_kernel, layout, frames, rows), name, jax.Shap...]
    another operation x4 -> x0, loops' own time: 32 us -> none  [causal_conv(): return lax.map(one_frame, jnp.arange(frames, dtype=jnp.int32))]
    all_to_all x1 -> x3, starting transfers between devices: 8.55 us -> 35.2 us  [the longest x2 31.1 us: from_all(): return lax.all_to_all(rows, ('seq', 'clip'), 0, 0, tiled=True)]
    ppermute x12, waiting for transfers between devices: 14.6 us -> 0.03 us  [the longest x4 0.01 us: moved(): return lax.ppermute(block, ('seq', 'clip'), route)]
  transfers between devices with their start and end apart: 14 -> 16, of which waited for: 6 -> 3; matrix products, arithmetic and copies ran while one was open for 8% -> 10% of each run, Pallas kernels for 0% -> 22%
where the time goes in v1:
time: 150 us; the launch traced here: 149 us
  starting transfers between devices  77.4 us (52%)
  Pallas kernels  33.4 us (22%)
  local copies, waits for them, and re-layouts  24.8 us (17%)
  waiting for transfers between devices  7.06 us (5%)
  other arithmetic  5.33 us (4%)
    all_to_all x2, starting transfers between devices, from_all(): return lax.all_to_all(rows, ('seq', 'clip'), 0, 0, tiled=True)  31.1 us
    ppermute x4, starting transfers between devices, moved(): return lax.ppermute(block, ('seq', 'clip'), route)  13.9 us
    unnamed x29, local copies, waits for them, and re-layouts  13.7 us
    ppermute x4, starting transfers between devices, moved(): return lax.ppermute(block, 'clip', route)  11 us
    pallas_call x2, Pallas kernels, down(): call(functools.partial(down_kernel, layout, frames, rows), name, jax.Shap...  10.8 us
    ppermute x4, starting transfers between devices, moved(): return lax.ppermute(block, 'seq', route)  10.4 us
    pallas_call x2, Pallas kernels, middle(): call(functools.partial(mid_kernel, layout, frames, rows, first), name, ja...  9.46 us
    all_to_all x1, starting transfers between devices, body(): lax.all_to_all(tokens, 'seq', split_axis=1, concat_axis=2, tiled=True)  6.93 us
  transfers between devices with their start and end apart: 16, of which 3 were waited for; matrix products, arithmetic and copies ran while one was open for 10% of the time, Pallas kernels for 22%

profile of v1, /device:TPU:1, one launch (start us, length us, event | category | flops | bytes accessed | tf_op | source)
XLA Modules:
  0.0 149.1 jit_solution(17134080075761771833)
XLA Ops:
  0.6 1.4 copy.98
  4.9 15.7 %all-to-all-start = ((f32[256,1,64]{2,1,0:T(1,128)}), f32[256,1,64]{2,1,0:T(1,128)S(1)}, u32[]{:S(2)}, u32[]{:S(2)}) async-start(f32[256,1,64]{2,1,0:T(1,128)} %broadcast_in_dim.29), calls=%async_computation | async-start | bytes 262144 | tf_op jit(solution)/shard_map/all_to_all | solution.py:326
  22.2 3.5 %collective-permute-start.6 = (bf16[4,3,128,96]{3,2,1,0:T(8,128)(2,1)}, bf16[4,3,128,96]{3,2,1,0:T(8,128)(2,1)}, u32[]{:S(2)}, u32[]{:S(2)}) collective-permute-start(bf16[4,3,128,96]{3,2,1,0:T(8,128)(2,1)} %get-tuple-element.27), channel_id=1, source_target_pairs={{0,8},{8,16},{16,24},{24,32},{32,40},{40,48},{48,56},{56,64},{64,7... | collective-permute-start | bytes 884744 | tf_op jit(solution)/shard_map/ppermute | solution.py:310
  25.8 2.5 %collective-permute-start.7 = (bf16[4,3,128,96]{3,2,1,0:T(8,128)(2,1)}, bf16[4,3,128,96]{3,2,1,0:T(8,128)(2,1)}, u32[]{:S(2)}, u32[]{:S(2)}) collective-permute-start(bf16[4,3,128,96]{3,2,1,0:T(8,128)(2,1)} %get-tuple-element.26), channel_id=1, source_target_pairs={{8,0},{16,8},{24,16},{32,24},{40,32},{48,40},{56,48},{64,56},{72,6... | collective-permute-start | bytes 884744 | tf_op jit(solution)/shard_map/ppermute | solution.py:310
  29.1 1.3 collective-permute-start.10
  30.4 1.3 collective-permute-start.9
  32.5 1.3 collective-permute-start.8
  35.0 1.3 copy-done.3
  36.9 6.9 %all-to-all-start.1 = ((bf16[4,128,2,192]{3,0,2,1:T(4,128)(2,1)}), bf16[4,128,2,192]{3,0,2,1:T(4,128)(2,1)}, u32[]{:S(2)}, u32[]{:S(2)}) async-start(bf16[4,128,2,192]{3,0,2,1:T(4,128)(2,1)} %copy.100), calls=%async_computation.1 | async-start | bytes 1048576 | tf_op jit(solution)/shard_map/all_to_all | solution.py:356
  47.0 5.6 %down_a.1.refs_0_ = bf16[2,6,64,192]{3,2,1,0:T(8,128)(2,1)} custom-call(f32[3]{0:T(128)S(1)} %add_convert_fusion.flags, bf16[3,4,4,192,128]{4,3,2,1,0:T(8,128)(2,1)S(1)} %combine_weights.1.weights, bf16[4,8,128,96]{3,2,1,0:T(8,128)(2,1)S(1)} %copy.106.refs_0_, bf16[4,3,128,96]{3,2,1,0:T(8,128)(2,1)} %collective-permute-done.6.refs_1_, ...), custom_call_target="tpu_custom_call" | custom-call | flops 2415919104 | bytes 4194304 | tf_op jit(solution)/shard_map/down_a/pallas_call | solution.py:133
  52.6 1.3 collective-permute-start.11
  53.9 1.6 %all-to-all-done.1 = bf16[4,128,2,192]{3,0,2,1:T(4,128)(2,1)} async-done(((bf16[4,128,2,192]{3,0,2,1:T(4,128)(2,1)}), bf16[4,128,2,192]{3,0,2,1:T(4,128)(2,1)}, u32[]{:S(2)}, u32[]{:S(2)}) %all-to-all-start.1) | async-done | bytes 393248 | tf_op jit(solution)/shard_map/all_to_all | solution.py:356
  55.5 1.4 copy.101
  58.2 2.1 %collective-permute-start = (bf16[4,2,64,192]{3,2,1,0:T(8,128)(2,1)S(1)}, bf16[4,2,64,192]{3,2,1,0:T(8,128)(2,1)S(1)}, u32[]{:S(2)}, u32[]{:S(2)}) collective-permute-start(bf16[4,2,64,192]{3,2,1,0:T(8,128)(2,1)S(1)} %get-tuple-element.31), channel_id=1, source_target_pairs={{0,8},{8,16},{16,24},{24,32},{32,40},{40,48},{48,56},{56,64},{64,7... | collective-permute-start | bytes 589832 | tf_op jit(solution)/shard_map/ppermute | solution.py:310
  60.8 2.3 %collective-permute-start.1 = (bf16[4,2,64,192]{3,2,1,0:T(8,128)(2,1)S(1)}, bf16[4,2,64,192]{3,2,1,0:T(8,128)(2,1)S(1)}, u32[]{:S(2)}, u32[]{:S(2)}) collective-permute-start(bf16[4,2,64,192]{3,2,1,0:T(8,128)(2,1)S(1)} %get-tuple-element.30), channel_id=1, source_target_pairs={{8,0},{16,8},{24,16},{32,24},{40,32},{48,40},{56,48},{64,56},{72,6... | collective-permute-start | bytes 589832 | tf_op jit(solution)/shard_map/ppermute | solution.py:310
  63.1 8.6 %collective-permute-start.4 = (bf16[2,2,64,192]{3,2,1,0:T(8,128)(2,1)S(1)}, bf16[2,2,64,192]{3,2,1,0:T(8,128)(2,1)S(1)}, u32[]{:S(2)}, u32[]{:S(2)}) collective-permute-start(bf16[2,2,64,192]{3,2,1,0:T(8,128)(2,1)S(1)} %get-tuple-element.29), channel_id=1, source_target_pairs={{0,9},{1,10},{2,11},{3,12},{4,13},{5,14},{6,15},{8,17},{9,18},{10,... | collective-permute-start | bytes 294920 | tf_op jit(solution)/shard_map/ppermute | solution.py:320
  71.7 2.7 %collective-permute-start.5 = (bf16[2,2,64,192]{3,2,1,0:T(8,128)(2,1)S(1)}, bf16[2,2,64,192]{3,2,1,0:T(8,128)(2,1)S(1)}, u32[]{:S(2)}, u32[]{:S(2)}) collective-permute-start(bf16[2,2,64,192]{3,2,1,0:T(8,128)(2,1)S(1)} %get-tuple-element.28), channel_id=1, source_target_pairs={{8,1},{9,2},{10,3},{11,4},{12,5},{13,6},{14,7},{16,9},{17,10},{18,... | collective-permute-start | bytes 294920 | tf_op jit(solution)/shard_map/ppermute | solution.py:320
  74.4 1.7 %copy-done.1 = bf16[3,4,4,192,128]{4,3,2,1,0:T(8,128)(2,1)S(1)} copy-done((bf16[3,4,4,192,128]{4,3,2,1,0:T(8,128)(2,1)S(1)}, bf16[3,4,4,192,128]{4,3,2,1,0:T(8,128)(2,1)}, u32[]{:S(2)}) %copy-start.1) | copy-done | bytes 2359320
  76.1 5.2 %down_b.1.refs_1_ = bf16[2,6,64,192]{3,2,1,0:T(8,128)(2,1)S(1)} custom-call(f32[3]{0:T(128)S(1)} %add_convert_fusion.flags, bf16[3,4,4,192,128]{4,3,2,1,0:T(8,128)(2,1)S(1)} %copy-done.1, bf16[4,8,128,96]{3,2,1,0:T(8,128)(2,1)S(1)} %copy.106.refs_0_, bf16[4,3,128,96]{3,2,1,0:T(8,128)(2,1)} %collective-permute-done.6.refs_1_, ...), custom_call_target="tpu_custom_call" | custom-call | flops 2415919104 | bytes 4194304 | tf_op jit(solution)/shard_map/down_b/pallas_call | solution.py:133
  81.3 3.6 %collective-permute-start.3 = (bf16[2,4,64,192]{3,2,1,0:T(8,128)(2,1)S(1)}, bf16[2,4,64,192]{3,2,1,0:T(8,128)(2,1)S(1)}, u32[]{:S(2)}, u32[]{:S(2)}) collective-permute-start(bf16[2,4,64,192]{3,2,1,0:T(8,128)(2,1)S(1)} %slice.56), channel_id=1, source_target_pairs={{0,1},{1,2},{2,3},{3,4},{4,5},{5,6},{6,7},{8,9},{9,10},{10,11},{11... | collective-permute-start | bytes 589832 | tf_op jit(solution)/shard_map/ppermute | solution.py:313
  85.0 4.7 %mid_b.1.refs_2_ = bf16[2,6,64,192]{3,2,1,0:T(8,128)(2,1)S(1)} custom-call(f32[3]{0:T(128)S(1)} %add_convert_fusion.flags, f32[2,192]{1,0:T(2,128)S(1)} %pad_maximum_fusion.stats, bf16[3,3,3,192,192]{4,3,2,1,0:T(8,128)(2,1)S(1)} %copy-done.4, bf16[4,4,64,192]{3,2,1,0:T(8,128)(2,1)S(1)} %all_to_all.35.refs_0_.tile_ref, ...), custom_call_target="tpu_custom_call" | custom-call | flops 2717908992 | bytes 4194304 | tf_op jit(solution)/shard_map/mid_b/pallas_call | solution.py:242
  89.7 4.8 %collective-permute-start.2 = (bf16[2,6,64,192]{3,2,1,0:T(8,128)(2,1)S(1)}, bf16[2,6,64,192]{3,2,1,0:T(8,128)(2,1)S(1)}, u32[]{:S(2)}, u32[]{:S(2)}) collective-permute-start(bf16[2,6,64,192]{3,2,1,0:T(8,128)(2,1)S(1)} %mid_b.1.refs_2_), channel_id=1, source_target_pairs={{0,1},{1,2},{2,3},{3,4},{4,5},{5,6},{6,7},{8,9},{9,10},{10,11},{11... | collective-permute-start | bytes 884744 | tf_op jit(solution)/shard_map/ppermute | solution.py:313
  94.5 6.4 %back.1 = (bf16[4,4,64,192]{3,2,1,0:T(8,128)(2,1)S(1)}, f32[2,192]{1,0:T(2,128)S(1)}) custom-call(f32[3]{0:T(128)S(1)} %add_convert_fusion.flags, f32[2,192]{1,0:T(2,128)S(1)} %pad_maximum_fusion.stats, bf16[3,3,3,192,192]{4,3,2,1,0:T(8,128)(2,1)S(1)} %copy-done.4, bf16[4,4,64,192]{3,2,1,0:T(8,128)(2,1)S(1)} %all_to_all.35.refs_0_.tile_ref, ...), custom_call_target="tpu_custom_call" | custom-call | flops 3623878656 | bytes 4194304 | tf_op jit(solution)/shard_map/back/pallas_call | solution.py:184
  102.3 15.4 %all-to-all-start.3 = ((f32[256,1,64]{2,1,0:T(1,128)}), f32[256,1,64]{2,1,0:T(1,128)S(1)}, u32[]{:S(2)}, u32[]{:S(2)}) async-start(f32[256,1,64]{2,1,0:T(1,128)} %broadcast_in_dim.32), calls=%async_computation.3 | async-start | bytes 262144 | tf_op jit(solution)/shard_map/all_to_all | solution.py:326
  117.7 1.7 %copy-done.5 = bf16[3,3,3,192,192]{4,3,2,1,0:T(8,128)(2,1)S(1)} copy-done((bf16[3,3,3,192,192]{4,3,2,1,0:T(8,128)(2,1)S(1)}, bf16[3,3,3,192,192]{4,3,2,1,0:T(8,128)(2,1)}, u32[]{:S(2)}) %copy-start.5) | copy-done | bytes 1990680
  119.5 4.7 %mid_a.1.refs_1_ = bf16[2,6,64,192]{3,2,1,0:T(8,128)(2,1)S(1)} custom-call(f32[3]{0:T(128)S(1)} %add_convert_fusion.flags, f32[2,192]{1,0:T(2,128)S(1)} %pad_maximum_fusion.stats, bf16[3,3,3,192,192]{4,3,2,1,0:T(8,128)(2,1)S(1)} %copy-done.5, bf16[4,4,64,192]{3,2,1,0:T(8,128)(2,1)S(1)} %all_to_all.35.refs_0_.tile_ref, ...), custom_call_target="tpu_custom_call" | custom-call | flops 2717908992 | bytes 4194304 | tf_op jit(solution)/shard_map/mid_a/pallas_call | solution.py:242
  125.0 1.2 copy.111
  126.2 4.5 %all-to-all-done.3 = f32[256,1,64]{2,1,0:T(1,128)S(1)} async-done(((f32[256,1,64]{2,1,0:T(1,128)}), f32[256,1,64]{2,1,0:T(1,128)S(1)}, u32[]{:S(2)}, u32[]{:S(2)}) %all-to-all-start.3) | async-done | bytes 65568 | tf_op jit(solution)/shard_map/all_to_all | solution.py:326
  130.7 4.1 %all-to-all-start.2 = ((bf16[4,4,64,192]{3,1,0,2:T(4,128)(2,1)}), bf16[4,4,64,192]{3,1,0,2:T(4,128)(2,1)S(1)}, u32[]{:S(2)}, u32[]{:S(2)}) async-start(bf16[4,4,64,192]{3,1,0,2:T(4,128)(2,1)} %copy.111), calls=%async_computation.2 | async-start | bytes 1048576 | tf_op jit(solution)/shard_map/all_to_all | solution.py:386
  135.5 1.7 %copy-done.2 = bf16[3,4,4,192,128]{4,3,2,1,0:T(8,128)(2,1)S(1)} copy-done((bf16[3,4,4,192,128]{4,3,2,1,0:T(8,128)(2,1)S(1)}, bf16[3,4,4,192,128]{4,3,2,1,0:T(8,128)(2,1)}, u32[]{:S(2)}) %copy-start.2) | copy-done | bytes 2359320
  138.2 6.2 %decode.1 = bf16[4,8,128,96]{3,2,1,0:T(8,128)(2,1)S(1)} custom-call(bf16[3,4,4,192,128]{4,3,2,1,0:T(8,128)(2,1)S(1)} %copy-done.2, bf16[2,6,64,192]{3,2,1,0:T(8,128)(2,1)S(1)} %collective-permute-done.2.refs_0_, bf16[2,6,64,192]{3,2,1,0:T(8,128)(2,1)S(1)} %copy-done.7, bf16[2,6,64,192]{3,2,1,0:T(8,128)(2,1)S(1)} %mid_b.1.refs_2_), custom_call_target="tpu_custom_call" | custom-call | flops 4831838208 | bytes 4194304 | tf_op jit(solution)/shard_map/decode/pallas_call | solution.py:293
  144.4 1.2 copy.114
  (88 shorter events, 19.9 us)
Async XLA Ops:
  0.6 20.0 %copy-start.11 = (bf16[4,8,128,96]{2,3,1,0:T(8,128)(2,1)S(1)}, bf16[4,8,128,96]{2,3,1,0:T(8,128)(2,1)}, u32[]{:S(2)}) copy-start(bf16[4,8,128,96]{2,3,1,0:T(8,128)(2,1)} %param.7) | copy-start | bytes 2359300
  2.1 2.9 %copy-start.8 = (bf16[4,128,2,192]{3,2,1,0:T(2,128)(2,1)}, bf16[4,128,2,192]{3,2,1,0:T(2,128)(2,1)S(1)}, u32[]{:S(2)}) copy-start(bf16[4,128,2,192]{3,2,1,0:T(2,128)(2,1)S(1)} %copy.98) | copy-start | bytes 1179652
  4.9 32.0 %all-to-all-start = ((f32[256,1,64]{2,1,0:T(1,128)}), f32[256,1,64]{2,1,0:T(1,128)S(1)}, u32[]{:S(2)}, u32[]{:S(2)}) async-start(f32[256,1,64]{2,1,0:T(1,128)} %broadcast_in_dim.29), calls=%async_computation | async-start | bytes 262144 | tf_op jit(solution)/shard_map/all_to_all | solution.py:326
  20.6 13.2 %copy-start.10 = (bf16[4,128,2,192]{1,3,2,0:T(8,128)(2,1)S(1)}, bf16[4,128,2,192]{1,3,2,0:T(8,128)(2,1)}, u32[]{:S(2)}) copy-start(bf16[4,128,2,192]{1,3,2,0:T(8,128)(2,1)} %param.4) | copy-start | bytes 1179652
  22.2 24.8 %collective-permute-start.6 = (bf16[4,3,128,96]{3,2,1,0:T(8,128)(2,1)}, bf16[4,3,128,96]{3,2,1,0:T(8,128)(2,1)}, u32[]{:S(2)}, u32[]{:S(2)}) collective-permute-start(bf16[4,3,128,96]{3,2,1,0:T(8,128)(2,1)} %get-tuple-element.27), channel_id=1, source_target_pairs={{0,8},{8,16},{16,24},{24,32},{32,40},{40,48},{48,56},{56,64},{64,7... | collective-permute-start | bytes 884744 | tf_op jit(solution)/shard_map/ppermute | solution.py:310
  25.8 21.3 %collective-permute-start.7 = (bf16[4,3,128,96]{3,2,1,0:T(8,128)(2,1)}, bf16[4,3,128,96]{3,2,1,0:T(8,128)(2,1)}, u32[]{:S(2)}, u32[]{:S(2)}) collective-permute-start(bf16[4,3,128,96]{3,2,1,0:T(8,128)(2,1)} %get-tuple-element.26), channel_id=1, source_target_pairs={{8,0},{16,8},{24,16},{32,24},{40,32},{48,40},{56,48},{64,56},{72,6... | collective-permute-start | bytes 884744 | tf_op jit(solution)/shard_map/ppermute | solution.py:310
  29.1 31.7 %collective-permute-start.10 = (bf16[2,3,128,96]{3,2,1,0:T(8,128)(2,1)}, bf16[2,3,128,96]{3,2,1,0:T(8,128)(2,1)}, u32[]{:S(2)}, u32[]{:S(2)}) collective-permute-start(bf16[2,3,128,96]{3,2,1,0:T(8,128)(2,1)} %get-tuple-element.24), channel_id=1, source_target_pairs={{9,0},{10,1},{11,2},{12,3},{13,4},{14,5},{15,6},{17,8},{18,9},{19,... | collective-permute-start | bytes 442376 | tf_op jit(solution)/shard_map/ppermute | solution.py:320
  30.4 32.7 %collective-permute-start.9 = (bf16[2,3,128,96]{3,2,1,0:T(8,128)(2,1)}, bf16[2,3,128,96]{3,2,1,0:T(8,128)(2,1)}, u32[]{:S(2)}, u32[]{:S(2)}) collective-permute-start(bf16[2,3,128,96]{3,2,1,0:T(8,128)(2,1)} %get-tuple-element.25), channel_id=1, source_target_pairs={{1,8},{2,9},{3,10},{4,11},{5,12},{6,13},{7,14},{9,16},{10,17},{11,... | collective-permute-start | bytes 442376 | tf_op jit(solution)/shard_map/ppermute | solution.py:320
  32.5 39.2 %collective-permute-start.8 = (bf16[2,8,128,96]{3,2,1,0:T(8,128)(2,1)}, bf16[2,8,128,96]{3,2,1,0:T(8,128)(2,1)}, u32[]{:S(2)}, u32[]{:S(2)}) collective-permute-start(bf16[2,8,128,96]{3,2,1,0:T(8,128)(2,1)} %slice.77), channel_id=1, source_target_pairs={{1,0},{2,1},{3,2},{4,3},{5,4},{6,5},{7,6},{9,8},{10,9},{11,10},{12... | collective-permute-start | bytes 1179656 | tf_op jit(solution)/shard_map/ppermute | solution.py:313
  35.0 1.3 copy-start.3
  36.8 15.8 %copy-start = (bf16[3,4,4,192,128]{4,3,2,1,0:T(8,128)(2,1)}, bf16[3,4,4,192,128]{4,3,2,1,0:T(8,128)(2,1)S(1)}, u32[]{:S(2)}) copy-start(bf16[3,4,4,192,128]{4,3,2,1,0:T(8,128)(2,1)S(1)} %combine_weights.1.weights) | copy-start | bytes 7077892
  36.9 18.6 %all-to-all-start.1 = ((bf16[4,128,2,192]{3,0,2,1:T(4,128)(2,1)}), bf16[4,128,2,192]{3,0,2,1:T(4,128)(2,1)}, u32[]{:S(2)}, u32[]{:S(2)}) async-start(bf16[4,128,2,192]{3,0,2,1:T(4,128)(2,1)} %copy.100), calls=%async_computation.1 | async-start | bytes 1048576 | tf_op jit(solution)/shard_map/all_to_all | solution.py:356
  52.6 41.9 %collective-permute-start.11 = (bf16[2,6,64,192]{3,2,1,0:T(8,128)(2,1)}, bf16[2,6,64,192]{3,2,1,0:T(8,128)(2,1)}, u32[]{:S(2)}, u32[]{:S(2)}) collective-permute-start(bf16[2,6,64,192]{3,2,1,0:T(8,128)(2,1)} %down_a.1.refs_0_), channel_id=1, source_target_pairs={{1,0},{2,1},{3,2},{4,3},{5,4},{6,5},{7,6},{9,8},{10,9},{11,10},{12... | collective-permute-start | bytes 884744 | tf_op jit(solution)/shard_map/ppermute | solution.py:313
  58.2 23.1 %collective-permute-start = (bf16[4,2,64,192]{3,2,1,0:T(8,128)(2,1)S(1)}, bf16[4,2,64,192]{3,2,1,0:T(8,128)(2,1)S(1)}, u32[]{:S(2)}, u32[]{:S(2)}) collective-permute-start(bf16[4,2,64,192]{3,2,1,0:T(8,128)(2,1)S(1)} %get-tuple-element.31), channel_id=1, source_target_pairs={{0,8},{8,16},{16,24},{24,32},{32,40},{40,48},{48,56},{56,64},{64,7... | collective-permute-start | bytes 589832 | tf_op jit(solution)/shard_map/ppermute | solution.py:310
  60.8 24.2 %collective-permute-start.1 = (bf16[4,2,64,192]{3,2,1,0:T(8,128)(2,1)S(1)}, bf16[4,2,64,192]{3,2,1,0:T(8,128)(2,1)S(1)}, u32[]{:S(2)}, u32[]{:S(2)}) collective-permute-start(bf16[4,2,64,192]{3,2,1,0:T(8,128)(2,1)S(1)} %get-tuple-element.30), channel_id=1, source_target_pairs={{8,0},{16,8},{24,16},{32,24},{40,32},{48,40},{56,48},{64,56},{72,6... | collective-permute-start | bytes 589832 | tf_op jit(solution)/shard_map/ppermute | solution.py:310
  63.1 54.6 %collective-permute-start.4 = (bf16[2,2,64,192]{3,2,1,0:T(8,128)(2,1)S(1)}, bf16[2,2,64,192]{3,2,1,0:T(8,128)(2,1)S(1)}, u32[]{:S(2)}, u32[]{:S(2)}) collective-permute-start(bf16[2,2,64,192]{3,2,1,0:T(8,128)(2,1)S(1)} %get-tuple-element.29), channel_id=1, source_target_pairs={{0,9},{1,10},{2,11},{3,12},{4,13},{5,14},{6,15},{8,17},{9,18},{10,... | collective-permute-start | bytes 294920 | tf_op jit(solution)/shard_map/ppermute | solution.py:320
  71.7 46.0 %collective-permute-start.5 = (bf16[2,2,64,192]{3,2,1,0:T(8,128)(2,1)S(1)}, bf16[2,2,64,192]{3,2,1,0:T(8,128)(2,1)S(1)}, u32[]{:S(2)}, u32[]{:S(2)}) collective-permute-start(bf16[2,2,64,192]{3,2,1,0:T(8,128)(2,1)S(1)} %get-tuple-element.28), channel_id=1, source_target_pairs={{8,1},{9,2},{10,3},{11,4},{12,5},{13,6},{14,7},{16,9},{17,10},{18,... | collective-permute-start | bytes 294920 | tf_op jit(solution)/shard_map/ppermute | solution.py:320
  74.4 1.7 %copy-start.1 = (bf16[3,4,4,192,128]{4,3,2,1,0:T(8,128)(2,1)S(1)}, bf16[3,4,4,192,128]{4,3,2,1,0:T(8,128)(2,1)}, u32[]{:S(2)}) copy-start(bf16[3,4,4,192,128]{4,3,2,1,0:T(8,128)(2,1)} %copy-done) | copy-start | bytes 7077892
  76.1 8.9 %copy-start.4 = (bf16[3,3,3,192,192]{4,3,2,1,0:T(8,128)(2,1)S(1)}, bf16[3,3,3,192,192]{4,3,2,1,0:T(8,128)(2,1)}, u32[]{:S(2)}) copy-start(bf16[3,3,3,192,192]{4,3,2,1,0:T(8,128)(2,1)} %weights.5) | copy-start | bytes 5971972
  81.3 36.4 %collective-permute-start.3 = (bf16[2,4,64,192]{3,2,1,0:T(8,128)(2,1)S(1)}, bf16[2,4,64,192]{3,2,1,0:T(8,128)(2,1)S(1)}, u32[]{:S(2)}, u32[]{:S(2)}) collective-permute-start(bf16[2,4,64,192]{3,2,1,0:T(8,128)(2,1)S(1)} %slice.56), channel_id=1, source_target_pairs={{0,1},{1,2},{2,3},{3,4},{4,5},{5,6},{6,7},{8,9},{9,10},{10,11},{11... | collective-permute-start | bytes 589832 | tf_op jit(solution)/shard_map/ppermute | solution.py:313
  89.7 45.8 %collective-permute-start.2 = (bf16[2,6,64,192]{3,2,1,0:T(8,128)(2,1)S(1)}, bf16[2,6,64,192]{3,2,1,0:T(8,128)(2,1)S(1)}, u32[]{:S(2)}, u32[]{:S(2)}) collective-permute-start(bf16[2,6,64,192]{3,2,1,0:T(8,128)(2,1)S(1)} %mid_b.1.refs_2_), channel_id=1, source_target_pairs={{0,1},{1,2},{2,3},{3,4},{4,5},{5,6},{6,7},{8,9},{9,10},{10,11},{11... | collective-permute-start | bytes 884744 | tf_op jit(solution)/shard_map/ppermute | solution.py:313
  102.3 28.4 %all-to-all-start.3 = ((f32[256,1,64]{2,1,0:T(1,128)}), f32[256,1,64]{2,1,0:T(1,128)S(1)}, u32[]{:S(2)}, u32[]{:S(2)}) async-start(f32[256,1,64]{2,1,0:T(1,128)} %broadcast_in_dim.32), calls=%async_computation.3 | async-start | bytes 262144 | tf_op jit(solution)/shard_map/all_to_all | solution.py:326
  117.7 1.8 %copy-start.5 = (bf16[3,3,3,192,192]{4,3,2,1,0:T(8,128)(2,1)S(1)}, bf16[3,3,3,192,192]{4,3,2,1,0:T(8,128)(2,1)}, u32[]{:S(2)}) copy-start(bf16[3,3,3,192,192]{4,3,2,1,0:T(8,128)(2,1)} %weights.5) | copy-start | bytes 5971972
  124.2 0.7 copy-start.6
  130.7 15.9 %all-to-all-start.2 = ((bf16[4,4,64,192]{3,1,0,2:T(4,128)(2,1)}), bf16[4,4,64,192]{3,1,0,2:T(4,128)(2,1)S(1)}, u32[]{:S(2)}, u32[]{:S(2)}) async-start(bf16[4,4,64,192]{3,1,0,2:T(4,128)(2,1)} %copy.111), calls=%async_computation.2 | async-start | bytes 1048576 | tf_op jit(solution)/shard_map/all_to_all | solution.py:386
  135.5 1.7 %copy-start.2 = (bf16[3,4,4,192,128]{4,3,2,1,0:T(8,128)(2,1)S(1)}, bf16[3,4,4,192,128]{4,3,2,1,0:T(8,128)(2,1)}, u32[]{:S(2)}) copy-start(bf16[3,4,4,192,128]{4,3,2,1,0:T(8,128)(2,1)} %copy-done) | copy-start | bytes 7077892
  137.2 1.0 copy-start.7
  144.4 2.6 %copy-start.9 = (bf16[4,128,2,192]{3,2,1,0:T(2,128)(2,1)S(1)}, bf16[4,128,2,192]{3,2,1,0:T(2,128)(2,1)}, u32[]{:S(2)}) copy-start(bf16[4,128,2,192]{3,2,1,0:T(2,128)(2,1)} %copy-done.8) | copy-start | bytes 1179652

commit v2 on v0

v2 whole, which is shorter than its diff:
```python
import functools

import jax
import jax.numpy as jnp
from jax import lax
from jax.experimental import pallas as pl
from jax.experimental.pallas import tpu as pltpu
from jax.sharding import PartitionSpec as P

GROUPS = 32
F32 = jnp.float32
BF16 = jnp.bfloat16
VMEM_LIMIT = 32 * 2**20
TAPS = ((2,), (1, 2), (0, 1), (0,))
EXTRA = 16


def vmem(count):
    return [pl.BlockSpec(memory_space=pltpu.VMEM)] * count


def smem():
    return pl.BlockSpec(memory_space=pltpu.SMEM)


def anywhere():
    return pl.BlockSpec(memory_space=pltpu.HBM)


def call(kernel, name, outs, in_specs, scratch, flops, moved_bytes=4 * 2**20):
    return pl.pallas_call(
        kernel,
        name=name,
        out_shape=outs,
        in_specs=in_specs,
        out_specs=jax.tree.map(lambda _: pl.BlockSpec(memory_space=pltpu.VMEM), outs),
        scratch_shapes=scratch,
        compiler_params=pltpu.CompilerParams(vmem_limit_bytes=VMEM_LIMIT),
        cost_estimate=pl.CostEstimate(flops=flops, bytes_accessed=moved_bytes, transcendentals=0),
    )


def array(shape, dtype=BF16):
    return jax.ShapeDtypeStruct(shape, dtype)


def kept(shape, dtype=BF16):
    return pltpu.VMEM(shape, dtype)


def near(block):
    return pltpu.with_memory_space_constraint(block, pltpu.VMEM)


def far(block):
    return pltpu.with_memory_space_constraint(block, pltpu.HBM)


def dot(lhs, rhs):
    return jnp.dot(lhs, rhs, preferred_element_type=F32)


def nt_dot(lhs, rhs):
    return lax.dot_general(lhs, rhs, (((1,), (1,)), ((), ())), preferred_element_type=F32)


def one_hot(rows, cols, place):
    width = min(cols, 128)
    target = place(lax.broadcasted_iota(jnp.int32, (rows, width), 0))
    target = target - lax.broadcasted_iota(jnp.int32, (rows, width), 1)
    blocks = [
        jnp.where(target == at, 1.0, 0.0).astype(BF16)[:, : cols - at]
        for at in range(0, cols, width)
    ]
    return jnp.concatenate(blocks, axis=1) if len(blocks) > 1 else blocks[0]


def same_group(chans):
    size = chans // GROUPS
    row = lax.broadcasted_iota(jnp.int32, (chans, chans), 0).astype(F32)
    col = lax.broadcasted_iota(jnp.int32, (chans, chans), 1).astype(F32)
    row, col = (jnp.floor((index + 0.5) / size) for index in (row, col))
    return jnp.where(row == col, 1.0, 0.0)


def group_sum(channels):
    return jnp.dot(
        channels,
        same_group(channels.shape[1]),
        precision=lax.Precision.HIGHEST,
        preferred_element_type=F32,
    )


def split_3(value):
    terms = []
    for _ in range(3):
        terms.append(value.astype(BF16).astype(F32))
        value = value - terms[-1]
    return terms


def extra_rows(one, two):
    rest = jnp.concatenate([one[:, 128:], two[:, 128:]], axis=1)
    row = lax.broadcasted_iota(jnp.int32, (EXTRA, 128), 0)
    out = jnp.zeros((EXTRA, 128), F32)
    for n, term in enumerate(split_3(one[:, :128]) + split_3(two[:, :128]) + split_3(rest)):
        out = jnp.where(row == n, term, out)
    return out


def from_extra(block):
    block = block.astype(F32)
    row = lax.broadcasted_iota(jnp.int32, block.shape, 1)
    one, two, rest = (
        jnp.sum(jnp.where((row >= k) & (row < k + 3), block, 0.0), axis=1) for k in (0, 3, 6)
    )
    return (
        jnp.concatenate([one, rest[:, :64]], axis=1),
        jnp.concatenate([two, rest[:, 64:]], axis=1),
    )


def store_dense(ref, frame, value):
    frames = ref.shape[0] * 2 // 3
    lane = 64 * (frame % 2)
    ref[frame] = value[..., :128]
    ref[frames + frame // 2, :, :, lane : lane + 64] = value[..., 128:]


def load_dense(ref, frame):
    frames = ref.shape[0] * 2 // 3
    lane = 64 * (frame % 2)
    return ref[frame], ref[frames + frame // 2, :, :, lane : lane + 64]


def fill(buffer, pieces, transform):
    rows = buffer.shape[1]
    for ref, source, count, t0, later in pieces:

        def one_frame(i, carry):
            for r in range(rows):
                buffer[t0 + i, r] = transform(ref[source + i, r], r, later)
            return carry

        lax.fori_loop(0, count, one_frame, 0)


def from_left(value, cols):
    column = lax.broadcasted_iota(jnp.int32, value.shape, 0) & (cols - 1)
    return jnp.where(column == 0, 0.0, pltpu.roll(value, 1, 0))


def from_right(value, cols):
    size = value.shape[0]
    column = lax.broadcasted_iota(jnp.int32, value.shape, 0) & (cols - 1)
    return jnp.where(column == cols - 1, 0.0, pltpu.roll(value, size - 1, 0))


def fetch(source, target, sem):
    copy = pltpu.make_async_copy(source, target, sem)
    copy.start()
    return copy


def combine_kernel(w_ref, out_ref):
    outs = w_ref.shape[4]

    def one_time(a, carry):
        w = [[w_ref[a, b, d].astype(F32) for d in range(3)] for b in range(3)]
        for p in range(4):
            rows = [functools.reduce(jnp.add, [w[b][d] for b in TAPS[p]]) for d in range(3)]
            for q in range(4):
                value = functools.reduce(jnp.add, [rows[d] for d in TAPS[q]])
                out_ref[a, p, q] = jnp.pad(value, ((0, 0), (0, 128 - outs))).astype(BF16)
        return carry

    lax.fori_loop(0, 3, one_time, 0)


def combined_weights(conv_two):
    shape = kept((3, 4, 4, conv_two.shape[3], 128))
    return call(combine_kernel, "combine_weights", shape, vmem(1), [], 10**6)(conv_two)


def edges_kernel(x_ref, first_ref, last_ref):
    lines = x_ref.shape[1]
    first_ref[...] = x_ref[:, 0:3]
    last_ref[...] = x_ref[:, lines - 3 : lines]


def edges(pixels):
    frames, _, outs, wide = pixels.shape
    shape = array((frames, 3, outs, wide))
    return call(edges_kernel, "edges", (shape, shape), vmem(1), [], 10**6)(pixels)


def moments_kernel(x_ref, out_ref):
    frames, stripe, chans, height = x_ref.shape
    total = jnp.zeros((chans, height), F32)
    for t in range(frames):
        for c in range(stripe):
            total = total + x_ref[t, c].astype(F32)
    mean = jnp.sum(total, axis=1, keepdims=True) / float(frames * stripe * height)
    spread = jnp.zeros((chans, height), F32)
    for t in range(frames):
        for c in range(stripe):
            spread = spread + (x_ref[t, c].astype(F32) - mean) ** 2
    spread = jnp.sum(spread, axis=1, keepdims=True)
    rows = [jnp.broadcast_to(v, (chans, 128)).T[0:1] for v in (mean, spread)]
    out_ref[...] = jnp.broadcast_to(jnp.concatenate(rows, axis=0)[None], out_ref.shape)


def moments(tokens, clips):
    shape = array((clips, 2, tokens.shape[2]), F32)
    return call(moments_kernel, "moments", shape, vmem(1), [], 10**6)(tokens)


def merged(means, spreads, held):
    mean = jnp.sum(means, axis=0, keepdims=True) / means.shape[0]
    spread = jnp.sum(spreads, axis=0, keepdims=True)
    return mean, spread + held * jnp.sum((means - mean) ** 2, axis=0, keepdims=True)


def pack_kernel(held, x_ref, parts_ref, out_ref):
    frames, stripe, chans, height = x_ref.shape
    seqs = out_ref.shape[0]
    rows = height // seqs
    select = one_hot(8 * seqs, height, lambda i: rows * (i >> 3) - 2 + (i & 7))

    def picked(x):
        return nt_dot(select, x).reshape(seqs, 8, 128)

    for n in range(frames // 2):
        pair = [x_ref.at[2 * n + k] for k in range(2)]
        blocks = [[x[c, 0:128] for c in range(stripe)] for x in pair]
        tails = [[x[c, 128:chans] for x in pair] for c in range(stripe)]
        blocks.append([jnp.concatenate(tail, axis=0) for tail in tails])
        for k, columns in enumerate(blocks):
            at = 48 * n + 16 * k
            rows_of = [picked(column) for column in columns]
            out_ref[:, at : at + 16] = jnp.concatenate(rows_of, axis=1).astype(BF16)
    extra = extra_rows(*merged(parts_ref[:, 0], parts_ref[:, 1], held)).astype(BF16)
    out_ref[:, 24 * frames :] = jnp.broadcast_to(extra[None], (seqs, EXTRA, 128))


def pack(tokens, parts, seqs, held):
    shape = array((seqs, 24 * tokens.shape[0] + EXTRA, 128))
    return call(functools.partial(pack_kernel, held), "pack", shape, vmem(2), [], 10**9)(
        tokens, parts
    )


def unpack_kernel(held, x_ref, tile_ref, last_ref, stats_ref):
    seqs = x_ref.shape[0]
    frames, rows, cols, chans = tile_ref.shape
    size = rows * cols

    order = one_hot(size, 16 * seqs, lambda i: ((i >> 1) & 31) * 16 + (i & 1) * 8 + (i >> 6))
    for n in range(frames // 2):
        blocks = [x_ref[:, 48 * n + 16 * k : 48 * n + 16 * (k + 1)] for k in range(3)]
        blocks = [block.reshape(16 * seqs, 128) for block in blocks]
        main = dot(order, jnp.concatenate(blocks[:2], axis=1)).astype(BF16)
        rest = dot(order, blocks[2]).astype(BF16)
        for k in range(2):
            t = 2 * n + k
            for ref, at in ((tile_ref, t), (last_ref, t - frames + 2)):
                if at >= 0:
                    part = main[:, 128 * k : 128 * (k + 1)]
                    ref[at, :, :, 0:128] = part.reshape(rows, cols, 128)
                    part = rest[:, 64 * k : 64 * (k + 1)]
                    ref[at, :, :, 128:chans] = part.reshape(rows, cols, 64)
    size = chans // GROUPS
    means, spreads = from_extra(x_ref[:, 24 * frames :])
    mean = group_sum(jnp.broadcast_to(jnp.sum(means, axis=0, keepdims=True), (8, chans)))
    mean = mean[0:1] / (seqs * size)
    spread = jnp.sum(spreads, axis=0, keepdims=True)
    spread = spread + held * jnp.sum((means - mean) ** 2, axis=0, keepdims=True)
    var = group_sum(jnp.broadcast_to(spread, (8, chans)))[0:1] / (held * seqs * size)
    stats_ref[...] = jnp.concatenate([mean, lax.rsqrt(var + 1e-06)], axis=0)


def unpack(blocks, frames, cols, chans, held):
    return call(
        functools.partial(unpack_kernel, held),
        "unpack",
        (
            kept((frames, 8, cols, chans)),
            kept((2, 8, cols, chans)),
            kept((2, chans), F32),
        ),
        vmem(1),
        [],
        10**9,
    )(blocks)


def down_kernel(first, plan, weights, flags, pixels, above, below, store, buffer):
    _, _, cols, _ = buffer.shape[1:]
    rows, outs = buffer.shape[2] - 1, weights.shape[3]
    chans, wide = pixels.shape[2:]
    select = one_hot(2 * cols, wide, lambda i: 2 * (i & (cols - 1)) + (i // cols))
    blank = jnp.zeros((128 - chans, wide), BF16)

    def one_frame(i, carry):
        at = first + i
        lines = [above.at[at, r] for r in range(3)]
        lines += [pixels.at[at, r] for r in range(pixels.shape[1])]
        lines += [below.at[at, r] for r in range(3)]
        for n in range(0, len(lines), 2):
            pair = [lines[n][...], blank, lines[n + 1][...], blank]
            picked = nt_dot(select, jnp.concatenate(pair, axis=0)).astype(BF16)
            for k in range(2):
                for j in range(2):
                    buffer[i, k, n // 2, :, 128 * j : 128 * (j + 1)] = picked[
                        cols * j : cols * (j + 1), 128 * k : 128 * (k + 1)
                    ]
        return carry

    lax.fori_loop(0, buffer.shape[0], one_frame, 0)

    size = rows * cols

    def products(frame, count, a, totals):
        here, left, right = totals
        frames = slice(frame - first, frame - first + count)
        lines = [
            buffer[frames, p % 2, p // 2 : p // 2 + rows].reshape(count * size, 256)
            for p in range(4)
        ]
        w = weights.at[a]
        for p in range(4):
            here = here + nt_dot(lines[p], jnp.concatenate([w[p, 1], w[p, 2]], axis=-1))
        for p in range(0, 4, 2):
            odd = jnp.concatenate([lines[p][:, 128:], lines[p + 1][:, 128:]], axis=-1)
            left = left + nt_dot(odd, jnp.concatenate([w[p, 0], w[p + 1, 0]], axis=-1))
            even = jnp.concatenate([lines[p][:, :128], lines[p + 1][:, :128]], axis=-1)
            right = right + nt_dot(even, jnp.concatenate([w[p, 3], w[p + 1, 3]], axis=-1))
        return here, left, right

    def zeros(count):
        return [jnp.zeros((count * size, outs), F32) for _ in range(3)]

    for n, (terms, extra, member) in enumerate(plan):
        totals = zeros(2)
        for frame, a in terms:
            totals = products(frame, 2, a, totals)
        here, left, right = totals
        total = here + from_left(left, cols) + from_right(right, cols)
        parts = [total[:size], total[size:]]
        if extra:
            here, left, right = products(*extra[:1], 1, *extra[1:], zeros(1))
            more = here + from_left(left, cols) + from_right(right, cols)
            parts[member] = parts[member] + more
        for k, part in enumerate(parts):
            part = part.reshape(rows, cols, outs)
            store(
                2 * n + k,
                [part[0:1] * flags[0], part[1 : rows - 1], part[rows - 1 :] * flags[1]],
            )


def early_kernel(plan, weights, flags, pixels, above, below, own_ref, sent_ref, buffer):
    def store(n, parts):
        value = jnp.concatenate([part.astype(BF16) for part in parts], axis=0)
        store_dense(sent_ref, n, value)
        if n < 2:
            own_ref[n] = value

    down_kernel(0, plan, weights, flags, pixels, above, below, store, buffer)


def late_kernel(first, plan, one_hbm, weights, flags, pixels, above, below, *refs):
    out_ref, one_ref, buffer, sem = refs
    copy = pltpu.make_async_copy(one_hbm, one_ref, sem)
    copy.start()

    def store(n, parts):
        out_ref[n] = jnp.concatenate(parts, axis=0)

    down_kernel(first, plan, weights, flags, pixels, above, below, store, buffer)
    copy.wait()


def down_cost(plan, size):
    return 2 * sum(2 * len(terms) + 1 for terms, *_ in plan) * size * 8 * 65536


def down_early(weights, flags, pixels, above, below, rows, cols):
    frames, outs = pixels.shape[0], weights.shape[3]
    plan = ((((0, 2), (1, 1), (2, 0)), (), 0), (((0, 0),), (0, 1), 1))
    return call(
        functools.partial(early_kernel, plan),
        "down_early",
        (kept((2, rows, cols, outs)), array((6, rows, cols, 128))),
        vmem(1) + [smem()] + vmem(3),
        [pltpu.VMEM((frames, 2, rows + 1, cols, 256), BF16)],
        down_cost(plan, rows * cols),
    )(weights, flags, pixels, above, below)


def down_late(conv_one, weights, flags, pixels, above, below, rows, cols):
    frames, outs = pixels.shape[0], weights.shape[3]
    plan = ((((2, 2),), (3, 1), 0),)
    return call(
        functools.partial(late_kernel, frames - 2, plan),
        "down_late",
        (kept((2, rows, cols, outs), F32), kept(conv_one.shape)),
        [anywhere()] + vmem(1) + [smem()] + vmem(3),
        [pltpu.VMEM((2, 2, rows + 1, cols, 256), BF16), pltpu.SemaphoreType.DMA],
        down_cost(plan, rows * cols),
    )(far(conv_one), weights, flags, pixels, above, below)


def back_kernel(stats, weights, tile_ref, early_ref, late_ref, next_ref, out_ref, buffer, rest):
    seqs = out_ref.shape[0]
    frames, _, cols, chans = tile_ref.shape
    rows = buffer.shape[1] - 2
    size = 2 * rows * cols
    for k in range(2):
        buffer[k] = early_ref[k]
        main, tail = load_dense(next_ref, k)
        buffer[frames + k, :, :, 0:128] = main
        buffer[frames + k, :, :, 128:chans] = tail
        main, tail = load_dense(next_ref, 2 + k)
        late = late_ref[k]
        main = (late[..., :128] + main.astype(F32)).astype(BF16)
        tail = (late[..., 128:] + tail.astype(F32)).astype(BF16)
        buffer[frames - 2 + k, :, :, 0:128] = main
        buffer[frames - 2 + k, :, :, 128:chans] = tail
    mean = stats[0:1]
    scale = stats[1:2]
    order = one_hot(
        size,
        size,
        lambda i: ((i >> 3) & 1) * (rows * cols) + (i & 3) * cols + 2 * (i >> 4) + ((i >> 2) & 1),
    )

    def two_frames(n, carry):
        first_sum, second_sum = carry
        t = 2 * n
        total = [jnp.zeros((size, chans), F32) for _ in range(3)]
        for dt in range(3):
            for dr in range(3):
                lhs = buffer[pl.ds(t + dt, 2), dr : dr + rows].reshape(size, chans)
                for dc in range(3):
                    total[dc] = total[dc] + nt_dot(lhs, weights[2 - dt, 2 - dr, 2 - dc])
        total = total[1] + from_left(total[0], cols) + from_right(total[2], cols)
        tile = tile_ref[pl.ds(t, 2), 2 : 2 + rows].reshape(size, chans)
        normed = (tile.astype(F32) - mean) * scale
        sigmoid = 1.0 / (1.0 + jnp.exp(-normed))
        grad = total * sigmoid * (1.0 + normed * (1.0 - sigmoid))
        first_sum = first_sum + jnp.sum(grad, axis=0, keepdims=True)
        second_sum = second_sum + jnp.sum(grad * normed, axis=0, keepdims=True)
        own = buffer[pl.ds(t, 2), 1 : 1 + rows].reshape(size, chans)
        base = (own.astype(F32) + grad * scale).astype(BF16)
        home = dot(order, base)
        main = home[:, :128].reshape(seqs, 16, 128).astype(BF16)
        out_ref[:, pl.ds(pl.multiple_of(16 * n, 16), 16)] = main
        tail = home[:, 128:].reshape(seqs, 2, 8, chans - 128)
        for k in range(2):
            rest[n, :, :, 64 * k : 64 * (k + 1)] = tail[:, k]
        return first_sum, second_sum

    none = jnp.zeros((1, chans), F32)
    sums = lax.fori_loop(0, frames // 2, two_frames, (none, none))
    both = jnp.concatenate([rest[n] for n in range(frames // 2)], axis=1)
    out_ref[:, 8 * frames : 12 * frames] = both.astype(BF16)
    extra = extra_rows(*sums).astype(BF16)
    out_ref[:, 12 * frames :] = jnp.broadcast_to(extra[None], (seqs, EXTRA, 128))


def back(stats, weights, tile, early, late, following, seqs):
    frames = tile.shape[0]
    _, ext, cols, chans = early.shape
    return call(
        back_kernel,
        "back",
        array((seqs, 12 * frames + EXTRA, 128)),
        vmem(6),
        [
            pltpu.VMEM((frames + 2, ext, cols, chans), BF16),
            pltpu.VMEM((frames // 2, seqs, 8, 128), F32),
        ],
        2 * frames * (ext - 2) * cols * 27 * 65536,
    )(stats, weights, tile, early, late, following)


def sums_kernel(x_ref, out_ref):
    one, two = from_extra(x_ref[...])
    sums = [jnp.sum(v, axis=0, keepdims=True) for v in (one, two)]
    out_ref[...] = jnp.broadcast_to(jnp.concatenate(sums, axis=0)[None], out_ref.shape)


def local_sums(blocks, frames, chans, clips):
    seqs = blocks.shape[0]
    at = 12 * frames // EXTRA
    return pl.pallas_call(
        sums_kernel,
        name="local_sums",
        grid=(1,),
        out_shape=array((clips, 2, chans), F32),
        in_specs=[pl.BlockSpec((seqs, EXTRA, 128), lambda i: (0, at, 0))],
        out_specs=pl.BlockSpec((clips, 2, chans), lambda i: (0, 0, 0)),
        compiler_params=pltpu.CompilerParams(vmem_limit_bytes=VMEM_LIMIT),
        cost_estimate=pl.CostEstimate(flops=10**6, bytes_accessed=10**5, transcendentals=0),
    )(blocks)


def token_kernel(count, x_ref, tokens_ref, stats_ref, parts_ref, out_ref):
    frames, stripe, chans, height = tokens_ref.shape
    seqs = x_ref.shape[0]
    sums = jnp.sum(parts_ref[...], axis=0)
    sums = group_sum(jnp.concatenate([sums, jnp.zeros((6, chans), F32)], axis=0)) / count
    first, second = (jnp.broadcast_to(sums[k : k + 1], (128, chans)).T for k in range(2))
    mean, scale = (jnp.broadcast_to(stats_ref[k : k + 1], (128, chans)).T for k in range(2))
    eye = one_hot(128, 128, lambda i: i)
    lanes = 16 * seqs

    order = one_hot(lanes, lanes, lambda i: ((i >> 2) & 3) * height + (i >> 4) * 4 + (i & 3))

    def turned(at):
        block = x_ref[:, at : at + 16].reshape(lanes, 128)
        return dot(nt_dot(eye, block).astype(BF16), order)

    rest = turned(8 * frames)
    for n in range(frames // 2):
        main = turned(16 * n)
        for k in range(2 * stripe):
            t, c = 2 * n + k // stripe, k % stripe
            at = stripe * n + c
            base = jnp.concatenate(
                [
                    main[:, height * k : height * (k + 1)],
                    rest[64 * (k // stripe) : 64 * (k // stripe + 1), height * at : height * (at + 1)],
                ],
                axis=0,
            )
            normed = (tokens_ref[t, c].astype(F32) - mean) * scale
            out_ref[t, c] = (base - (first + normed * second) * scale).astype(BF16)


def token_gradient(blocks, tokens, stats, parts, count):
    return call(
        functools.partial(token_kernel, count),
        "token_gradient",
        array(tokens.shape),
        vmem(4),
        [],
        10**9,
    )(blocks, tokens, stats, parts)


def fetch(source, target, sems):
    copies = [pltpu.make_async_copy(source.at[k], target.at[k], sems.at[k]) for k in range(3)]
    for copy in copies:
        copy.start()
    return copies


def mid_kernel(flags, stats, w_hbm, tile_ref, before_ref, out_ref, sent_ref, buffer, weights, sems):
    copies = fetch(w_hbm, weights, sems)
    frames, rows, cols, chans = out_ref.shape
    size = 2 * rows * cols
    mean = stats[0:1]
    scale = stats[1:2]

    def activate(value, row, later):
        normed = (value.astype(F32) - mean) * scale
        act = normed / (1.0 + jnp.exp(-normed))
        if row < 2:
            act = act * flags[0]
        if row >= rows:
            act = act * flags[1]
        if later:
            act = act * flags[2]
        return act.astype(BF16)

    fill(buffer, [(before_ref, 0, 2, 0, True), (tile_ref, 0, frames, 2, False)], activate)
    for copy in copies:
        copy.wait()

    def two_frames(n, carry):
        t = 2 * n
        total = [jnp.zeros((size, chans), F32) for _ in range(3)]
        for dt in range(3):
            for dr in range(3):
                lhs = buffer[pl.ds(t + dt, 2), dr : dr + rows].reshape(size, chans)
                for dc in range(3):
                    total[dc] = total[dc] + dot(lhs, weights[dt, dr, dc])
        total = total[1] + from_left(total[0], cols) + from_right(total[2], cols)
        total = total.reshape(2, rows, cols, chans)
        total = total + tile_ref[pl.ds(t, 2), 1 : 1 + rows].astype(F32)
        out_ref[pl.ds(t, 2), 0:1] = (total[:, 0:1] * flags[0]).astype(BF16)
        out_ref[pl.ds(t, 2), 1 : rows - 1] = total[:, 1 : rows - 1].astype(BF16)
        out_ref[pl.ds(t, 2), rows - 1 : rows] = (total[:, rows - 1 :] * flags[1]).astype(BF16)
        return carry

    lax.fori_loop(0, frames // 2, two_frames, 0)
    for k in range(2):
        store_dense(sent_ref, k, out_ref[frames - 2 + k])


def middle(flags, stats, weights, tile, before):
    frames, ext, cols, chans = tile.shape
    rows = ext - 2
    return call(
        mid_kernel,
        "middle",
        (kept((frames, rows, cols, chans)), array((3, rows, cols, 128))),
        [smem()] + vmem(1) + [anywhere()] + vmem(2),
        [
            pltpu.VMEM((frames + 2, ext, cols, chans), BF16),
            pltpu.VMEM(weights.shape, BF16),
            pltpu.SemaphoreType.DMA((3,)),
        ],
        2 * frames * rows * cols * 27 * 65536,
    )(flags, stats, far(weights), tile, before)


def decode_kernel(w_hbm, before_ref, mid_ref, out_ref, buffer, wide, weights, sems):
    copies = fetch(w_hbm, weights, sems)
    frames, _, cols, chans = mid_ref.shape
    lines, outs, _ = out_ref.shape[1:]
    rows = lines // 2
    for k in range(2):
        main, tail = load_dense(before_ref, k)
        buffer[k, :, :, 0:128] = main
        buffer[k, :, :, 128:chans] = tail
    buffer[2:] = mid_ref[...]
    eye = one_hot(outs, 128, lambda i: i)
    size = 2 * rows * cols

    for t in range(0, frames, 2):
        for i, taps in enumerate((((0, 3), (1, 1)), ((1, 2), (2, 0)))):
            here, aside = (jnp.zeros((size, 256), F32) for _ in range(2))
            for dt in range(3):
                if t + i == 0:
                    copies[dt].wait()
                for dr, p in taps:
                    w = weights.at[dt, p]
                    lhs = buffer[t + dt : t + dt + 2, dr : dr + rows].reshape(size, chans)
                    here = here + dot(lhs, jnp.concatenate([w[1], w[2]], axis=-1))
                    aside = aside + dot(lhs, jnp.concatenate([w[3], w[0]], axis=-1))
            even = (here[:, :128] + from_left(aside[:, :128], cols)).reshape(2, rows, cols, 128)
            odd = (here[:, 128:] + from_right(aside[:, 128:], cols)).reshape(2, rows, cols, 128)
            for k in range(2):
                for r in range(rows):
                    wide[k, 2 * r + i, pl.ds(0, cols, stride=2), :] = even[k, r]
                    wide[k, 2 * r + i, pl.ds(1, cols, stride=2), :] = odd[k, r]
        for k in range(2):
            for r in range(rows):
                pair = wide[k, 2 * r : 2 * r + 2].reshape(4 * cols, 128).astype(BF16)
                turned = nt_dot(eye, pair).astype(BF16)
                out_ref[t + k, 2 * r] = turned[:, 0 : 2 * cols]
                out_ref[t + k, 2 * r + 1] = turned[:, 2 * cols :]


def decode(weights, before, mid, outs):
    frames, ext, cols, chans = mid.shape
    rows = ext - 2
    return call(
        decode_kernel,
        "decode",
        array((frames, 2 * rows, outs, 2 * cols)),
        [anywhere()] + vmem(2),
        [
            pltpu.VMEM((frames + 2, ext, cols, chans), BF16),
            pltpu.VMEM((2, 2 * rows, 2 * cols, 128), F32),
            pltpu.VMEM(weights.shape, BF16),
            pltpu.SemaphoreType.DMA((3,)),
        ],
        2 * frames * rows * cols * 24 * 65536,
    )(far(weights), before, mid)


def moved(block, clip_step, seq_step):
    clips, seqs = lax.axis_size("clip"), lax.axis_size("seq")
    if clip_step == 0:
        route = [(i - seq_step, i) for i in range(seqs) if 0 <= i - seq_step < seqs]
        return lax.ppermute(block, "seq", route)
    if seq_step == 0:
        route = [(i - clip_step, i) for i in range(clips) if 0 <= i - clip_step < clips]
        return lax.ppermute(block, "clip", route)
    route = [
        ((s - seq_step) * clips + c - clip_step, s * clips + c)
        for s in range(seqs)
        for c in range(clips)
        if 0 <= c - clip_step < clips and 0 <= s - seq_step < seqs
    ]
    return lax.ppermute(block, ("seq", "clip"), route)


def exchanged(blocks, axis):
    return lax.all_to_all(blocks, axis, 0, 0, tiled=True)


def body(tokens, conv_one, conv_two, pixel_grad):
    frames, height, stripe, chans = tokens.shape
    lines, wide, outs = pixel_grad.shape[1:]
    rows, cols = lines // 2, wide // 2
    clips, seqs = lax.axis_size("clip"), lax.axis_size("seq")
    clip, seq = lax.axis_index("clip"), lax.axis_index("seq")
    flags = jnp.stack([seq != 0, seq != seqs - 1, clip != 0]).astype(F32)
    tokens = tokens.transpose(0, 2, 3, 1)
    pixels = pixel_grad.transpose(0, 1, 3, 2)
    held = float(frames * height * stripe)

    own_parts = moments(tokens, clips)
    pixels, own_parts = lax.optimization_barrier((pixels, own_parts))
    parts = exchanged(own_parts, "clip")
    first, last = edges(pixels)
    above, below = moved(last, 0, 1), moved(first, 0, -1)
    packed = pack(tokens, parts, seqs, held)
    both = combined_weights(conv_two)
    above, below, both, packed = lax.optimization_barrier((above, below, both, packed))

    blocks = exchanged(packed, "seq")
    early, sent = down_early(near(both), flags, pixels, above, below, rows + 2, cols)
    following = moved(sent, -1, 0)
    early = near(early)
    tile, tile_last, stats = unpack(blocks, frames, cols, chans, held * clips)
    tile_z = moved(tile_last, 1, 0)
    above, below, tile = lax.optimization_barrier((above, below, tile))
    tile, stats = near(tile), near(stats)

    late, near_one = down_late(conv_one, near(both), flags, pixels, above, below, rows + 2, cols)
    blocks = back(stats, near(near_one), tile, early, near(late), following, seqs)
    home = exchanged(blocks, "seq")

    mid, mid_last = middle(flags, stats, conv_one, tile, tile_z)
    decoded = decode(both, moved(mid_last, 1, 0), near(mid), outs)

    sums = exchanged(local_sums(home, frames, chans, clips), "clip")
    sums, decoded = lax.optimization_barrier((sums, decoded))
    count = held * seqs * clips * (chans // GROUPS)
    token_grad = token_gradient(home, tokens, stats, sums, count)
    return (decoded.transpose(0, 1, 3, 2), token_grad.transpose(0, 3, 1, 2))


def solution(mesh):
    return jax.shard_map(
        body,
        mesh=mesh,
        in_specs=(P("clip", None, "seq", None), P(), P(), P("clip", "seq", None, None)),
        out_specs=(P("clip", "seq", None, None), P("clip", None, "seq", None)),
        check_vma=False,
    )
```

time: 596 us -> 105 us (0.18)
  blocking collectives: 236 us -> 0 us
  local copies, waits for them, and re-layouts: 141 us -> 6.33 us
  matrix products: 60.5 us -> 0 us
  other arithmetic: 50.7 us -> 0.08 us
  Pallas kernels: 0 us -> 41.4 us
  loops' own time: 32 us -> 0 us
  starting transfers between devices: 52.6 us -> 42 us
    psum x3 -> x0, blocking collectives: 236 us -> none  [the longest x1 82.6 us: body(): lax.psum(jnp.sum(values, axis=(0, 1, 2, 4), keepdims=True), ('seq', 'clip'))]
    slice x40 -> x0, local copies, waits for them, and re-layouts: 65.4 us -> none  [the longest x16 41.4 us: one_frame(): window[:, :, 0:cols]]
    dot_general x144 -> x0, matrix products: 60.5 us -> none  [one_frame(): jnp.dot(piece, flat_kernel[tap_time, tap_row], preferred_element_type=jnp...]
    pallas_call x0 -> x12, Pallas kernels: none -> 41.4 us  [the longest x1 8.8 us: middle(): call(mid_kernel, 'middle', (kept((frames, rows, cols, chans)), array((3,...]
    concatenate x22 -> x0, other arithmetic: 36.4 us -> none  [the longest x16 20.7 us: one_frame(): jnp.concatenate([window[:, :, 0:cols], window[:, :, 1:cols + 1], window[:...]
    another operation x4 -> x0, loops' own time: 32 us -> none  [causal_conv(): return lax.map(one_frame, jnp.arange(frames, dtype=jnp.int32))]
    ppermute x12 -> x5, starting transfers between devices: 35.5 us -> 13.9 us  [the longest x2 7.14 us: moved(): return lax.ppermute(block, 'seq', route)]
    transpose x4 -> x0, local copies, waits for them, and re-layouts: 12.7 us -> none  [flipped(): return jnp.swapaxes(kernel[::-1, ::-1, ::-1], 3, 4)]
  transfers between devices with their start and end apart: 14 -> 9, of which waited for: 6 -> 4; matrix products, arithmetic and copies ran while one was open for 8% -> 0% of each run, Pallas kernels for 0% -> 37%
where the time goes in v2:
time: 105 us; the launch traced here: 103 us
  starting transfers between devices  42 us (40%)
  Pallas kernels  41.4 us (39%)
  waiting for transfers between devices  12.8 us (12%)
  local copies, waits for them, and re-layouts  6.33 us (6%)
    all_to_all x4, starting transfers between devices, exchanged(): return lax.all_to_all(blocks, axis, 0, 0, tiled=True)  28.1 us
    all_to_all x4, waiting for transfers between devices, exchanged(): return lax.all_to_all(blocks, axis, 0, 0, tiled=True)  10.7 us
    pallas_call x1, Pallas kernels, middle(): call(mid_kernel, 'middle', (kept((frames, rows, cols, chans)), array((3,...  8.8 us
    pallas_call x1, Pallas kernels, back(): call(back_kernel, 'back', array((seqs, 12 * frames + EXTRA, 128)), vmem(6...  7.83 us
    pallas_call x1, Pallas kernels, down_early(): call(functools.partial(early_kernel, plan), 'down_early', (kept((2, rows,...  7.53 us
    ppermute x2, starting transfers between devices, moved(): return lax.ppermute(block, 'seq', route)  7.14 us
    ppermute x3, starting transfers between devices, moved(): return lax.ppermute(block, 'clip', route)  6.71 us
    unnamed x22, local copies, waits for them, and re-layouts  6.33 us
  transfers between devices with their start and end apart: 9, of which 4 were waited for; matrix products, arithmetic and copies ran while one was open for 0% of the time, Pallas kernels for 37%

profile of v2, /device:TPU:1, one launch (start us, length us, event | category | flops | bytes accessed | tf_op | source)
XLA Modules:
  0.0 103.4 jit_solution(17246971614632738463)
XLA Ops:
  0.6 1.0 copy-done.5
  1.6 0.9 moments.1
  2.6 1.1 %copy-done.1 = bf16[4,8,128,96]{2,3,1,0:T(8,128)(2,1)S(1)} copy-done((bf16[4,8,128,96]{2,3,1,0:T(8,128)(2,1)S(1)}, bf16[4,8,128,96]{2,3,1,0:T(8,128)(2,1)}, u32[]{:S(2)}) %copy-start.1) | copy-done | bytes 786456
  3.7 0.8 edges.1
  4.5 4.6 %collective-permute-start = (bf16[4,3,96,128]{3,2,1,0:T(8,128)(2,1)}, bf16[4,3,96,128]{3,2,1,0:T(8,128)(2,1)}, u32[]{:S(2)}, u32[]{:S(2)}) collective-permute-start(bf16[4,3,96,128]{3,2,1,0:T(8,128)(2,1)} %get-tuple-element.25), channel_id=1, source_target_pairs={{0,8},{8,16},{16,24},{24,32},{32,40},{40,48},{48,56},{56,64},{64,7... | collective-permute-start | bytes 884744 | tf_op jit(solution)/shard_map/ppermute | solution.py:681
  9.1 2.6 %collective-permute-start.1 = (bf16[4,3,96,128]{3,2,1,0:T(8,128)(2,1)}, bf16[4,3,96,128]{3,2,1,0:T(8,128)(2,1)}, u32[]{:S(2)}, u32[]{:S(2)}) collective-permute-start(bf16[4,3,96,128]{3,2,1,0:T(8,128)(2,1)} %get-tuple-element.26), channel_id=1, source_target_pairs={{8,0},{16,8},{24,16},{32,24},{40,32},{48,40},{56,48},{64,56},{72,6... | collective-permute-start | bytes 884744 | tf_op jit(solution)/shard_map/ppermute | solution.py:681
  11.7 7.6 %all-to-all-start = ((f32[8,2,192]{2,1,0:T(2,128)}), f32[8,2,192]{2,1,0:T(2,128)S(1)}, u32[]{:S(2)}, u32[]{:S(2)}) async-start(f32[8,2,192]{2,1,0:T(2,128)} %moments.1), calls=%async_computation | async-start | bytes 32768 | tf_op jit(solution)/shard_map/all_to_all | solution.py:695
  19.3 1.3 %copy-done.3 = bf16[3,3,3,192,96]{4,3,2,1,0:T(8,128)(2,1)S(1)} copy-done((bf16[3,3,3,192,96]{4,3,2,1,0:T(8,128)(2,1)S(1)}, bf16[3,3,3,192,96]{4,3,2,1,0:T(8,128)(2,1)}, u32[]{:S(2)}) %copy-start.3) | copy-done | bytes 995352
  20.6 0.5 combine_weights.1.weights.w_hbm
  21.1 4.9 %all-to-all-done.parts_ref = f32[8,2,192]{2,1,0:T(2,128)S(1)} async-done(((f32[8,2,192]{2,1,0:T(2,128)}), f32[8,2,192]{2,1,0:T(2,128)S(1)}, u32[]{:S(2)}, u32[]{:S(2)}) %all-to-all-start) | async-done | bytes 12320 | tf_op jit(solution)/shard_map/all_to_all | solution.py:695
  26.0 0.4 pack.1
  26.4 0.9 copy-done.4
  27.3 9.0 %all-to-all-start.1 = ((bf16[32,112,128]{2,1,0:T(8,128)(2,1)}), bf16[32,112,128]{2,1,0:T(8,128)(2,1)}, u32[]{:S(2)}, u32[]{:S(2)}) async-start(bf16[32,112,128]{2,1,0:T(8,128)(2,1)} %copy-done.4), calls=%async_computation.1 | async-start | bytes 1835008 | tf_op jit(solution)/shard_map/all_to_all | solution.py:695
  36.3 0.1 add_convert_fusion.flags
  36.4 7.5 %down_early.1 = (bf16[2,6,64,192]{3,2,1,0:T(8,128)(2,1)S(1)}, bf16[6,6,64,128]{3,2,1,0:T(8,128)(2,1)}) custom-call(bf16[3,4,4,192,128]{4,3,2,1,0:T(8,128)(2,1)S(1)} %combine_weights.1.weights.w_hbm, f32[3]{0:T(128)S(1)} %add_convert_fusion.flags, bf16[4,8,96,128]{3,2,1,0:T(8,128)(2,1)S(1)} %bitcast.8, bf16[4,3,96,128]{3,2,1,0:T(8,128)(2,1)} %collective-permute-done.above, ...), custom_call_target="tpu_custom_call" | custom-call | flops 4026531840 | bytes 4194304 | tf_op jit(solution)/shard_map/down_early/pallas_call | solution.py:392
  43.9 0.7 copy-done.9
  44.7 1.3 %collective-permute-start.2 = (bf16[6,6,64,128]{3,2,1,0:T(8,128)(2,1)}, bf16[6,6,64,128]{3,2,1,0:T(8,128)(2,1)}, u32[]{:S(2)}, u32[]{:S(2)}) collective-permute-start(bf16[6,6,64,128]{3,2,1,0:T(8,128)(2,1)} %get-tuple-element.40), channel_id=1, source_target_pairs={{1,0},{2,1},{3,2},{4,3},{5,4},{6,5},{7,6},{9,8},{10,9},{11,10},{12... | collective-permute-start | bytes 1769480 | tf_op jit(solution)/shard_map/ppermute | solution.py:684
  46.0 5.9 %all-to-all-done.1.x_ref = bf16[32,112,128]{2,1,0:T(8,128)(2,1)} async-done(((bf16[32,112,128]{2,1,0:T(8,128)(2,1)}), bf16[32,112,128]{2,1,0:T(8,128)(2,1)}, u32[]{:S(2)}, u32[]{:S(2)}) %all-to-all-start.1) | async-done | bytes 917536 | tf_op jit(solution)/shard_map/all_to_all | solution.py:695
  51.8 2.9 %unpack.1 = (bf16[4,8,64,192]{3,2,1,0:T(8,128)(2,1)S(1)}, bf16[2,8,64,192]{3,2,1,0:T(8,128)(2,1)}, f32[2,192]{1,0:T(2,128)S(1)}) custom-call(bf16[32,112,128]{2,1,0:T(8,128)(2,1)} %all-to-all-done.1.x_ref), custom_call_target="tpu_custom_call" | custom-call | flops 1000000000 | bytes 4194304 | tf_op jit(solution)/shard_map/unpack/pallas_call | solution.py:284
  54.7 3.2 %collective-permute-start.3 = (bf16[2,8,64,192]{3,2,1,0:T(8,128)(2,1)}, bf16[2,8,64,192]{3,2,1,0:T(8,128)(2,1)}, u32[]{:S(2)}, u32[]{:S(2)}) collective-permute-start(bf16[2,8,64,192]{3,2,1,0:T(8,128)(2,1)} %get-tuple-element.41), channel_id=1, source_target_pairs={{0,1},{1,2},{2,3},{3,4},{4,5},{5,6},{6,7},{8,9},{9,10},{10,11},{11... | collective-permute-start | bytes 1179656 | tf_op jit(solution)/shard_map/ppermute | solution.py:684
  57.9 3.3 %down_late.1 = (f32[2,6,64,192]{3,2,1,0:T(8,128)S(1)}, bf16[3,3,3,192,192]{4,3,2,1,0:T(8,128)(2,1)S(1)}) custom-call(bf16[3,3,3,192,192]{4,3,2,1,0:T(8,128)(2,1)} %w_hbm.1, bf16[3,4,4,192,128]{4,3,2,1,0:T(8,128)(2,1)S(1)} %combine_weights.1.weights.w_hbm, f32[3]{0:T(128)S(1)} %add_convert_fusion.flags, bf16[4,8,96,128]{3,2,1,0:T(8,128)(2,1)S(1)} %bitcast.9, ...), custom_call_target="tpu_custom_call" | custom-call | flops 1207959552 | bytes 4194304 | tf_op jit(solution)/shard_map/down_late/pallas_call | solution.py:405
  61.3 0.2 collective-permute-done.2.next_ref
  61.5 7.8 %back.1 = bf16[32,64,128]{2,1,0:T(8,128)(2,1)} custom-call(f32[2,192]{1,0:T(2,128)S(1)} %get-tuple-element.29.stats.stats_ref, bf16[3,3,3,192,192]{4,3,2,1,0:T(8,128)(2,1)S(1)} %get-tuple-element.36.weights, bf16[4,8,64,192]{3,2,1,0:T(8,128)(2,1)S(1)} %get-tuple-element.37.tile_ref, bf16[2,6,64,192]{3,2,1,0:T(8,128)(2,1)S(1)} %copy-done.10, ...), custom_call_target="tpu_custom_call" | custom-call | flops 3623878656 | bytes 4194304 | tf_op jit(solution)/shard_map/back/pallas_call | solution.py:476
  69.3 8.2 %all-to-all-start.2 = ((bf16[32,64,128]{2,1,0:T(8,128)(2,1)}), bf16[32,64,128]{2,1,0:T(8,128)(2,1)S(1)}, u32[]{:S(2)}, u32[]{:S(2)}) async-start(bf16[32,64,128]{2,1,0:T(8,128)(2,1)} %back.1), calls=%async_computation.2 | async-start | bytes 1048576 | tf_op jit(solution)/shard_map/all_to_all | solution.py:695
  77.5 1.2 %copy-done.8 = bf16[4,8,64,192]{3,2,1,0:T(8,128)(2,1)S(1)} copy-done((bf16[4,8,64,192]{3,2,1,0:T(8,128)(2,1)S(1)}, bf16[4,8,64,192]{3,2,1,0:T(8,128)(2,1)}, u32[]{:S(2)}) %copy-start.8) | copy-done | bytes 786456
  78.7 8.8 %middle.1 = (bf16[4,6,64,192]{3,2,1,0:T(8,128)(2,1)S(1)}, bf16[3,6,64,128]{3,2,1,0:T(8,128)(2,1)S(1)}) custom-call(f32[3]{0:T(128)S(1)} %add_convert_fusion.flags, f32[2,192]{1,0:T(2,128)S(1)} %get-tuple-element.29.stats.stats_ref, bf16[3,3,3,192,192]{4,3,2,1,0:T(8,128)(2,1)} %w_hbm.1, bf16[4,8,64,192]{3,2,1,0:T(8,128)(2,1)S(1)} %copy-done.8, ...), custom_call_target="tpu_custom_call" | custom-call | flops 5435817984 | bytes 4194304 | tf_op jit(solution)/shard_map/middle/pallas_call | solution.py:607
  87.5 2.3 %collective-permute-start.4 = (bf16[3,6,64,128]{3,2,1,0:T(8,128)(2,1)S(1)}, bf16[3,6,64,128]{3,2,1,0:T(8,128)(2,1)S(1)}, u32[]{:S(2)}, u32[]{:S(2)}) collective-permute-start(bf16[3,6,64,128]{3,2,1,0:T(8,128)(2,1)S(1)} %get-tuple-element.42), channel_id=1, source_target_pairs={{0,1},{1,2},{2,3},{3,4},{4,5},{5,6},{6,7},{8,9},{9,10},{10,11},{11... | collective-permute-start | bytes 884744 | tf_op jit(solution)/shard_map/ppermute | solution.py:684
  89.8 0.8 local_sums.1
  90.6 3.3 %all-to-all-start.3 = ((f32[8,2,192]{2,1,0:T(2,128)}), f32[8,2,192]{2,1,0:T(2,128)S(1)}, u32[]{:S(2)}, u32[]{:S(2)}) async-start(f32[8,2,192]{2,1,0:T(2,128)} %local_sums.1), calls=%async_computation.3 | async-start | bytes 32768 | tf_op jit(solution)/shard_map/all_to_all | solution.py:695
  93.9 1.8 %collective-permute-done.4.before_ref = bf16[3,6,64,128]{3,2,1,0:T(8,128)(2,1)S(1)} collective-permute-done((bf16[3,6,64,128]{3,2,1,0:T(8,128)(2,1)S(1)}, bf16[3,6,64,128]{3,2,1,0:T(8,128)(2,1)S(1)}, u32[]{:S(2)}, u32[]{:S(2)}) %collective-permute-start.4) | collective-permute-done | bytes 294944 | tf_op jit(solution)/shard_map/ppermute | solution.py:684
  95.7 6.1 %decode.1 = bf16[4,8,96,128]{3,2,1,0:T(8,128)(2,1)} custom-call(bf16[3,4,4,192,128]{4,3,2,1,0:T(8,128)(2,1)} %copy-done, bf16[3,6,64,128]{3,2,1,0:T(8,128)(2,1)S(1)} %collective-permute-done.4.before_ref, bf16[4,6,64,192]{3,2,1,0:T(8,128)(2,1)S(1)} %get-tuple-element.43.mid_ref), custom_call_target="tpu_custom_call" | custom-call | flops 3221225472 | bytes 4194304 | tf_op jit(solution)/shard_map/decode/pallas_call | solution.py:662
  101.8 1.6 %token_gradient.1 = bf16[4,2,192,128]{3,2,1,0:T(8,128)(2,1)} custom-call(bf16[32,64,128]{2,1,0:T(8,128)(2,1)S(1)} %all-to-all-done.2.x_ref, bf16[4,2,192,128]{3,2,1,0:T(8,128)(2,1)S(1)} %bitcast.12, f32[2,192]{1,0:T(2,128)S(1)} %get-tuple-element.29.stats.stats_ref, f32[8,2,192]{2,1,0:T(2,128)S(1)} %all-to-all-done.3.parts_ref), custom_call_target="tpu_custom_call" | custom-call | flops 1000000000 | bytes 4194304 | tf_op jit(solution)/shard_map/token_gradient/pallas_call | solution.py:544
  (21 shorter events, 0.0 us)
Async XLA Ops:
  0.6 1.0 copy-start.5
  1.6 24.3 %copy-start.6 = (bf16[4,128,2,192]{1,3,2,0:T(8,128)(2,1)S(1)}, bf16[4,128,2,192]{1,3,2,0:T(8,128)(2,1)}, u32[]{:S(2)}) copy-start(bf16[4,128,2,192]{1,3,2,0:T(8,128)(2,1)} %param.4) | copy-start | bytes 1179652
  2.6 1.1 %copy-start.1 = (bf16[4,8,128,96]{2,3,1,0:T(8,128)(2,1)S(1)}, bf16[4,8,128,96]{2,3,1,0:T(8,128)(2,1)}, u32[]{:S(2)}) copy-start(bf16[4,8,128,96]{2,3,1,0:T(8,128)(2,1)} %param.7) | copy-start | bytes 2359300
  4.5 22.7 %collective-permute-start = (bf16[4,3,96,128]{3,2,1,0:T(8,128)(2,1)}, bf16[4,3,96,128]{3,2,1,0:T(8,128)(2,1)}, u32[]{:S(2)}, u32[]{:S(2)}) collective-permute-start(bf16[4,3,96,128]{3,2,1,0:T(8,128)(2,1)} %get-tuple-element.25), channel_id=1, source_target_pairs={{0,8},{8,16},{16,24},{24,32},{32,40},{40,48},{48,56},{56,64},{64,7... | collective-permute-start | bytes 884744 | tf_op jit(solution)/shard_map/ppermute | solution.py:681
  9.1 18.1 %collective-permute-start.1 = (bf16[4,3,96,128]{3,2,1,0:T(8,128)(2,1)}, bf16[4,3,96,128]{3,2,1,0:T(8,128)(2,1)}, u32[]{:S(2)}, u32[]{:S(2)}) collective-permute-start(bf16[4,3,96,128]{3,2,1,0:T(8,128)(2,1)} %get-tuple-element.26), channel_id=1, source_target_pairs={{8,0},{16,8},{24,16},{32,24},{40,32},{48,40},{56,48},{64,56},{72,6... | collective-permute-start | bytes 884744 | tf_op jit(solution)/shard_map/ppermute | solution.py:681
  11.7 14.3 %all-to-all-start = ((f32[8,2,192]{2,1,0:T(2,128)}), f32[8,2,192]{2,1,0:T(2,128)S(1)}, u32[]{:S(2)}, u32[]{:S(2)}) async-start(f32[8,2,192]{2,1,0:T(2,128)} %moments.1), calls=%async_computation | async-start | bytes 32768 | tf_op jit(solution)/shard_map/all_to_all | solution.py:695
  19.3 1.3 %copy-start.3 = (bf16[3,3,3,192,96]{4,3,2,1,0:T(8,128)(2,1)S(1)}, bf16[3,3,3,192,96]{4,3,2,1,0:T(8,128)(2,1)}, u32[]{:S(2)}) copy-start(bf16[3,3,3,192,96]{4,3,2,1,0:T(8,128)(2,1)} %w_ref.1) | copy-start | bytes 2985988
  21.1 36.8 %copy-start = (bf16[3,4,4,192,128]{4,3,2,1,0:T(8,128)(2,1)}, bf16[3,4,4,192,128]{4,3,2,1,0:T(8,128)(2,1)S(1)}, u32[]{:S(2)}) copy-start(bf16[3,4,4,192,128]{4,3,2,1,0:T(8,128)(2,1)S(1)} %combine_weights.1.weights.w_hbm) | copy-start | bytes 7077892
  21.1 15.3 %copy-start.2 = (bf16[4,8,128,96]{2,3,1,0:T(8,128)(2,1)S(1)}, bf16[4,8,128,96]{2,3,1,0:T(8,128)(2,1)}, u32[]{:S(2)}) copy-start(bf16[4,8,128,96]{2,3,1,0:T(8,128)(2,1)} %param.7) | copy-start | bytes 2359300
  26.3 0.9 copy-start.4
  27.3 24.6 %all-to-all-start.1 = ((bf16[32,112,128]{2,1,0:T(8,128)(2,1)}), bf16[32,112,128]{2,1,0:T(8,128)(2,1)}, u32[]{:S(2)}, u32[]{:S(2)}) async-start(bf16[32,112,128]{2,1,0:T(8,128)(2,1)} %copy-done.4), calls=%async_computation.1 | async-start | bytes 1835008 | tf_op jit(solution)/shard_map/all_to_all | solution.py:695
  43.9 0.7 copy-start.9
  44.7 16.8 %collective-permute-start.2 = (bf16[6,6,64,128]{3,2,1,0:T(8,128)(2,1)}, bf16[6,6,64,128]{3,2,1,0:T(8,128)(2,1)}, u32[]{:S(2)}, u32[]{:S(2)}) collective-permute-start(bf16[6,6,64,128]{3,2,1,0:T(8,128)(2,1)} %get-tuple-element.40), channel_id=1, source_target_pairs={{1,0},{2,1},{3,2},{4,3},{5,4},{6,5},{7,6},{9,8},{10,9},{11,10},{12... | collective-permute-start | bytes 1769480 | tf_op jit(solution)/shard_map/ppermute | solution.py:684
  54.7 6.8 %copy-start.7 = (bf16[4,8,64,192]{3,2,1,0:T(8,128)(2,1)}, bf16[4,8,64,192]{3,2,1,0:T(8,128)(2,1)S(1)}, u32[]{:S(2)}) copy-start(bf16[4,8,64,192]{3,2,1,0:T(8,128)(2,1)S(1)} %get-tuple-element.37.tile_ref) | copy-start | bytes 2359300
  54.7 6.8 %copy-start.10 = (bf16[2,6,64,192]{3,2,1,0:T(8,128)(2,1)S(1)}, bf16[2,6,64,192]{3,2,1,0:T(8,128)(2,1)}, u32[]{:S(2)}) copy-start(bf16[2,6,64,192]{3,2,1,0:T(8,128)(2,1)} %copy-done.9) | copy-start | bytes 884740
  54.7 22.8 %collective-permute-start.3 = (bf16[2,8,64,192]{3,2,1,0:T(8,128)(2,1)}, bf16[2,8,64,192]{3,2,1,0:T(8,128)(2,1)}, u32[]{:S(2)}, u32[]{:S(2)}) collective-permute-start(bf16[2,8,64,192]{3,2,1,0:T(8,128)(2,1)} %get-tuple-element.41), channel_id=1, source_target_pairs={{0,1},{1,2},{2,3},{3,4},{4,5},{5,6},{6,7},{8,9},{9,10},{10,11},{11... | collective-permute-start | bytes 1179656 | tf_op jit(solution)/shard_map/ppermute | solution.py:684
  69.3 20.5 %all-to-all-start.2 = ((bf16[32,64,128]{2,1,0:T(8,128)(2,1)}), bf16[32,64,128]{2,1,0:T(8,128)(2,1)S(1)}, u32[]{:S(2)}, u32[]{:S(2)}) async-start(bf16[32,64,128]{2,1,0:T(8,128)(2,1)} %back.1), calls=%async_computation.2 | async-start | bytes 1048576 | tf_op jit(solution)/shard_map/all_to_all | solution.py:695
  77.5 1.2 %copy-start.8 = (bf16[4,8,64,192]{3,2,1,0:T(8,128)(2,1)S(1)}, bf16[4,8,64,192]{3,2,1,0:T(8,128)(2,1)}, u32[]{:S(2)}) copy-start(bf16[4,8,64,192]{3,2,1,0:T(8,128)(2,1)} %copy-done.7) | copy-start | bytes 2359300
  87.5 8.2 %collective-permute-start.4 = (bf16[3,6,64,128]{3,2,1,0:T(8,128)(2,1)S(1)}, bf16[3,6,64,128]{3,2,1,0:T(8,128)(2,1)S(1)}, u32[]{:S(2)}, u32[]{:S(2)}) collective-permute-start(bf16[3,6,64,128]{3,2,1,0:T(8,128)(2,1)S(1)} %get-tuple-element.42), channel_id=1, source_target_pairs={{0,1},{1,2},{2,3},{3,4},{4,5},{5,6},{6,7},{8,9},{9,10},{10,11},{11... | collective-permute-start | bytes 884744 | tf_op jit(solution)/shard_map/ppermute | solution.py:684
  90.6 11.3 %all-to-all-start.3 = ((f32[8,2,192]{2,1,0:T(2,128)}), f32[8,2,192]{2,1,0:T(2,128)S(1)}, u32[]{:S(2)}, u32[]{:S(2)}) async-start(f32[8,2,192]{2,1,0:T(2,128)} %local_sums.1), calls=%async_computation.3 | async-start | bytes 32768 | tf_op jit(solution)/shard_map/all_to_all | solution.py:695

commit v3 on v2

--- a/solution.py
+++ b/solution.py
@@ -134,18 +134,6 @@
     return ref[frame], ref[frames + frame // 2, :, :, lane : lane + 64]
 
 
-def fill(buffer, pieces, transform):
-    rows = buffer.shape[1]
-    for ref, source, count, t0, later in pieces:
-
-        def one_frame(i, carry):
-            for r in range(rows):
-                buffer[t0 + i, r] = transform(ref[source + i, r], r, later)
-            return carry
-
-        lax.fori_loop(0, count, one_frame, 0)
-
-
 def from_left(value, cols):
     column = lax.broadcasted_iota(jnp.int32, value.shape, 0) & (cols - 1)
     return jnp.where(column == 0, 0.0, pltpu.roll(value, 1, 0))
@@ -183,19 +171,38 @@
     return call(combine_kernel, "combine_weights", shape, vmem(1), [], 10**6)(conv_two)
 
 
-def edges_kernel(x_ref, first_ref, last_ref):
-    lines = x_ref.shape[1]
-    first_ref[...] = x_ref[:, 0:3]
-    last_ref[...] = x_ref[:, lines - 3 : lines]
+def edges_kernel(x_hbm, first_hbm, last_hbm, near_ref, sems):
+    lines = x_hbm.shape[1]
+    ends = ((0, first_hbm), (lines - 3, last_hbm))
+    for k, (at, _) in enumerate(ends):
+        pltpu.make_async_copy(x_hbm.at[:, pl.ds(at, 3)], near_ref.at[k], sems.at[0, k]).start()
+    copies = []
+    for k, (at, ref) in enumerate(ends):
+        pltpu.make_async_copy(x_hbm.at[:, pl.ds(at, 3)], near_ref.at[k], sems.at[0, k]).wait()
+        copies.append(pltpu.make_async_copy(near_ref.at[k], ref, sems.at[1, k]))
+        copies[k].start()
+    for copy in copies:
+        copy.wait()
 
 
 def edges(pixels):
     frames, _, outs, wide = pixels.shape
-    shape = array((frames, 3, outs, wide))
-    return call(edges_kernel, "edges", (shape, shape), vmem(1), [], 10**6)(pixels)
-
-
-def moments_kernel(x_ref, out_ref):
+    shape = pltpu.HBM((frames, 3, outs, wide), BF16)
+    return pl.pallas_call(
+        edges_kernel,
+        name="edges",
+        out_shape=(shape, shape),
+        in_specs=[anywhere()],
+        out_specs=(anywhere(), anywhere()),
+        scratch_shapes=[
+            pltpu.VMEM((2, *shape.shape), BF16),
+            pltpu.SemaphoreType.DMA((2, 2)),
+        ],
+        cost_estimate=pl.CostEstimate(flops=10**6, bytes_accessed=10**6, transcendentals=0),
+    )(far(pixels))
+
+
+def own_moments(x_ref):
     frames, stripe, chans, height = x_ref.shape
     total = jnp.zeros((chans, height), F32)
     for t in range(frames):
@@ -207,13 +214,7 @@
         for c in range(stripe):
             spread = spread + (x_ref[t, c].astype(F32) - mean) ** 2
     spread = jnp.sum(spread, axis=1, keepdims=True)
-    rows = [jnp.broadcast_to(v, (chans, 128)).T[0:1] for v in (mean, spread)]
-    out_ref[...] = jnp.broadcast_to(jnp.concatenate(rows, axis=0)[None], out_ref.shape)
-
-
-def moments(tokens, clips):
-    shape = array((clips, 2, tokens.shape[2]), F32)
-    return call(moments_kernel, "moments", shape, vmem(1), [], 10**6)(tokens)
+    return [jnp.broadcast_to(v, (chans, 128)).T[0:1] for v in (mean, spread)]
 
 
 def merged(means, spreads, held):
@@ -222,7 +223,7 @@
     return mean, spread + held * jnp.sum((means - mean) ** 2, axis=0, keepdims=True)
 
 
-def pack_kernel(held, x_ref, parts_ref, out_ref):
+def pack_kernel(x_ref, out_ref):
     frames, stripe, chans, height = x_ref.shape
     seqs = out_ref.shape[0]
     rows = height // seqs
@@ -240,18 +241,16 @@
             at = 48 * n + 16 * k
             rows_of = [picked(column) for column in columns]
             out_ref[:, at : at + 16] = jnp.concatenate(rows_of, axis=1).astype(BF16)
-    extra = extra_rows(*merged(parts_ref[:, 0], parts_ref[:, 1], held)).astype(BF16)
+    extra = extra_rows(*own_moments(x_ref)).astype(BF16)
     out_ref[:, 24 * frames :] = jnp.broadcast_to(extra[None], (seqs, EXTRA, 128))
 
 
-def pack(tokens, parts, seqs, held):
-    shape = array((seqs, 24 * tokens.shape[0] + EXTRA, 128))
-    return call(functools.partial(pack_kernel, held), "pack", shape, vmem(2), [], 10**9)(
-        tokens, parts
-    )
-
-
-def unpack_kernel(held, x_ref, tile_ref, last_ref, stats_ref):
+def pack(tokens, seqs):
+    shape = pltpu.HBM((seqs, 24 * tokens.shape[0] + EXTRA, 128), BF16)
+    return call(pack_kernel, "pack", shape, vmem(1), [], 10**9)(tokens)
+
+
+def unpack_kernel(held, x_ref, tile_ref, last_ref, parts_ref):
     seqs = x_ref.shape[0]
     frames, rows, cols, chans = tile_ref.shape
     size = rows * cols
@@ -270,24 +269,18 @@
                     ref[at, :, :, 0:128] = part.reshape(rows, cols, 128)
                     part = rest[:, 64 * k : 64 * (k + 1)]
                     ref[at, :, :, 128:chans] = part.reshape(rows, cols, 64)
-    size = chans // GROUPS
-    means, spreads = from_extra(x_ref[:, 24 * frames :])
-    mean = group_sum(jnp.broadcast_to(jnp.sum(means, axis=0, keepdims=True), (8, chans)))
-    mean = mean[0:1] / (seqs * size)
-    spread = jnp.sum(spreads, axis=0, keepdims=True)
-    spread = spread + held * jnp.sum((means - mean) ** 2, axis=0, keepdims=True)
-    var = group_sum(jnp.broadcast_to(spread, (8, chans)))[0:1] / (held * seqs * size)
-    stats_ref[...] = jnp.concatenate([mean, lax.rsqrt(var + 1e-06)], axis=0)
-
-
-def unpack(blocks, frames, cols, chans, held):
+    parts = merged(*from_extra(x_ref[:, 24 * frames :]), held)
+    parts_ref[...] = jnp.broadcast_to(jnp.concatenate(parts, axis=0)[None], parts_ref.shape)
+
+
+def unpack(blocks, frames, cols, chans, clips, held):
     return call(
         functools.partial(unpack_kernel, held),
         "unpack",
         (
-            kept((frames, 8, cols, chans)),
-            kept((2, 8, cols, chans)),
-            kept((2, chans), F32),
+            pltpu.HBM((frames, 8, cols, chans), BF16),
+            pltpu.HBM((2, 8, cols, chans), BF16),
+            pltpu.HBM((clips, 2, chans), F32),
         ),
         vmem(1),
         [],
@@ -295,29 +288,63 @@
     )(blocks)
 
 
-def down_kernel(first, plan, weights, flags, pixels, above, below, store, buffer):
+def stats_kernel(held, parts_ref, stats_ref):
+    clips, _, chans = parts_ref.shape
+    means, spreads = parts_ref[:, 0], parts_ref[:, 1]
+    size = chans // GROUPS
+    mean = group_sum(jnp.broadcast_to(jnp.sum(means, axis=0, keepdims=True), (8, chans)))
+    mean = mean[0:1] / (clips * size)
+    spread = jnp.sum(spreads, axis=0, keepdims=True)
+    spread = spread + held * jnp.sum((means - mean) ** 2, axis=0, keepdims=True)
+    var = group_sum(jnp.broadcast_to(spread, (8, chans)))[0:1] / (held * clips * size)
+    stats_ref[...] = jnp.concatenate([mean, lax.rsqrt(var + 1e-06)], axis=0)
+
+
+def group_stats(parts, held):
+    shape = kept(parts.shape[1:], F32)
+    kernel = functools.partial(stats_kernel, held)
+    return call(kernel, "group_stats", shape, vmem(1), [], 10**6)(parts)
+
+
+def down_kernel(first, plan, weights, flags, sources, store, buffer, beside, sems):
     _, _, cols, _ = buffer.shape[1:]
     rows, outs = buffer.shape[2] - 1, weights.shape[3]
-    chans, wide = pixels.shape[2:]
+    pixels, *sides = sources
+    count = buffer.shape[0]
+    lines, chans, wide = pixels.shape[1:]
+    copies = [
+        pltpu.make_async_copy(side.at[pl.ds(first, count)], beside.at[k], sems.at[k])
+        for k, side in enumerate(sides)
+    ]
+    for copy in copies:
+        copy.start()
     select = one_hot(2 * cols, wide, lambda i: 2 * (i & (cols - 1)) + (i // cols))
     blank = jnp.zeros((128 - chans, wide), BF16)
 
-    def one_frame(i, carry):
-        at = first + i
-        lines = [above.at[at, r] for r in range(3)]
-        lines += [pixels.at[at, r] for r in range(pixels.shape[1])]
-        lines += [below.at[at, r] for r in range(3)]
-        for n in range(0, len(lines), 2):
-            pair = [lines[n][...], blank, lines[n + 1][...], blank]
-            picked = nt_dot(select, jnp.concatenate(pair, axis=0)).astype(BF16)
-            for k in range(2):
-                for j in range(2):
-                    buffer[i, k, n // 2, :, 128 * j : 128 * (j + 1)] = picked[
-                        cols * j : cols * (j + 1), 128 * k : 128 * (k + 1)
-                    ]
-        return carry
-
-    lax.fori_loop(0, buffer.shape[0], one_frame, 0)
+    def line(i, n):
+        if 3 <= n < 3 + lines:
+            return pixels[first + i, n - 3]
+        return beside[0, i, n] if n < 3 else beside[1, i, n - 3 - lines]
+
+    def place(inner):
+        def one_frame(i, carry):
+            for n in range(0, lines + 6, 2):
+                if (3 < n < 2 + lines) == inner:
+                    pair = [line(i, n), blank, line(i, n + 1), blank]
+                    picked = nt_dot(select, jnp.concatenate(pair, axis=0)).astype(BF16)
+                    for k in range(2):
+                        for j in range(2):
+                            buffer[i, k, n // 2, :, 128 * j : 128 * (j + 1)] = picked[
+                                cols * j : cols * (j + 1), 128 * k : 128 * (k + 1)
+                            ]
+            return carry
+
+        lax.fori_loop(0, count, one_frame, 0)
+
+    place(True)
+    for copy in copies:
+        copy.wait()
+    place(False)
 
     size = rows * cols
 
@@ -360,26 +387,27 @@
             )
 
 
-def early_kernel(plan, weights, flags, pixels, above, below, own_ref, sent_ref, buffer):
+def early_kernel(plan, weights, flags, pixels, above, below, sent_ref, *scratch):
     def store(n, parts):
-        value = jnp.concatenate([part.astype(BF16) for part in parts], axis=0)
-        store_dense(sent_ref, n, value)
-        if n < 2:
-            own_ref[n] = value
-
-    down_kernel(0, plan, weights, flags, pixels, above, below, store, buffer)
-
-
-def late_kernel(first, plan, one_hbm, weights, flags, pixels, above, below, *refs):
-    out_ref, one_ref, buffer, sem = refs
-    copy = pltpu.make_async_copy(one_hbm, one_ref, sem)
-    copy.start()
-
+        store_dense(sent_ref, n, jnp.concatenate([part.astype(BF16) for part in parts], axis=0))
+
+    down_kernel(0, plan, weights, flags, (pixels, above, below), store, *scratch)
+
+
+def late_kernel(first, plan, weights, flags, pixels, above, below, out_ref, *scratch):
     def store(n, parts):
         out_ref[n] = jnp.concatenate(parts, axis=0)
 
-    down_kernel(first, plan, weights, flags, pixels, above, below, store, buffer)
-    copy.wait()
+    down_kernel(first, plan, weights, flags, (pixels, above, below), store, *scratch)
+
+
+def down_scratch(count, pixels, rows, cols):
+    _, _, chans, wide = pixels.shape
+    return [
+        pltpu.VMEM((count, 2, rows + 1, cols, 256), BF16),
+        pltpu.VMEM((2, count, 3, chans, wide), BF16),
+        pltpu.SemaphoreType.DMA((2,)),
+    ]
 
 
 def down_cost(plan, size):
@@ -387,47 +415,68 @@
 
 
 def down_early(weights, flags, pixels, above, below, rows, cols):
-    frames, outs = pixels.shape[0], weights.shape[3]
+    frames = pixels.shape[0]
     plan = ((((0, 2), (1, 1), (2, 0)), (), 0), (((0, 0),), (0, 1), 1))
     return call(
         functools.partial(early_kernel, plan),
         "down_early",
-        (kept((2, rows, cols, outs)), array((6, rows, cols, 128))),
-        vmem(1) + [smem()] + vmem(3),
-        [pltpu.VMEM((frames, 2, rows + 1, cols, 256), BF16)],
+        pltpu.HBM((6, rows, cols, 128), BF16),
+        vmem(1) + [smem()] + vmem(1) + [anywhere()] * 2,
+        down_scratch(frames, pixels, rows, cols),
         down_cost(plan, rows * cols),
-    )(weights, flags, pixels, above, below)
-
-
-def down_late(conv_one, weights, flags, pixels, above, below, rows, cols):
+    )(weights, flags, near(pixels), far(above), far(below))
+
+
+def down_late(weights, flags, pixels, above, below, rows, cols):
     frames, outs = pixels.shape[0], weights.shape[3]
     plan = ((((2, 2),), (3, 1), 0),)
     return call(
         functools.partial(late_kernel, frames - 2, plan),
         "down_late",
-        (kept((2, rows, cols, outs), F32), kept(conv_one.shape)),
-        [anywhere()] + vmem(1) + [smem()] + vmem(3),
-        [pltpu.VMEM((2, 2, rows + 1, cols, 256), BF16), pltpu.SemaphoreType.DMA],
+        pltpu.HBM((2, rows, cols, outs), F32),
+        vmem(1) + [smem()] + vmem(1) + [anywhere()] * 2,
+        down_scratch(2, pixels, rows, cols),
         down_cost(plan, rows * cols),
-    )(far(conv_one), weights, flags, pixels, above, below)
-
-
-def back_kernel(stats, weights, tile_ref, early_ref, late_ref, next_ref, out_ref, buffer, rest):
+    )(weights, flags, near(pixels), far(above), far(below))
+
+
+def back_kernel(
+    stats, w_hbm, tile_hbm, own_hbm, late_hbm, next_hbm, out_ref, *scratch
+):
+    main, rows_pair, frames_pair, rest, weights, tile_ref, own_ref, late_ref, next_ref, sems = scratch
+    frames, rows, cols, chans = tile_ref.shape
+    pairs = (
+        (own_hbm.at[pl.ds(0, 2)], own_ref.at[pl.ds(0, 2)]),
+        (own_hbm.at[pl.ds(4, 1)], own_ref.at[pl.ds(2, 1)]),
+        (next_hbm, next_ref),
+        (late_hbm, late_ref),
+        (w_hbm, weights),
+        (tile_hbm.at[:, pl.ds(2, rows)], tile_ref),
+    )
+    copies = [pltpu.make_async_copy(*pair, sems.at[k]) for k, pair in enumerate(pairs)]
+    for copy in copies:
+        copy.start()
     seqs = out_ref.shape[0]
-    frames, _, cols, chans = tile_ref.shape
-    rows = buffer.shape[1] - 2
     size = 2 * rows * cols
+    buffer = Packed(main, rows_pair, frames_pair)
+    buffer.clear()
+    for copy in copies[:3]:
+        copy.wait()
     for k in range(2):
-        buffer[k] = early_ref[k]
-        main, tail = load_dense(next_ref, k)
-        buffer[frames + k, :, :, 0:128] = main
-        buffer[frames + k, :, :, 128:chans] = tail
-        main, tail = load_dense(next_ref, 2 + k)
+        for at, ref in ((k, own_ref), (frames + k, next_ref)):
+            block, tail = load_dense(ref, k)
+            for r in range(rows + 2):
+                buffer.put(at, r, block[r], tail[r])
+    copies[3].wait()
+    for k in range(2):
+        block, tail = load_dense(next_ref, 2 + k)
         late = late_ref[k]
-        main = (late[..., :128] + main.astype(F32)).astype(BF16)
+        block = (late[..., :128] + block.astype(F32)).astype(BF16)
         tail = (late[..., 128:] + tail.astype(F32)).astype(BF16)
-        buffer[frames - 2 + k, :, :, 0:128] = main
-        buffer[frames - 2 + k, :, :, 128:chans] = tail
+        for r in range(rows + 2):
+            buffer.put(frames - 2 + k, r, block[r], tail[r])
+    for copy in copies[4:]:
+        copy.wait()
     mean = stats[0:1]
     scale = stats[1:2]
     order = one_hot(
@@ -440,23 +489,30 @@
         first_sum, second_sum = carry
         t = 2 * n
         total = [jnp.zeros((size, chans), F32) for _ in range(3)]
-        for dt in range(3):
-            for dr in range(3):
-                lhs = buffer[pl.ds(t + dt, 2), dr : dr + rows].reshape(size, chans)
-                for dc in range(3):
-                    total[dc] = total[dc] + nt_dot(lhs, weights[2 - dt, 2 - dr, 2 - dc])
+        for lhs, holds in buffer.operands(t, 2, rows):
+            for dc in range(3):
+                taps = [
+                    weights[2 - tap[0], 2 - tap[1], 2 - dc, :, PARTS[tap[2]]]
+                    if tap
+                    else jnp.zeros((chans, 64), BF16)
+                    for tap in holds
+                ]
+                total[dc] = total[dc] + nt_dot(lhs, jnp.concatenate(taps, axis=1))
         total = total[1] + from_left(total[0], cols) + from_right(total[2], cols)
-        tile = tile_ref[pl.ds(t, 2), 2 : 2 + rows].reshape(size, chans)
+        tile = tile_ref[pl.ds(t, 2)].reshape(size, chans)
         normed = (tile.astype(F32) - mean) * scale
         sigmoid = 1.0 / (1.0 + jnp.exp(-normed))
         grad = total * sigmoid * (1.0 + normed * (1.0 - sigmoid))
         first_sum = first_sum + jnp.sum(grad, axis=0, keepdims=True)
         second_sum = second_sum + jnp.sum(grad * normed, axis=0, keepdims=True)
-        own = buffer[pl.ds(t, 2), 1 : 1 + rows].reshape(size, chans)
-        base = (own.astype(F32) + grad * scale).astype(BF16)
+        own = [
+            ref[pl.ds(t, 2), 1 : 1 + rows].reshape(size, 128) for ref in (main, rows_pair)
+        ]
+        own = jnp.concatenate(own, axis=1)[:, :chans].astype(F32)
+        base = (own + grad * scale).astype(BF16)
         home = dot(order, base)
-        main = home[:, :128].reshape(seqs, 16, 128).astype(BF16)
-        out_ref[:, pl.ds(pl.multiple_of(16 * n, 16), 16)] = main
+        block = home[:, :128].reshape(seqs, 16, 128).astype(BF16)
+        out_ref[:, pl.ds(pl.multiple_of(16 * n, 16), 16)] = block
         tail = home[:, 128:].reshape(seqs, 2, 8, chans - 128)
         for k in range(2):
             rest[n, :, :, 64 * k : 64 * (k + 1)] = tail[:, k]
@@ -470,20 +526,26 @@
     out_ref[:, 12 * frames :] = jnp.broadcast_to(extra[None], (seqs, EXTRA, 128))
 
 
-def back(stats, weights, tile, early, late, following, seqs):
-    frames = tile.shape[0]
-    _, ext, cols, chans = early.shape
+def back(stats, weights, tile, own, late, following, seqs):
+    frames, ext, cols, chans = tile.shape
+    rows = ext - 4
     return call(
         back_kernel,
         "back",
-        array((seqs, 12 * frames + EXTRA, 128)),
-        vmem(6),
+        pltpu.HBM((seqs, 12 * frames + EXTRA, 128), BF16),
+        vmem(1) + [anywhere()] * 5,
         [
-            pltpu.VMEM((frames + 2, ext, cols, chans), BF16),
+            *packed_scratch(frames + 2, rows + 2, cols),
             pltpu.VMEM((frames // 2, seqs, 8, 128), F32),
+            pltpu.VMEM(weights.shape, BF16),
+            pltpu.VMEM((frames, rows, cols, chans), BF16),
+            pltpu.VMEM((3, *own.shape[1:]), BF16),
+            pltpu.VMEM(late.shape, F32),
+            pltpu.VMEM(following.shape, BF16),
+            pltpu.SemaphoreType.DMA((6,)),
         ],
-        2 * frames * (ext - 2) * cols * 27 * 65536,
-    )(stats, weights, tile, early, late, following)
+        2 * frames * rows * cols * 21 * 65536,
+    )(stats, far(weights), far(tile), far(own), far(late), far(following))
 
 
 def sums_kernel(x_ref, out_ref):
@@ -551,6 +613,46 @@
     )(blocks, tokens, stats, parts)
 
 
+class Packed:
+    def __init__(self, main, rows_pair, frames_pair):
+        self.main, self.rows_pair, self.frames_pair = main, rows_pair, frames_pair
+
+    def clear(self):
+        self.rows_pair[...] = jnp.zeros_like(self.rows_pair)
+        self.frames_pair[...] = jnp.zeros_like(self.frames_pair)
+
+    def put(self, t, r, main, rest):
+        self.main[t, r] = main
+        self.rows_pair[t, r, :, 0:64] = rest
+        self.frames_pair[t, r, :, 0:64] = rest
+        if r > 0:
+            self.rows_pair[t, r - 1, :, 64:128] = rest
+        if not (isinstance(t, int) and t == 0):
+            self.frames_pair[t - 1, r, :, 64:128] = rest
+
+    def operands(self, t, count, rows):
+        def get(ref, dt, dr):
+            block = ref[pl.ds(t + dt, count), dr : dr + rows]
+            return block.reshape(count * rows * block.shape[2], 128)
+
+        tiles = [(get(self.main, dt, dr), [(dt, dr, 0)]) for dt in range(3) for dr in range(3)]
+        for dt in range(3):
+            tiles.append((get(self.rows_pair, dt, 0), [(dt, 0, 1), (dt, 1, 1)]))
+        tiles.append((get(self.frames_pair, 0, 2), [(0, 2, 1), (1, 2, 1)]))
+        tiles.append((get(self.rows_pair, 2, 2), [(2, 2, 1), None]))
+        return [
+            (jnp.concatenate([one, two], axis=1), has + more)
+            for (one, has), (two, more) in zip(tiles[::2], tiles[1::2])
+        ]
+
+
+def packed_scratch(frames, rows, cols):
+    return [pltpu.VMEM((frames, rows, cols, 128), BF16) for _ in range(3)]
+
+
+PARTS = (slice(0, 128), slice(128, 192))
+
+
 def fetch(source, target, sems):
     copies = [pltpu.make_async_copy(source.at[k], target.at[k], sems.at[k]) for k in range(3)]
     for copy in copies:
@@ -558,7 +660,12 @@
     return copies
 
 
-def mid_kernel(flags, stats, w_hbm, tile_ref, before_ref, out_ref, sent_ref, buffer, weights, sems):
+def mid_kernel(
+    flags, stats, w_hbm, tile_hbm, before_ref, out_ref, sent_ref, *scratch
+):
+    main, rows_pair, frames_pair, weights, sems, tile_ref, sem = scratch
+    tile_copy = pltpu.make_async_copy(tile_hbm, tile_ref, sem)
+    tile_copy.start()
     copies = fetch(w_hbm, weights, sems)
     frames, rows, cols, chans = out_ref.shape
     size = 2 * rows * cols
@@ -576,18 +683,36 @@
             act = act * flags[2]
         return act.astype(BF16)
 
-    fill(buffer, [(before_ref, 0, 2, 0, True), (tile_ref, 0, frames, 2, False)], activate)
+    buffer = Packed(main, rows_pair, frames_pair)
+    buffer.clear()
+    for t in range(2):
+        for r in range(rows + 2):
+            act = activate(before_ref[t, r], r, True)
+            buffer.put(t, r, act[:, :128], act[:, 128:])
+    tile_copy.wait()
+
+    def one_frame(t, carry):
+        for r in range(rows + 2):
+            act = activate(tile_ref[t, r], r, False)
+            buffer.put(t + 2, r, act[:, :128], act[:, 128:])
+        return carry
+
+    lax.fori_loop(0, frames, one_frame, 0)
     for copy in copies:
         copy.wait()
 
     def two_frames(n, carry):
         t = 2 * n
         total = [jnp.zeros((size, chans), F32) for _ in range(3)]
-        for dt in range(3):
-            for dr in range(3):
-                lhs = buffer[pl.ds(t + dt, 2), dr : dr + rows].reshape(size, chans)
-                for dc in range(3):
-                    total[dc] = total[dc] + dot(lhs, weights[dt, dr, dc])
+        for lhs, holds in buffer.operands(t, 2, rows):
+            for dc in range(3):
+                taps = [
+                    weights[tap[0], tap[1], dc, PARTS[tap[2]]]
+                    if tap
+                    else jnp.zeros((64, chans), BF16)
+                    for tap in holds
+                ]
+                total[dc] = total[dc] + dot(lhs, jnp.concatenate(taps, axis=0))
         total = total[1] + from_left(total[0], cols) + from_right(total[2], cols)
         total = total.reshape(2, rows, cols, chans)
         total = total + tile_ref[pl.ds(t, 2), 1 : 1 + rows].astype(F32)
@@ -608,40 +733,72 @@
         mid_kernel,
         "middle",
         (kept((frames, rows, cols, chans)), array((3, rows, cols, 128))),
-        [smem()] + vmem(1) + [anywhere()] + vmem(2),
+        [smem()] + vmem(1) + [anywhere()] * 2 + vmem(1),
         [
-            pltpu.VMEM((frames + 2, ext, cols, chans), BF16),
+            *packed_scratch(frames + 2, ext, cols),
             pltpu.VMEM(weights.shape, BF16),
             pltpu.SemaphoreType.DMA((3,)),
+            pltpu.VMEM(tile.shape, BF16),
+            pltpu.SemaphoreType.DMA,
         ],
         2 * frames * rows * cols * 27 * 65536,
     )(flags, stats, far(weights), tile, before)
 
 
-def decode_kernel(w_hbm, before_ref, mid_ref, out_ref, buffer, wide, weights, sems):
+def decode_kernel(
+    w_hbm, before_ref, mid_ref, out_ref, main_ref, pair_ref, wide, weights, sems
+):
     copies = fetch(w_hbm, weights, sems)
-    frames, _, cols, chans = mid_ref.shape
+    frames, ext, cols, chans = mid_ref.shape
     lines, outs, _ = out_ref.shape[1:]
     rows = lines // 2
+    pair_ref[:, ext - 1] = jnp.zeros_like(pair_ref[:, ext - 1])
+
+    def put(at, main, rest):
+        main_ref[at] = main
+        pair_ref[at, :, :, 0:64] = rest
+        pair_ref[at, 0 : ext - 1, :, 64:128] = rest[1:]
+
     for k in range(2):
-        main, tail = load_dense(before_ref, k)
-        buffer[k, :, :, 0:128] = main
-        buffer[k, :, :, 128:chans] = tail
-    buffer[2:] = mid_ref[...]
+        put(k, *load_dense(before_ref, k))
+
+    def one_frame(t, carry):
+        value = mid_ref[t]
+        put(t + 2, value[..., :128], value[..., 128:])
+        return carry
+
+    lax.fori_loop(0, frames, one_frame, 0)
     eye = one_hot(outs, 128, lambda i: i)
     size = 2 * rows * cols
 
     for t in range(0, frames, 2):
         for i, taps in enumerate((((0, 3), (1, 1)), ((1, 2), (2, 0)))):
             here, aside = (jnp.zeros((size, 256), F32) for _ in range(2))
+            tiles = []
             for dt in range(3):
                 if t + i == 0:
                     copies[dt].wait()
-                for dr, p in taps:
-                    w = weights.at[dt, p]
-                    lhs = buffer[t + dt : t + dt + 2, dr : dr + rows].reshape(size, chans)
-                    here = here + dot(lhs, jnp.concatenate([w[1], w[2]], axis=-1))
-                    aside = aside + dot(lhs, jnp.concatenate([w[3], w[0]], axis=-1))
+                at = slice(t + dt, t + dt + 2)
+                (dr, p), (below, q) = taps
+                for ref, row, parts in (
+                    (main_ref, dr, [(p, slice(0, 128))]),
+                    (main_ref, below, [(q, slice(0, 128))]),
+                    (pair_ref, dr, [(p, slice(128, 192)), (q, slice(128, 192))]),
+                ):
+                    lhs = ref[at, row : row + rows].reshape(size, 128)
+                    tiles.append((lhs, [(weights.at[dt, tap], part) for tap, part in parts]))
+            for n in range(0, len(tiles), 2):
+                lhs = jnp.concatenate([lhs for lhs, _ in tiles[n : n + 2]], axis=1)
+                taken = [tap for _, some in tiles[n : n + 2] for tap in some]
+                for into, (one, two) in enumerate(((1, 2), (3, 0))):
+                    rhs = [
+                        jnp.concatenate([w[one, part], w[two, part]], axis=1) for w, part in taken
+                    ]
+                    rhs = jnp.concatenate(rhs, axis=0)
+                    if into == 0:
+                        here = here + dot(lhs, rhs)
+                    else:
+                        aside = aside + dot(lhs, rhs)
             even = (here[:, :128] + from_left(aside[:, :128], cols)).reshape(2, rows, cols, 128)
             odd = (here[:, 128:] + from_right(aside[:, 128:], cols)).reshape(2, rows, cols, 128)
             for k in range(2):
@@ -665,7 +822,8 @@
         array((frames, 2 * rows, outs, 2 * cols)),
         [anywhere()] + vmem(2),
         [
-            pltpu.VMEM((frames + 2, ext, cols, chans), BF16),
+            pltpu.VMEM((frames + 2, ext, cols, 128), BF16),
+            pltpu.VMEM((frames + 2, ext, cols, 128), BF16),
             pltpu.VMEM((2, 2 * rows, 2 * cols, 128), F32),
             pltpu.VMEM(weights.shape, BF16),
             pltpu.SemaphoreType.DMA((3,)),
@@ -706,27 +864,25 @@
     pixels = pixel_grad.transpose(0, 1, 3, 2)
     held = float(frames * height * stripe)
 
-    own_parts = moments(tokens, clips)
-    pixels, own_parts = lax.optimization_barrier((pixels, own_parts))
-    parts = exchanged(own_parts, "clip")
     first, last = edges(pixels)
     above, below = moved(last, 0, 1), moved(first, 0, -1)
-    packed = pack(tokens, parts, seqs, held)
+    packed = pack(tokens, seqs)
     both = combined_weights(conv_two)
     above, below, both, packed = lax.optimization_barrier((above, below, both, packed))
 
     blocks = exchanged(packed, "seq")
-    early, sent = down_early(near(both), flags, pixels, above, below, rows + 2, cols)
-    following = moved(sent, -1, 0)
-    early = near(early)
-    tile, tile_last, stats = unpack(blocks, frames, cols, chans, held * clips)
+    own = far(down_early(near(both), flags, pixels, above, below, rows + 2, cols))
+    following = moved(own, -1, 0)
+    tile, tile_last, parts = unpack(blocks, frames, cols, chans, clips, held)
+    tile = far(tile)
+    late = down_late(near(both), flags, pixels, above, below, rows + 2, cols)
+    parts, late = lax.optimization_barrier((exchanged(parts, "clip"), late))
+    stats = group_stats(parts, held * seqs)
+    tile_last, stats = lax.optimization_barrier((tile_last, stats))
     tile_z = moved(tile_last, 1, 0)
-    above, below, tile = lax.optimization_barrier((above, below, tile))
-    tile, stats = near(tile), near(stats)
-
-    late, near_one = down_late(conv_one, near(both), flags, pixels, above, below, rows + 2, cols)
-    blocks = back(stats, near(near_one), tile, early, near(late), following, seqs)
-    home = exchanged(blocks, "seq")
+    stats = near(stats)
+
+    home = exchanged(back(stats, conv_one, tile, own, late, following, seqs), "seq")
 
     mid, mid_last = middle(flags, stats, conv_one, tile, tile_z)
     decoded = decode(both, moved(mid_last, 1, 0), near(mid), outs)

time: 105 us -> 99.7 us (0.950)
  local copies, waits for them, and re-layouts: 6.33 us -> 1.34 us
  starting transfers between devices: 42 us -> 38.9 us
  Pallas kernels: 41.4 us -> 44.2 us
    unnamed x22 -> x10, local copies, waits for them, and re-layouts: 6.33 us -> 1.34 us
    pallas_call x7, Pallas kernels: 23.7 us -> 27.3 us  [the longest x1 8.13 us: back(): call(back_kernel, 'back', pltpu.HBM((seqs, 12 * frames + EXTRA, 128), BF1...]
    ppermute x2, waiting for transfers between devices: 0.01 us -> 2.51 us  [moved(): return lax.ppermute(block, 'seq', route)]
    all_to_all x4, starting transfers between devices: 28.1 us -> 25.9 us  [exchanged(): return lax.all_to_all(blocks, axis, 0, 0, tiled=True)]
    ppermute x3, waiting for transfers between devices: 2.07 us -> 0.51 us  [moved(): return lax.ppermute(block, 'clip', route)]
  transfers between devices with their start and end apart: 9 -> 9, of which waited for: 4 -> 5; matrix products, arithmetic and copies ran while one was open for 0% -> 0% of each run, Pallas kernels for 37% -> 41%
where the time goes in v3:
time: 99.7 us; the launch traced here: 98.5 us
  Pallas kernels  44.2 us (44%)
  starting transfers between devices  38.9 us (39%)
  waiting for transfers between devices  13.1 us (13%)
  local copies, waits for them, and re-layouts  1.34 us (1%)
    all_to_all x4, starting transfers between devices, exchanged(): return lax.all_to_all(blocks, axis, 0, 0, tiled=True)  25.9 us
    all_to_all x4, waiting for transfers between devices, exchanged(): return lax.all_to_all(blocks, axis, 0, 0, tiled=True)  10.1 us
    pallas_call x1, Pallas kernels, back(): call(back_kernel, 'back', pltpu.HBM((seqs, 12 * frames + EXTRA, 128), BF1...  8.13 us
    pallas_call x1, Pallas kernels, middle(): call(mid_kernel, 'middle', (kept((frames, rows, cols, chans)), array((3,...  8.09 us
    pallas_call x1, Pallas kernels, down_early(): call(functools.partial(early_kernel, plan), 'down_early', pltpu.HBM((6, r...  7.61 us
    ppermute x2, starting transfers between devices, moved(): return lax.ppermute(block, 'seq', route)  7.15 us
    pallas_call x1, Pallas kernels, decode(): call(decode_kernel, 'decode', array((frames, 2 * rows, outs, 2 * cols)),...  5.98 us
    ppermute x3, starting transfers between devices, moved(): return lax.ppermute(block, 'clip', route)  5.81 us
  transfers between devices with their start and end apart: 9, of which 5 were waited for; matrix products, arithmetic and copies ran while one was open for 0% of the time, Pallas kernels for 41%

profile of v3, /device:TPU:1, one launch (start us, length us, event | category | flops | bytes accessed | tf_op | source)
XLA Modules:
  0.0 98.5 jit_solution(9343632377590075844)
XLA Ops:
  0.6 0.0 copy-start.3
  0.6 1.9 %edges.1 = (bf16[4,3,96,128]{3,2,1,0:T(8,128)(2,1)}, bf16[4,3,96,128]{3,2,1,0:T(8,128)(2,1)}) custom-call(bf16[4,8,96,128]{3,2,1,0:T(8,128)(2,1)} %bitcast.7), custom_call_target="tpu_custom_call" | custom-call | flops 1000000 | bytes 1000000 | tf_op jit(solution)/shard_map/edges/pallas_call | solution.py:191
  2.5 4.6 %collective-permute-start = (bf16[4,3,96,128]{3,2,1,0:T(8,128)(2,1)}, bf16[4,3,96,128]{3,2,1,0:T(8,128)(2,1)}, u32[]{:S(2)}, u32[]{:S(2)}) collective-permute-start(bf16[4,3,96,128]{3,2,1,0:T(8,128)(2,1)} %get-tuple-element.19), channel_id=1, source_target_pairs={{0,8},{8,16},{16,24},{24,32},{32,40},{40,48},{48,56},{56,64},{64,7... | collective-permute-start | bytes 884744 | tf_op jit(solution)/shard_map/ppermute | solution.py:839
  7.1 2.6 %collective-permute-start.1 = (bf16[4,3,96,128]{3,2,1,0:T(8,128)(2,1)}, bf16[4,3,96,128]{3,2,1,0:T(8,128)(2,1)}, u32[]{:S(2)}, u32[]{:S(2)}) collective-permute-start(bf16[4,3,96,128]{3,2,1,0:T(8,128)(2,1)} %get-tuple-element.20), channel_id=1, source_target_pairs={{8,0},{16,8},{24,16},{32,24},{40,32},{48,40},{56,48},{64,56},{72,6... | collective-permute-start | bytes 884744 | tf_op jit(solution)/shard_map/ppermute | solution.py:839
  9.7 0.0 copy-start.2
  9.7 1.3 %copy-done.2 = bf16[3,3,3,192,96]{4,3,2,1,0:T(8,128)(2,1)S(1)} copy-done((bf16[3,3,3,192,96]{4,3,2,1,0:T(8,128)(2,1)S(1)}, bf16[3,3,3,192,96]{4,3,2,1,0:T(8,128)(2,1)}, u32[]{:S(2)}) %copy-start.2) | copy-done | bytes 995352
  11.0 0.5 combine_weights.1.weights.w_hbm
  11.5 0.0 copy-start.1
  11.5 1.4 %pack.1 = bf16[32,112,128]{2,1,0:T(8,128)(2,1)} custom-call(bf16[4,2,192,128]{3,2,1,0:T(8,128)(2,1)S(1)} %bitcast.10), custom_call_target="tpu_custom_call" | custom-call | flops 1000000000 | bytes 4194304 | tf_op jit(solution)/shard_map/pack/pallas_call | solution.py:250
  13.0 2.5 %collective-permute-done.1.below = bf16[4,3,96,128]{3,2,1,0:T(8,128)(2,1)} collective-permute-done((bf16[4,3,96,128]{3,2,1,0:T(8,128)(2,1)}, bf16[4,3,96,128]{3,2,1,0:T(8,128)(2,1)}, u32[]{:S(2)}, u32[]{:S(2)}) %collective-permute-start.1) | collective-permute-done | bytes 294944 | tf_op jit(solution)/shard_map/ppermute | solution.py:839
  15.5 8.5 %all-to-all-start = ((bf16[32,112,128]{2,1,0:T(8,128)(2,1)}), bf16[32,112,128]{2,1,0:T(8,128)(2,1)}, u32[]{:S(2)}, u32[]{:S(2)}) async-start(bf16[32,112,128]{2,1,0:T(8,128)(2,1)} %pack.1), calls=%async_computation | async-start | bytes 1835008 | tf_op jit(solution)/shard_map/all_to_all | solution.py:853
  23.9 0.1 add_convert_fusion.flags
  24.0 7.6 %down_early.1.own_hbm = bf16[6,6,64,128]{3,2,1,0:T(8,128)(2,1)} custom-call(bf16[3,4,4,192,128]{4,3,2,1,0:T(8,128)(2,1)S(1)} %combine_weights.1.weights.w_hbm, f32[3]{0:T(128)S(1)} %add_convert_fusion.flags, bf16[4,8,96,128]{3,2,1,0:T(8,128)(2,1)S(1)} %bitcast.8, bf16[4,3,96,128]{3,2,1,0:T(8,128)(2,1)} %collective-permute-done.above, ...), custom_call_target="tpu_custom_call" | custom-call | flops 4026531840 | bytes 4194304 | tf_op jit(solution)/shard_map/down_early/pallas_call | solution.py:420
  31.6 1.3 %collective-permute-start.2 = (bf16[6,6,64,128]{3,2,1,0:T(8,128)(2,1)}, bf16[6,6,64,128]{3,2,1,0:T(8,128)(2,1)}, u32[]{:S(2)}, u32[]{:S(2)}) collective-permute-start(bf16[6,6,64,128]{3,2,1,0:T(8,128)(2,1)} %down_early.1.own_hbm), channel_id=1, source_target_pairs={{1,0},{2,1},{3,2},{4,3},{5,4},{6,5},{7,6},{9,8},{10,9},{11,10},{12... | collective-permute-start | bytes 1769480 | tf_op jit(solution)/shard_map/ppermute | solution.py:842
  32.9 6.5 %all-to-all-done.x_ref = bf16[32,112,128]{2,1,0:T(8,128)(2,1)} async-done(((bf16[32,112,128]{2,1,0:T(8,128)(2,1)}), bf16[32,112,128]{2,1,0:T(8,128)(2,1)}, u32[]{:S(2)}, u32[]{:S(2)}) %all-to-all-start) | async-done | bytes 917536 | tf_op jit(solution)/shard_map/all_to_all | solution.py:853
  39.5 3.3 %unpack.1 = (bf16[4,8,64,192]{3,2,1,0:T(8,128)(2,1)}, bf16[2,8,64,192]{3,2,1,0:T(8,128)(2,1)}, f32[8,2,192]{2,1,0:T(2,128)}) custom-call(bf16[32,112,128]{2,1,0:T(8,128)(2,1)} %all-to-all-done.x_ref), custom_call_target="tpu_custom_call" | custom-call | flops 1000000000 | bytes 4194304 | tf_op jit(solution)/shard_map/unpack/pallas_call | solution.py:277
  42.8 8.2 %all-to-all-start.1 = ((f32[8,2,192]{2,1,0:T(2,128)}), f32[8,2,192]{2,1,0:T(2,128)S(1)}, u32[]{:S(2)}, u32[]{:S(2)}) async-start(f32[8,2,192]{2,1,0:T(2,128)} %get-tuple-element.23), calls=%async_computation.1 | async-start | bytes 32768 | tf_op jit(solution)/shard_map/all_to_all | solution.py:853
  51.0 4.4 %down_late.1.late_hbm = f32[2,6,64,192]{3,2,1,0:T(8,128)} custom-call(bf16[3,4,4,192,128]{4,3,2,1,0:T(8,128)(2,1)S(1)} %combine_weights.1.weights.w_hbm, f32[3]{0:T(128)S(1)} %add_convert_fusion.flags, bf16[4,8,96,128]{3,2,1,0:T(8,128)(2,1)S(1)} %bitcast.9, bf16[4,3,96,128]{3,2,1,0:T(8,128)(2,1)} %collective-permute-done.above, ...), custom_call_target="tpu_custom_call" | custom-call | flops 1207959552 | bytes 4194304 | tf_op jit(solution)/shard_map/down_late/pallas_call | solution.py:433
  55.4 2.2 %all-to-all-done.1.parts_ref = f32[8,2,192]{2,1,0:T(2,128)S(1)} async-done(((f32[8,2,192]{2,1,0:T(2,128)}), f32[8,2,192]{2,1,0:T(2,128)S(1)}, u32[]{:S(2)}, u32[]{:S(2)}) %all-to-all-start.1) | async-done | bytes 12320 | tf_op jit(solution)/shard_map/all_to_all | solution.py:853
  57.6 0.6 group_stats.1.stats.stats_ref
  58.1 2.4 %collective-permute-start.3 = (bf16[2,8,64,192]{3,2,1,0:T(8,128)(2,1)}, bf16[2,8,64,192]{3,2,1,0:T(8,128)(2,1)S(1)}, u32[]{:S(2)}, u32[]{:S(2)}) collective-permute-start(bf16[2,8,64,192]{3,2,1,0:T(8,128)(2,1)} %get-tuple-element.31), channel_id=1, source_target_pairs={{0,1},{1,2},{2,3},{3,4},{4,5},{5,6},{6,7},{8,9},{9,10},{10,11},{11... | collective-permute-start | bytes 1179656 | tf_op jit(solution)/shard_map/ppermute | solution.py:842
  60.5 8.1 %back.1 = bf16[32,64,128]{2,1,0:T(8,128)(2,1)} custom-call(f32[2,192]{1,0:T(2,128)S(1)} %group_stats.1.stats.stats_ref, bf16[3,3,3,192,192]{4,3,2,1,0:T(8,128)(2,1)} %w_hbm.3, bf16[4,8,64,192]{3,2,1,0:T(8,128)(2,1)} %get-tuple-element.29.tile_hbm, bf16[6,6,64,128]{3,2,1,0:T(8,128)(2,1)} %down_early.1.own_hbm, f32[2,6,64,192]{3,2,1,0:T(8,128)} %down_late.1.late_hbm, ...), custom_call_target="tpu_custom_call" | custom-call | flops 2818572288 | bytes 4194304 | tf_op jit(solution)/shard_map/back/pallas_call | solution.py:532
  68.7 5.9 %all-to-all-start.2 = ((bf16[32,64,128]{2,1,0:T(8,128)(2,1)}), bf16[32,64,128]{2,1,0:T(8,128)(2,1)S(1)}, u32[]{:S(2)}, u32[]{:S(2)}) async-start(bf16[32,64,128]{2,1,0:T(8,128)(2,1)} %back.1), calls=%async_computation.2 | async-start | bytes 1048576 | tf_op jit(solution)/shard_map/all_to_all | solution.py:853
  74.6 8.1 %middle.1 = (bf16[4,6,64,192]{3,2,1,0:T(8,128)(2,1)S(1)}, bf16[3,6,64,128]{3,2,1,0:T(8,128)(2,1)S(1)}) custom-call(f32[3]{0:T(128)S(1)} %add_convert_fusion.flags, f32[2,192]{1,0:T(2,128)S(1)} %group_stats.1.stats.stats_ref, bf16[3,3,3,192,192]{4,3,2,1,0:T(8,128)(2,1)} %w_hbm.3, bf16[4,8,64,192]{3,2,1,0:T(8,128)(2,1)} %get-tuple-element.29.tile_hbm, ...), custom_call_target="tpu_custom_call" | custom-call | flops 5435817984 | bytes 4194304 | tf_op jit(solution)/shard_map/middle/pallas_call | solution.py:732
  82.7 2.2 %collective-permute-start.4 = (bf16[3,6,64,128]{3,2,1,0:T(8,128)(2,1)S(1)}, bf16[3,6,64,128]{3,2,1,0:T(8,128)(2,1)S(1)}, u32[]{:S(2)}, u32[]{:S(2)}) collective-permute-start(bf16[3,6,64,128]{3,2,1,0:T(8,128)(2,1)S(1)} %get-tuple-element.32), channel_id=1, source_target_pairs={{0,1},{1,2},{2,3},{3,4},{4,5},{5,6},{6,7},{8,9},{9,10},{10,11},{11... | collective-permute-start | bytes 884744 | tf_op jit(solution)/shard_map/ppermute | solution.py:842
  84.9 1.3 %all-to-all-done.2.x_ref = bf16[32,64,128]{2,1,0:T(8,128)(2,1)S(1)} async-done(((bf16[32,64,128]{2,1,0:T(8,128)(2,1)}), bf16[32,64,128]{2,1,0:T(8,128)(2,1)S(1)}, u32[]{:S(2)}, u32[]{:S(2)}) %all-to-all-start.2) | async-done | bytes 524320 | tf_op jit(solution)/shard_map/all_to_all | solution.py:853
  86.2 0.8 local_sums.1
  87.0 3.3 %all-to-all-start.3 = ((f32[8,2,192]{2,1,0:T(2,128)}), f32[8,2,192]{2,1,0:T(2,128)S(1)}, u32[]{:S(2)}, u32[]{:S(2)}) async-start(f32[8,2,192]{2,1,0:T(2,128)} %local_sums.1), calls=%async_computation.3 | async-start | bytes 32768 | tf_op jit(solution)/shard_map/all_to_all | solution.py:853
  90.3 0.5 collective-permute-done.4.before_ref
  90.8 6.0 %decode.1 = bf16[4,8,96,128]{3,2,1,0:T(8,128)(2,1)} custom-call(bf16[3,4,4,192,128]{4,3,2,1,0:T(8,128)(2,1)} %copy-done, bf16[3,6,64,128]{3,2,1,0:T(8,128)(2,1)S(1)} %collective-permute-done.4.before_ref, bf16[4,6,64,192]{3,2,1,0:T(8,128)(2,1)S(1)} %get-tuple-element.33.mid_ref), custom_call_target="tpu_custom_call" | custom-call | flops 3221225472 | bytes 4194304 | tf_op jit(solution)/shard_map/decode/pallas_call | solution.py:819
  96.8 0.0 all-to-all-done.3.parts_ref
  96.9 1.6 %token_gradient.1 = bf16[4,2,192,128]{3,2,1,0:T(8,128)(2,1)} custom-call(bf16[32,64,128]{2,1,0:T(8,128)(2,1)S(1)} %all-to-all-done.2.x_ref, bf16[4,2,192,128]{3,2,1,0:T(8,128)(2,1)S(1)} %bitcast.11, f32[2,192]{1,0:T(2,128)S(1)} %group_stats.1.stats.stats_ref, f32[8,2,192]{2,1,0:T(2,128)S(1)} %all-to-all-done.3.parts_ref), custom_call_target="tpu_custom_call" | custom-call | flops 1000000000 | bytes 4194304 | tf_op jit(solution)/shard_map/token_gradient/pallas_call | solution.py:606
  (9 shorter events, 0.0 us)
Async XLA Ops:
  0.6 10.9 %copy-start.3 = (bf16[4,128,2,192]{1,3,2,0:T(8,128)(2,1)S(1)}, bf16[4,128,2,192]{1,3,2,0:T(8,128)(2,1)}, u32[]{:S(2)}) copy-start(bf16[4,128,2,192]{1,3,2,0:T(8,128)(2,1)} %param.4) | copy-start | bytes 1179652
  2.5 10.5 %collective-permute-start = (bf16[4,3,96,128]{3,2,1,0:T(8,128)(2,1)}, bf16[4,3,96,128]{3,2,1,0:T(8,128)(2,1)}, u32[]{:S(2)}, u32[]{:S(2)}) collective-permute-start(bf16[4,3,96,128]{3,2,1,0:T(8,128)(2,1)} %get-tuple-element.19), channel_id=1, source_target_pairs={{0,8},{8,16},{16,24},{24,32},{32,40},{40,48},{48,56},{56,64},{64,7... | collective-permute-start | bytes 884744 | tf_op jit(solution)/shard_map/ppermute | solution.py:839
  7.1 8.4 %collective-permute-start.1 = (bf16[4,3,96,128]{3,2,1,0:T(8,128)(2,1)}, bf16[4,3,96,128]{3,2,1,0:T(8,128)(2,1)}, u32[]{:S(2)}, u32[]{:S(2)}) collective-permute-start(bf16[4,3,96,128]{3,2,1,0:T(8,128)(2,1)} %get-tuple-element.20), channel_id=1, source_target_pairs={{8,0},{16,8},{24,16},{32,24},{40,32},{48,40},{56,48},{64,56},{72,6... | collective-permute-start | bytes 884744 | tf_op jit(solution)/shard_map/ppermute | solution.py:839
  9.7 1.3 %copy-start.2 = (bf16[3,3,3,192,96]{4,3,2,1,0:T(8,128)(2,1)S(1)}, bf16[3,3,3,192,96]{4,3,2,1,0:T(8,128)(2,1)}, u32[]{:S(2)}) copy-start(bf16[3,3,3,192,96]{4,3,2,1,0:T(8,128)(2,1)} %w_ref.1) | copy-start | bytes 2985988
  11.5 39.5 %copy-start = (bf16[3,4,4,192,128]{4,3,2,1,0:T(8,128)(2,1)}, bf16[3,4,4,192,128]{4,3,2,1,0:T(8,128)(2,1)S(1)}, u32[]{:S(2)}) copy-start(bf16[3,4,4,192,128]{4,3,2,1,0:T(8,128)(2,1)S(1)} %combine_weights.1.weights.w_hbm) | copy-start | bytes 7077892
  11.5 12.5 %copy-start.1 = (bf16[4,8,128,96]{2,3,1,0:T(8,128)(2,1)S(1)}, bf16[4,8,128,96]{2,3,1,0:T(8,128)(2,1)}, u32[]{:S(2)}) copy-start(bf16[4,8,128,96]{2,3,1,0:T(8,128)(2,1)} %param.7) | copy-start | bytes 2359300
  15.5 24.0 %all-to-all-start = ((bf16[32,112,128]{2,1,0:T(8,128)(2,1)}), bf16[32,112,128]{2,1,0:T(8,128)(2,1)}, u32[]{:S(2)}, u32[]{:S(2)}) async-start(bf16[32,112,128]{2,1,0:T(8,128)(2,1)} %pack.1), calls=%async_computation | async-start | bytes 1835008 | tf_op jit(solution)/shard_map/all_to_all | solution.py:853
  31.6 28.9 %collective-permute-start.2 = (bf16[6,6,64,128]{3,2,1,0:T(8,128)(2,1)}, bf16[6,6,64,128]{3,2,1,0:T(8,128)(2,1)}, u32[]{:S(2)}, u32[]{:S(2)}) collective-permute-start(bf16[6,6,64,128]{3,2,1,0:T(8,128)(2,1)} %down_early.1.own_hbm), channel_id=1, source_target_pairs={{1,0},{2,1},{3,2},{4,3},{5,4},{6,5},{7,6},{9,8},{10,9},{11,10},{12... | collective-permute-start | bytes 1769480 | tf_op jit(solution)/shard_map/ppermute | solution.py:842
  42.8 14.8 %all-to-all-start.1 = ((f32[8,2,192]{2,1,0:T(2,128)}), f32[8,2,192]{2,1,0:T(2,128)S(1)}, u32[]{:S(2)}, u32[]{:S(2)}) async-start(f32[8,2,192]{2,1,0:T(2,128)} %get-tuple-element.23), calls=%async_computation.1 | async-start | bytes 32768 | tf_op jit(solution)/shard_map/all_to_all | solution.py:853
  58.1 16.5 %collective-permute-start.3 = (bf16[2,8,64,192]{3,2,1,0:T(8,128)(2,1)}, bf16[2,8,64,192]{3,2,1,0:T(8,128)(2,1)S(1)}, u32[]{:S(2)}, u32[]{:S(2)}) collective-permute-start(bf16[2,8,64,192]{3,2,1,0:T(8,128)(2,1)} %get-tuple-element.31), channel_id=1, source_target_pairs={{0,1},{1,2},{2,3},{3,4},{4,5},{5,6},{6,7},{8,9},{9,10},{10,11},{11... | collective-permute-start | bytes 1179656 | tf_op jit(solution)/shard_map/ppermute | solution.py:842
  68.7 17.6 %all-to-all-start.2 = ((bf16[32,64,128]{2,1,0:T(8,128)(2,1)}), bf16[32,64,128]{2,1,0:T(8,128)(2,1)S(1)}, u32[]{:S(2)}, u32[]{:S(2)}) async-start(bf16[32,64,128]{2,1,0:T(8,128)(2,1)} %back.1), calls=%async_computation.2 | async-start | bytes 1048576 | tf_op jit(solution)/shard_map/all_to_all | solution.py:853
  82.7 8.1 %collective-permute-start.4 = (bf16[3,6,64,128]{3,2,1,0:T(8,128)(2,1)S(1)}, bf16[3,6,64,128]{3,2,1,0:T(8,128)(2,1)S(1)}, u32[]{:S(2)}, u32[]{:S(2)}) collective-permute-start(bf16[3,6,64,128]{3,2,1,0:T(8,128)(2,1)S(1)} %get-tuple-element.32), channel_id=1, source_target_pairs={{0,1},{1,2},{2,3},{3,4},{4,5},{5,6},{6,7},{8,9},{9,10},{10,11},{11... | collective-permute-start | bytes 884744 | tf_op jit(solution)/shard_map/ppermute | solution.py:842
  87.0 9.9 %all-to-all-start.3 = ((f32[8,2,192]{2,1,0:T(2,128)}), f32[8,2,192]{2,1,0:T(2,128)S(1)}, u32[]{:S(2)}, u32[]{:S(2)}) async-start(f32[8,2,192]{2,1,0:T(2,128)} %local_sums.1), calls=%async_computation.3 | async-start | bytes 32768 | tf_op jit(solution)/shard_map/all_to_all | solution.py:853
  90.8 6.0 %copy-start.4 = (bf16[4,128,2,192]{1,3,2,0:T(8,128)(2,1)S(1)}, bf16[4,128,2,192]{1,3,2,0:T(8,128)(2,1)}, u32[]{:S(2)}) copy-start(bf16[4,128,2,192]{1,3,2,0:T(8,128)(2,1)} %param.4) | copy-start | bytes 1179652

commit v4 on v3

--- a/solution.py
+++ b/solution.py
@@ -288,7 +288,7 @@
     )(blocks)
 
 
-def stats_kernel(held, parts_ref, stats_ref):
+def group_stats(parts_ref, held):
     clips, _, chans = parts_ref.shape
     means, spreads = parts_ref[:, 0], parts_ref[:, 1]
     size = chans // GROUPS
@@ -297,13 +297,7 @@
     spread = jnp.sum(spreads, axis=0, keepdims=True)
     spread = spread + held * jnp.sum((means - mean) ** 2, axis=0, keepdims=True)
     var = group_sum(jnp.broadcast_to(spread, (8, chans)))[0:1] / (held * clips * size)
-    stats_ref[...] = jnp.concatenate([mean, lax.rsqrt(var + 1e-06)], axis=0)
-
-
-def group_stats(parts, held):
-    shape = kept(parts.shape[1:], F32)
-    kernel = functools.partial(stats_kernel, held)
-    return call(kernel, "group_stats", shape, vmem(1), [], 10**6)(parts)
+    return mean, lax.rsqrt(var + 1e-06)
 
 
 def down_kernel(first, plan, weights, flags, sources, store, buffer, beside, sems):
@@ -328,15 +322,16 @@
 
     def place(inner):
         def one_frame(i, carry):
-            for n in range(0, lines + 6, 2):
-                if (3 < n < 2 + lines) == inner:
-                    pair = [line(i, n), blank, line(i, n + 1), blank]
-                    picked = nt_dot(select, jnp.concatenate(pair, axis=0)).astype(BF16)
-                    for k in range(2):
-                        for j in range(2):
-                            buffer[i, k, n // 2, :, 128 * j : 128 * (j + 1)] = picked[
-                                cols * j : cols * (j + 1), 128 * k : 128 * (k + 1)
-                            ]
+            firsts = [n for n in range(0, lines + 6, 2) if (3 < n < 2 + lines) == inner]
+            rhs = [x for n in firsts for k in range(2) for x in (line(i, n + k), blank)]
+            picked = nt_dot(select, jnp.concatenate(rhs, axis=0)).astype(BF16)
+            for m, n in enumerate(firsts):
+                for k in range(2):
+                    for j in range(2):
+                        at = 256 * m + 128 * k
+                        buffer[i, k, n // 2, :, 128 * j : 128 * (j + 1)] = picked[
+                            cols * j : cols * (j + 1), at : at + 128
+                        ]
             return carry
 
         lax.fori_loop(0, count, one_frame, 0)
@@ -387,11 +382,22 @@
             )
 
 
-def early_kernel(plan, weights, flags, pixels, above, below, sent_ref, *scratch):
+def early_kernel(plan, weights, flags, pixels, above, below, out_hbm, *scratch):
+    *scratch, sent_ref, out_sems = scratch
+    copies = [
+        pltpu.make_async_copy(sent_ref.at[pl.ds(at, n)], out_hbm.at[pl.ds(at, n)], out_sems.at[k])
+        for k, (at, n) in enumerate(((0, 2), (4, 1), (2, 2), (5, 1)))
+    ]
+
     def store(n, parts):
         store_dense(sent_ref, n, jnp.concatenate([part.astype(BF16) for part in parts], axis=0))
+        if n % 2 == 1:
+            for copy in copies[n - 1 : n + 1]:
+                copy.start()
 
     down_kernel(0, plan, weights, flags, (pixels, above, below), store, *scratch)
+    for copy in copies:
+        copy.wait()
 
 
 def late_kernel(first, plan, weights, flags, pixels, above, below, out_ref, *scratch):
@@ -417,13 +423,21 @@
 def down_early(weights, flags, pixels, above, below, rows, cols):
     frames = pixels.shape[0]
     plan = ((((0, 2), (1, 1), (2, 0)), (), 0), (((0, 0),), (0, 1), 1))
-    return call(
+    return pl.pallas_call(
         functools.partial(early_kernel, plan),
-        "down_early",
-        pltpu.HBM((6, rows, cols, 128), BF16),
-        vmem(1) + [smem()] + vmem(1) + [anywhere()] * 2,
-        down_scratch(frames, pixels, rows, cols),
-        down_cost(plan, rows * cols),
+        name="down_early",
+        out_shape=pltpu.HBM((6, rows, cols, 128), BF16),
+        in_specs=vmem(1) + [smem()] + vmem(1) + [anywhere()] * 2,
+        out_specs=anywhere(),
+        scratch_shapes=[
+            *down_scratch(frames, pixels, rows, cols),
+            pltpu.VMEM((6, rows, cols, 128), BF16),
+            pltpu.SemaphoreType.DMA((4,)),
+        ],
+        compiler_params=pltpu.CompilerParams(vmem_limit_bytes=VMEM_LIMIT),
+        cost_estimate=pl.CostEstimate(
+            flops=down_cost(plan, rows * cols), bytes_accessed=4 * 2**20, transcendentals=0
+        ),
     )(weights, flags, near(pixels), far(above), far(below))
 
 
@@ -441,7 +455,7 @@
 
 
 def back_kernel(
-    stats, w_hbm, tile_hbm, own_hbm, late_hbm, next_hbm, out_ref, *scratch
+    held, parts_ref, w_hbm, tile_hbm, own_hbm, late_hbm, next_hbm, out_ref, stats_ref, *scratch
 ):
     main, rows_pair, frames_pair, rest, weights, tile_ref, own_ref, late_ref, next_ref, sems = scratch
     frames, rows, cols, chans = tile_ref.shape
@@ -458,6 +472,8 @@
         copy.start()
     seqs = out_ref.shape[0]
     size = 2 * rows * cols
+    mean, scale = group_stats(parts_ref, held)
+    stats_ref[...] = jnp.concatenate([mean, scale], axis=0)
     buffer = Packed(main, rows_pair, frames_pair)
     buffer.clear()
     for copy in copies[:3]:
@@ -477,8 +493,6 @@
             buffer.put(frames - 2 + k, r, block[r], tail[r])
     for copy in copies[4:]:
         copy.wait()
-    mean = stats[0:1]
-    scale = stats[1:2]
     order = one_hot(
         size,
         size,
@@ -526,13 +540,13 @@
     out_ref[:, 12 * frames :] = jnp.broadcast_to(extra[None], (seqs, EXTRA, 128))
 
 
-def back(stats, weights, tile, own, late, following, seqs):
+def back(parts, held, weights, tile, own, late, following, seqs):
     frames, ext, cols, chans = tile.shape
     rows = ext - 4
     return call(
-        back_kernel,
+        functools.partial(back_kernel, held),
         "back",
-        pltpu.HBM((seqs, 12 * frames + EXTRA, 128), BF16),
+        (pltpu.HBM((seqs, 12 * frames + EXTRA, 128), BF16), kept((2, chans), F32)),
         vmem(1) + [anywhere()] * 5,
         [
             *packed_scratch(frames + 2, rows + 2, cols),
@@ -545,7 +559,7 @@
             pltpu.SemaphoreType.DMA((6,)),
         ],
         2 * frames * rows * cols * 21 * 65536,
-    )(stats, far(weights), far(tile), far(own), far(late), far(following))
+    )(parts, far(weights), far(tile), far(own), far(late), far(following))
 
 
 def sums_kernel(x_ref, out_ref):
@@ -868,7 +882,7 @@
     above, below = moved(last, 0, 1), moved(first, 0, -1)
     packed = pack(tokens, seqs)
     both = combined_weights(conv_two)
-    above, below, both, packed = lax.optimization_barrier((above, below, both, packed))
+    above, both, packed = lax.optimization_barrier((above, both, packed))
 
     blocks = exchanged(packed, "seq")
     own = far(down_early(near(both), flags, pixels, above, below, rows + 2, cols))
@@ -877,12 +891,11 @@
     tile = far(tile)
     late = down_late(near(both), flags, pixels, above, below, rows + 2, cols)
     parts, late = lax.optimization_barrier((exchanged(parts, "clip"), late))
-    stats = group_stats(parts, held * seqs)
-    tile_last, stats = lax.optimization_barrier((tile_last, stats))
+    parts, tile_last = lax.optimization_barrier((parts, tile_last))
     tile_z = moved(tile_last, 1, 0)
-    stats = near(stats)
-
-    home = exchanged(back(stats, conv_one, tile, own, late, following, seqs), "seq")
+
+    blocks, stats = back(parts, held * seqs, conv_one, tile, own, late, following, seqs)
+    home, stats = exchanged(blocks, "seq"), near(stats)
 
     mid, mid_last = middle(flags, stats, conv_one, tile, tile_z)
     decoded = decode(both, moved(mid_last, 1, 0), near(mid), outs)

time: 99.7 us -> 95.1 us (0.954)
  waiting for transfers between devices: 13.1 us -> 10.7 us
  starting transfers between devices: 38.9 us -> 37.6 us
    ppermute x2, waiting for transfers between devices: 2.51 us -> 0.01 us  [moved(): return lax.ppermute(block, 'seq', route)]
    pallas_call x3 -> x2, Pallas kernels: 16.3 us -> 15.9 us  [the longest x1 8.33 us: back(): call(functools.partial(back_kernel, held), 'back', (pltpu.HBM((seqs, 12 *...]
  transfers between devices with their start and end apart: 9 -> 9, of which waited for: 5 -> 5; matrix products, arithmetic and copies ran while one was open for 0% -> 0% of each run, Pallas kernels for 41% -> 43%
where the time goes in v4:
time: 95.1 us; the launch traced here: 93.9 us
  Pallas kernels  43.7 us (46%)
  starting transfers between devices  37.6 us (40%)
  waiting for transfers between devices  10.7 us (11%)
  local copies, waits for them, and re-layouts  1.01 us (1%)
    all_to_all x4, starting transfers between devices, exchanged(): return lax.all_to_all(blocks, axis, 0, 0, tiled=True)  25.1 us
    all_to_all x4, waiting for transfers between devices, exchanged(): return lax.all_to_all(blocks, axis, 0, 0, tiled=True)  10.2 us
    pallas_call x1, Pallas kernels, back(): call(functools.partial(back_kernel, held), 'back', (pltpu.HBM((seqs, 12 *...  8.33 us
    pallas_call x1, Pallas kernels, middle(): call(mid_kernel, 'middle', (kept((frames, rows, cols, chans)), array((3,...  8.09 us
    pallas_call x1, Pallas kernels, down_early(): pl.pallas_call(functools.partial(early_kernel, plan), name='down_early',...  7.56 us
    ppermute x2, starting transfers between devices, moved(): return lax.ppermute(block, 'seq', route)  6.65 us
    pallas_call x1, Pallas kernels, decode(): call(decode_kernel, 'decode', array((frames, 2 * rows, outs, 2 * cols)),...  5.98 us
    ppermute x3, starting transfers between devices, moved(): return lax.ppermute(block, 'clip', route)  5.79 us
  transfers between devices with their start and end apart: 9, of which 5 were waited for; matrix products, arithmetic and copies ran while one was open for 0% of the time, Pallas kernels for 43%

profile of v4, /device:TPU:1, one launch (start us, length us, event | category | flops | bytes accessed | tf_op | source)
XLA Modules:
  0.0 93.9 jit_solution(1190184294803995962)
XLA Ops:
  0.6 1.8 %edges.1 = (bf16[4,3,96,128]{3,2,1,0:T(8,128)(2,1)}, bf16[4,3,96,128]{3,2,1,0:T(8,128)(2,1)}) custom-call(bf16[4,8,96,128]{3,2,1,0:T(8,128)(2,1)} %bitcast.7), custom_call_target="tpu_custom_call" | custom-call | flops 1000000 | bytes 1000000 | tf_op jit(solution)/shard_map/edges/pallas_call | solution.py:191
  2.4 0.0 copy-start.2
  2.5 4.7 %collective-permute-start = (bf16[4,3,96,128]{3,2,1,0:T(8,128)(2,1)}, bf16[4,3,96,128]{3,2,1,0:T(8,128)(2,1)S(1)}, u32[]{:S(2)}, u32[]{:S(2)}) collective-permute-start(bf16[4,3,96,128]{3,2,1,0:T(8,128)(2,1)} %get-tuple-element.20), channel_id=1, source_target_pairs={{0,8},{8,16},{16,24},{24,32},{32,40},{40,48},{48,56},{56,64},{64,7... | collective-permute-start | bytes 884744 | tf_op jit(solution)/shard_map/ppermute | solution.py:853
  7.2 1.9 %collective-permute-start.1 = (bf16[4,3,96,128]{3,2,1,0:T(8,128)(2,1)}, bf16[4,3,96,128]{3,2,1,0:T(8,128)(2,1)}, u32[]{:S(2)}, u32[]{:S(2)}) collective-permute-start(bf16[4,3,96,128]{3,2,1,0:T(8,128)(2,1)} %get-tuple-element.25), channel_id=1, source_target_pairs={{8,0},{16,8},{24,16},{32,24},{40,32},{48,40},{56,48},{64,56},{72,6... | collective-permute-start | bytes 884744 | tf_op jit(solution)/shard_map/ppermute | solution.py:853
  9.1 0.0 copy-start.3
  9.1 1.0 %copy-done.3 = bf16[4,128,2,192]{1,3,2,0:T(8,128)(2,1)S(1)} copy-done((bf16[4,128,2,192]{1,3,2,0:T(8,128)(2,1)S(1)}, bf16[4,128,2,192]{1,3,2,0:T(8,128)(2,1)}, u32[]{:S(2)}) %copy-start.3) | copy-done | bytes 393240
  10.1 1.4 %pack.1 = bf16[32,112,128]{2,1,0:T(8,128)(2,1)} custom-call(bf16[4,2,192,128]{3,2,1,0:T(8,128)(2,1)S(1)} %bitcast.10), custom_call_target="tpu_custom_call" | custom-call | flops 1000000000 | bytes 4194304 | tf_op jit(solution)/shard_map/pack/pallas_call | solution.py:250
  11.5 0.5 combine_weights.1.weights.w_hbm
  12.0 0.0 collective-permute-done.above
  12.1 7.7 %all-to-all-start = ((bf16[32,112,128]{2,1,0:T(8,128)(2,1)}), bf16[32,112,128]{2,1,0:T(8,128)(2,1)}, u32[]{:S(2)}, u32[]{:S(2)}) async-start(bf16[32,112,128]{2,1,0:T(8,128)(2,1)} %pack.1), calls=%async_computation | async-start | bytes 1835008 | tf_op jit(solution)/shard_map/all_to_all | solution.py:867
  19.8 0.1 add_convert_fusion.flags
  19.9 0.0 collective-permute-done.1.below
  19.9 7.6 %down_early.1.own_hbm = bf16[6,6,64,128]{3,2,1,0:T(8,128)(2,1)} custom-call(bf16[3,4,4,192,128]{4,3,2,1,0:T(8,128)(2,1)S(1)} %combine_weights.1.weights.w_hbm, f32[3]{0:T(128)S(1)} %add_convert_fusion.flags, bf16[4,8,96,128]{3,2,1,0:T(8,128)(2,1)S(1)} %bitcast.8, bf16[4,3,96,128]{3,2,1,0:T(8,128)(2,1)} %copy-done.5, ...), custom_call_target="tpu_custom_call" | custom-call | flops 4026531840 | bytes 4194304 | tf_op jit(solution)/shard_map/down_early/pallas_call | solution.py:426
  27.4 1.3 %collective-permute-start.2 = (bf16[6,6,64,128]{3,2,1,0:T(8,128)(2,1)}, bf16[6,6,64,128]{3,2,1,0:T(8,128)(2,1)}, u32[]{:S(2)}, u32[]{:S(2)}) collective-permute-start(bf16[6,6,64,128]{3,2,1,0:T(8,128)(2,1)} %down_early.1.own_hbm), channel_id=1, source_target_pairs={{1,0},{2,1},{3,2},{4,3},{5,4},{6,5},{7,6},{9,8},{10,9},{11,10},{12... | collective-permute-start | bytes 1769480 | tf_op jit(solution)/shard_map/ppermute | solution.py:856
  28.7 6.6 %all-to-all-done.x_ref = bf16[32,112,128]{2,1,0:T(8,128)(2,1)} async-done(((bf16[32,112,128]{2,1,0:T(8,128)(2,1)}), bf16[32,112,128]{2,1,0:T(8,128)(2,1)}, u32[]{:S(2)}, u32[]{:S(2)}) %all-to-all-start) | async-done | bytes 917536 | tf_op jit(solution)/shard_map/all_to_all | solution.py:867
  35.3 3.3 %unpack.1 = (bf16[4,8,64,192]{3,2,1,0:T(8,128)(2,1)}, bf16[2,8,64,192]{3,2,1,0:T(8,128)(2,1)}, f32[8,2,192]{2,1,0:T(2,128)}) custom-call(bf16[32,112,128]{2,1,0:T(8,128)(2,1)} %all-to-all-done.x_ref), custom_call_target="tpu_custom_call" | custom-call | flops 1000000000 | bytes 4194304 | tf_op jit(solution)/shard_map/unpack/pallas_call | solution.py:277
  38.6 8.2 %all-to-all-start.1 = ((f32[8,2,192]{2,1,0:T(2,128)}), f32[8,2,192]{2,1,0:T(2,128)S(1)}, u32[]{:S(2)}, u32[]{:S(2)}) async-start(f32[8,2,192]{2,1,0:T(2,128)} %get-tuple-element.22), calls=%async_computation.1 | async-start | bytes 32768 | tf_op jit(solution)/shard_map/all_to_all | solution.py:867
  46.8 4.4 %down_late.1.late_hbm = f32[2,6,64,192]{3,2,1,0:T(8,128)} custom-call(bf16[3,4,4,192,128]{4,3,2,1,0:T(8,128)(2,1)S(1)} %combine_weights.1.weights.w_hbm, f32[3]{0:T(128)S(1)} %add_convert_fusion.flags, bf16[4,8,96,128]{3,2,1,0:T(8,128)(2,1)S(1)} %bitcast.9, bf16[4,3,96,128]{3,2,1,0:T(8,128)(2,1)} %copy-done.5, ...), custom_call_target="tpu_custom_call" | custom-call | flops 1207959552 | bytes 4194304 | tf_op jit(solution)/shard_map/down_late/pallas_call | solution.py:447
  51.2 2.2 %all-to-all-done.1.parts_ref = f32[8,2,192]{2,1,0:T(2,128)S(1)} async-done(((f32[8,2,192]{2,1,0:T(2,128)}), f32[8,2,192]{2,1,0:T(2,128)S(1)}, u32[]{:S(2)}, u32[]{:S(2)}) %all-to-all-start.1) | async-done | bytes 12320 | tf_op jit(solution)/shard_map/all_to_all | solution.py:867
  53.4 2.3 %collective-permute-start.3 = (bf16[2,8,64,192]{3,2,1,0:T(8,128)(2,1)}, bf16[2,8,64,192]{3,2,1,0:T(8,128)(2,1)S(1)}, u32[]{:S(2)}, u32[]{:S(2)}) collective-permute-start(bf16[2,8,64,192]{3,2,1,0:T(8,128)(2,1)} %get-tuple-element.33), channel_id=1, source_target_pairs={{0,1},{1,2},{2,3},{3,4},{4,5},{5,6},{6,7},{8,9},{9,10},{10,11},{11... | collective-permute-start | bytes 1179656 | tf_op jit(solution)/shard_map/ppermute | solution.py:856
  55.8 0.0 collective-permute-done.2.next_hbm
  55.8 8.3 %back.1 = (bf16[32,64,128]{2,1,0:T(8,128)(2,1)}, f32[2,192]{1,0:T(2,128)S(1)}) custom-call(f32[8,2,192]{2,1,0:T(2,128)S(1)} %all-to-all-done.1.parts_ref, bf16[3,3,3,192,192]{4,3,2,1,0:T(8,128)(2,1)} %w_hbm.3, bf16[4,8,64,192]{3,2,1,0:T(8,128)(2,1)} %get-tuple-element.29.tile_hbm, bf16[6,6,64,128]{3,2,1,0:T(8,128)(2,1)} %down_early.1.own_hbm, ...), custom_call_target="tpu_custom_call" | custom-call | flops 2818572288 | bytes 4194304 | tf_op jit(solution)/shard_map/back/pallas_call | solution.py:546
  64.1 5.9 %all-to-all-start.2 = ((bf16[32,64,128]{2,1,0:T(8,128)(2,1)}), bf16[32,64,128]{2,1,0:T(8,128)(2,1)S(1)}, u32[]{:S(2)}, u32[]{:S(2)}) async-start(bf16[32,64,128]{2,1,0:T(8,128)(2,1)} %get-tuple-element.31), calls=%async_computation.2 | async-start | bytes 1048576 | tf_op jit(solution)/shard_map/all_to_all | solution.py:867
  70.0 8.1 %middle.1 = (bf16[4,6,64,192]{3,2,1,0:T(8,128)(2,1)S(1)}, bf16[3,6,64,128]{3,2,1,0:T(8,128)(2,1)S(1)}) custom-call(f32[3]{0:T(128)S(1)} %add_convert_fusion.flags, f32[2,192]{1,0:T(2,128)S(1)} %get-tuple-element.32.stats.stats_ref, bf16[3,3,3,192,192]{4,3,2,1,0:T(8,128)(2,1)} %w_hbm.3, bf16[4,8,64,192]{3,2,1,0:T(8,128)(2,1)} %get-tuple-element.29.tile_hbm, ...), custom_call_target="tpu_custom_call" | custom-call | flops 5435817984 | bytes 4194304 | tf_op jit(solution)/shard_map/middle/pallas_call | solution.py:746
  78.1 2.1 %collective-permute-start.4 = (bf16[3,6,64,128]{3,2,1,0:T(8,128)(2,1)S(1)}, bf16[3,6,64,128]{3,2,1,0:T(8,128)(2,1)S(1)}, u32[]{:S(2)}, u32[]{:S(2)}) collective-permute-start(bf16[3,6,64,128]{3,2,1,0:T(8,128)(2,1)S(1)} %get-tuple-element.34), channel_id=1, source_target_pairs={{0,1},{1,2},{2,3},{3,4},{4,5},{5,6},{6,7},{8,9},{9,10},{10,11},{11... | collective-permute-start | bytes 884744 | tf_op jit(solution)/shard_map/ppermute | solution.py:856
  80.3 1.3 %all-to-all-done.2.x_ref = bf16[32,64,128]{2,1,0:T(8,128)(2,1)S(1)} async-done(((bf16[32,64,128]{2,1,0:T(8,128)(2,1)}), bf16[32,64,128]{2,1,0:T(8,128)(2,1)S(1)}, u32[]{:S(2)}, u32[]{:S(2)}) %all-to-all-start.2) | async-done | bytes 524320 | tf_op jit(solution)/shard_map/all_to_all | solution.py:867
  81.6 0.8 local_sums.1
  82.4 3.3 %all-to-all-start.3 = ((f32[8,2,192]{2,1,0:T(2,128)}), f32[8,2,192]{2,1,0:T(2,128)S(1)}, u32[]{:S(2)}, u32[]{:S(2)}) async-start(f32[8,2,192]{2,1,0:T(2,128)} %local_sums.1), calls=%async_computation.3 | async-start | bytes 32768 | tf_op jit(solution)/shard_map/all_to_all | solution.py:867
  85.7 0.5 collective-permute-done.4.before_ref
  86.2 6.0 %decode.1 = bf16[4,8,96,128]{3,2,1,0:T(8,128)(2,1)} custom-call(bf16[3,4,4,192,128]{4,3,2,1,0:T(8,128)(2,1)} %copy-done, bf16[3,6,64,128]{3,2,1,0:T(8,128)(2,1)S(1)} %collective-permute-done.4.before_ref, bf16[4,6,64,192]{3,2,1,0:T(8,128)(2,1)S(1)} %get-tuple-element.35.mid_ref), custom_call_target="tpu_custom_call" | custom-call | flops 3221225472 | bytes 4194304 | tf_op jit(solution)/shard_map/decode/pallas_call | solution.py:833
  92.2 0.1 all-to-all-done.3.parts_ref
  92.3 1.6 %token_gradient.1 = bf16[4,2,192,128]{3,2,1,0:T(8,128)(2,1)} custom-call(bf16[32,64,128]{2,1,0:T(8,128)(2,1)S(1)} %all-to-all-done.2.x_ref, bf16[4,2,192,128]{3,2,1,0:T(8,128)(2,1)S(1)} %bitcast.11, f32[2,192]{1,0:T(2,128)S(1)} %get-tuple-element.32.stats.stats_ref, f32[8,2,192]{2,1,0:T(2,128)S(1)} %all-to-all-done.3.parts_ref), custom_call_target="tpu_custom_call" | custom-call | flops 1000000000 | bytes 4194304 | tf_op jit(solution)/shard_map/token_gradient/pallas_call | solution.py:620
  (10 shorter events, 0.0 us)
Async XLA Ops:
  2.4 9.1 %copy-start.2 = (bf16[3,3,3,192,96]{4,3,2,1,0:T(8,128)(2,1)S(1)}, bf16[3,3,3,192,96]{4,3,2,1,0:T(8,128)(2,1)}, u32[]{:S(2)}) copy-start(bf16[3,3,3,192,96]{4,3,2,1,0:T(8,128)(2,1)} %w_ref.1) | copy-start | bytes 2985988
  2.5 9.6 %collective-permute-start = (bf16[4,3,96,128]{3,2,1,0:T(8,128)(2,1)}, bf16[4,3,96,128]{3,2,1,0:T(8,128)(2,1)S(1)}, u32[]{:S(2)}, u32[]{:S(2)}) collective-permute-start(bf16[4,3,96,128]{3,2,1,0:T(8,128)(2,1)} %get-tuple-element.20), channel_id=1, source_target_pairs={{0,8},{8,16},{16,24},{24,32},{32,40},{40,48},{48,56},{56,64},{64,7... | collective-permute-start | bytes 884744 | tf_op jit(solution)/shard_map/ppermute | solution.py:853
  7.2 12.7 %collective-permute-start.1 = (bf16[4,3,96,128]{3,2,1,0:T(8,128)(2,1)}, bf16[4,3,96,128]{3,2,1,0:T(8,128)(2,1)}, u32[]{:S(2)}, u32[]{:S(2)}) collective-permute-start(bf16[4,3,96,128]{3,2,1,0:T(8,128)(2,1)} %get-tuple-element.25), channel_id=1, source_target_pairs={{8,0},{16,8},{24,16},{32,24},{40,32},{48,40},{56,48},{64,56},{72,6... | collective-permute-start | bytes 884744 | tf_op jit(solution)/shard_map/ppermute | solution.py:853
  9.1 1.0 %copy-start.3 = (bf16[4,128,2,192]{1,3,2,0:T(8,128)(2,1)S(1)}, bf16[4,128,2,192]{1,3,2,0:T(8,128)(2,1)}, u32[]{:S(2)}) copy-start(bf16[4,128,2,192]{1,3,2,0:T(8,128)(2,1)} %param.4) | copy-start | bytes 1179652
  11.5 8.3 %copy-start.1 = (bf16[4,8,128,96]{2,3,1,0:T(8,128)(2,1)S(1)}, bf16[4,8,128,96]{2,3,1,0:T(8,128)(2,1)}, u32[]{:S(2)}) copy-start(bf16[4,8,128,96]{2,3,1,0:T(8,128)(2,1)} %param.7) | copy-start | bytes 2359300
  12.0 34.7 %copy-start = (bf16[3,4,4,192,128]{4,3,2,1,0:T(8,128)(2,1)}, bf16[3,4,4,192,128]{4,3,2,1,0:T(8,128)(2,1)S(1)}, u32[]{:S(2)}) copy-start(bf16[3,4,4,192,128]{4,3,2,1,0:T(8,128)(2,1)S(1)} %combine_weights.1.weights.w_hbm) | copy-start | bytes 7077892
  12.1 7.8 %copy-start.5 = (bf16[4,3,96,128]{3,2,1,0:T(8,128)(2,1)}, bf16[4,3,96,128]{3,2,1,0:T(8,128)(2,1)S(1)}, u32[]{:S(2)}) copy-start(bf16[4,3,96,128]{3,2,1,0:T(8,128)(2,1)S(1)} %collective-permute-done.above) | copy-start | bytes 884740
  12.1 23.2 %all-to-all-start = ((bf16[32,112,128]{2,1,0:T(8,128)(2,1)}), bf16[32,112,128]{2,1,0:T(8,128)(2,1)}, u32[]{:S(2)}, u32[]{:S(2)}) async-start(bf16[32,112,128]{2,1,0:T(8,128)(2,1)} %pack.1), calls=%async_computation | async-start | bytes 1835008 | tf_op jit(solution)/shard_map/all_to_all | solution.py:867
  27.4 28.3 %collective-permute-start.2 = (bf16[6,6,64,128]{3,2,1,0:T(8,128)(2,1)}, bf16[6,6,64,128]{3,2,1,0:T(8,128)(2,1)}, u32[]{:S(2)}, u32[]{:S(2)}) collective-permute-start(bf16[6,6,64,128]{3,2,1,0:T(8,128)(2,1)} %down_early.1.own_hbm), channel_id=1, source_target_pairs={{1,0},{2,1},{3,2},{4,3},{5,4},{6,5},{7,6},{9,8},{10,9},{11,10},{12... | collective-permute-start | bytes 1769480 | tf_op jit(solution)/shard_map/ppermute | solution.py:856
  38.6 14.8 %all-to-all-start.1 = ((f32[8,2,192]{2,1,0:T(2,128)}), f32[8,2,192]{2,1,0:T(2,128)S(1)}, u32[]{:S(2)}, u32[]{:S(2)}) async-start(f32[8,2,192]{2,1,0:T(2,128)} %get-tuple-element.22), calls=%async_computation.1 | async-start | bytes 32768 | tf_op jit(solution)/shard_map/all_to_all | solution.py:867
  53.4 16.6 %collective-permute-start.3 = (bf16[2,8,64,192]{3,2,1,0:T(8,128)(2,1)}, bf16[2,8,64,192]{3,2,1,0:T(8,128)(2,1)S(1)}, u32[]{:S(2)}, u32[]{:S(2)}) collective-permute-start(bf16[2,8,64,192]{3,2,1,0:T(8,128)(2,1)} %get-tuple-element.33), channel_id=1, source_target_pairs={{0,1},{1,2},{2,3},{3,4},{4,5},{5,6},{6,7},{8,9},{9,10},{10,11},{11... | collective-permute-start | bytes 1179656 | tf_op jit(solution)/shard_map/ppermute | solution.py:856
  64.1 17.5 %all-to-all-start.2 = ((bf16[32,64,128]{2,1,0:T(8,128)(2,1)}), bf16[32,64,128]{2,1,0:T(8,128)(2,1)S(1)}, u32[]{:S(2)}, u32[]{:S(2)}) async-start(bf16[32,64,128]{2,1,0:T(8,128)(2,1)} %get-tuple-element.31), calls=%async_computation.2 | async-start | bytes 1048576 | tf_op jit(solution)/shard_map/all_to_all | solution.py:867
  78.1 8.1 %collective-permute-start.4 = (bf16[3,6,64,128]{3,2,1,0:T(8,128)(2,1)S(1)}, bf16[3,6,64,128]{3,2,1,0:T(8,128)(2,1)S(1)}, u32[]{:S(2)}, u32[]{:S(2)}) collective-permute-start(bf16[3,6,64,128]{3,2,1,0:T(8,128)(2,1)S(1)} %get-tuple-element.34), channel_id=1, source_target_pairs={{0,1},{1,2},{2,3},{3,4},{4,5},{5,6},{6,7},{8,9},{9,10},{10,11},{11... | collective-permute-start | bytes 884744 | tf_op jit(solution)/shard_map/ppermute | solution.py:856
  82.4 9.9 %all-to-all-start.3 = ((f32[8,2,192]{2,1,0:T(2,128)}), f32[8,2,192]{2,1,0:T(2,128)S(1)}, u32[]{:S(2)}, u32[]{:S(2)}) async-start(f32[8,2,192]{2,1,0:T(2,128)} %local_sums.1), calls=%async_computation.3 | async-start | bytes 32768 | tf_op jit(solution)/shard_map/all_to_all | solution.py:867
  86.2 6.0 %copy-start.4 = (bf16[4,128,2,192]{1,3,2,0:T(8,128)(2,1)S(1)}, bf16[4,128,2,192]{1,3,2,0:T(8,128)(2,1)}, u32[]{:S(2)}) copy-start(bf16[4,128,2,192]{1,3,2,0:T(8,128)(2,1)} %param.4) | copy-start | bytes 1179652

commit v5 on v4

--- a/solution.py
+++ b/solution.py
@@ -759,10 +759,18 @@
     )(flags, stats, far(weights), tile, before)
 
 
-def decode_kernel(
-    w_hbm, before_ref, mid_ref, out_ref, main_ref, pair_ref, wide, weights, sems
-):
-    copies = fetch(w_hbm, weights, sems)
+def bring_kernel(x_hbm, out_ref, sem):
+    copy = pltpu.make_async_copy(x_hbm, out_ref, sem)
+    copy.start()
+    copy.wait()
+
+
+def brought(x):
+    scratch = [pltpu.SemaphoreType.DMA]
+    return near(call(bring_kernel, "bring", kept(x.shape), [anywhere()], scratch, 10**6)(far(x)))
+
+
+def decode_kernel(weights, before_ref, mid_ref, out_ref, main_ref, pair_ref, wide):
     frames, ext, cols, chans = mid_ref.shape
     lines, outs, _ = out_ref.shape[1:]
     rows = lines // 2
@@ -790,8 +798,6 @@
             here, aside = (jnp.zeros((size, 256), F32) for _ in range(2))
             tiles = []
             for dt in range(3):
-                if t + i == 0:
-                    copies[dt].wait()
                 at = slice(t + dt, t + dt + 2)
                 (dr, p), (below, q) = taps
                 for ref, row, parts in (
@@ -834,16 +840,14 @@
         decode_kernel,
         "decode",
         array((frames, 2 * rows, outs, 2 * cols)),
-        [anywhere()] + vmem(2),
+        vmem(3),
         [
             pltpu.VMEM((frames + 2, ext, cols, 128), BF16),
             pltpu.VMEM((frames + 2, ext, cols, 128), BF16),
             pltpu.VMEM((2, 2 * rows, 2 * cols, 128), F32),
-            pltpu.VMEM(weights.shape, BF16),
-            pltpu.SemaphoreType.DMA((3,)),
         ],
         2 * frames * rows * cols * 24 * 65536,
-    )(far(weights), before, mid)
+    )(weights, before, mid)
 
 
 def moved(block, clip_step, seq_step):
@@ -898,9 +902,10 @@
     home, stats = exchanged(blocks, "seq"), near(stats)
 
     mid, mid_last = middle(flags, stats, conv_one, tile, tile_z)
-    decoded = decode(both, moved(mid_last, 1, 0), near(mid), outs)
-
-    sums = exchanged(local_sums(home, frames, chans, clips), "clip")
+    sums, both = lax.optimization_barrier((local_sums(home, frames, chans, clips), both))
+    decoded = decode(brought(both), moved(mid_last, 1, 0), near(mid), outs)
+
+    sums = exchanged(sums, "clip")
     sums, decoded = lax.optimization_barrier((sums, decoded))
     count = held * seqs * clips * (chans // GROUPS)
     token_grad = token_gradient(home, tokens, stats, sums, count)

time: 95.1 us -> 94.6 us (level)
    pallas_call x0 -> x1, Pallas kernels: none -> 1.67 us  [brought(): call(bring_kernel, 'bring', kept(x.shape), [anywhere()], scratch, 10 ** 6)]
    pallas_call x1, Pallas kernels: 5.98 us -> 4.87 us  [decode(): call(decode_kernel, 'decode', array((frames, 2 * rows, outs, 2 * cols)),...]
  transfers between devices with their start and end apart: 9 -> 9, of which waited for: 5 -> 3; matrix products, arithmetic and copies ran while one was open for 0% -> 0% of each run, Pallas kernels for 43% -> 43%
where the time goes in v5:
time: 94.6 us; the launch traced here: 93.9 us
  Pallas kernels  44.2 us (47%)
  starting transfers between devices  37.6 us (40%)
  waiting for transfers between devices  10.1 us (11%)
  local copies, waits for them, and re-layouts  1.02 us (1%)
    all_to_all x4, starting transfers between devices, exchanged(): return lax.all_to_all(blocks, axis, 0, 0, tiled=True)  25.1 us
    all_to_all x4, waiting for transfers between devices, exchanged(): return lax.all_to_all(blocks, axis, 0, 0, tiled=True)  10.1 us
    pallas_call x1, Pallas kernels, back(): call(functools.partial(back_kernel, held), 'back', (pltpu.HBM((seqs, 12 *...  8.33 us
    pallas_call x1, Pallas kernels, middle(): call(mid_kernel, 'middle', (kept((frames, rows, cols, chans)), array((3,...  8.09 us
    pallas_call x1, Pallas kernels, down_early(): pl.pallas_call(functools.partial(early_kernel, plan), name='down_early',...  7.56 us
    ppermute x2, starting transfers between devices, moved(): return lax.ppermute(block, 'seq', route)  6.65 us
    ppermute x3, starting transfers between devices, moved(): return lax.ppermute(block, 'clip', route)  5.79 us
    pallas_call x1, Pallas kernels, decode(): call(decode_kernel, 'decode', array((frames, 2 * rows, outs, 2 * cols)),...  4.87 us
  transfers between devices with their start and end apart: 9, of which 3 were waited for; matrix products, arithmetic and copies ran while one was open for 0% of the time, Pallas kernels for 43%

profile of v5, /device:TPU:1, one launch (start us, length us, event | category | flops | bytes accessed | tf_op | source)
XLA Modules:
  0.0 93.9 jit_solution(15240404486000942531)
XLA Ops:
  0.6 1.8 %edges.1 = (bf16[4,3,96,128]{3,2,1,0:T(8,128)(2,1)}, bf16[4,3,96,128]{3,2,1,0:T(8,128)(2,1)}) custom-call(bf16[4,8,96,128]{3,2,1,0:T(8,128)(2,1)} %bitcast.7), custom_call_target="tpu_custom_call" | custom-call | flops 1000000 | bytes 1000000 | tf_op jit(solution)/shard_map/edges/pallas_call | solution.py:191
  2.4 0.0 copy-start.2
  2.5 4.7 %collective-permute-start = (bf16[4,3,96,128]{3,2,1,0:T(8,128)(2,1)}, bf16[4,3,96,128]{3,2,1,0:T(8,128)(2,1)S(1)}, u32[]{:S(2)}, u32[]{:S(2)}) collective-permute-start(bf16[4,3,96,128]{3,2,1,0:T(8,128)(2,1)} %get-tuple-element.22), channel_id=1, source_target_pairs={{0,8},{8,16},{16,24},{24,32},{32,40},{40,48},{48,56},{56,64},{64,7... | collective-permute-start | bytes 884744 | tf_op jit(solution)/shard_map/ppermute | solution.py:857
  7.2 1.9 %collective-permute-start.1 = (bf16[4,3,96,128]{3,2,1,0:T(8,128)(2,1)}, bf16[4,3,96,128]{3,2,1,0:T(8,128)(2,1)}, u32[]{:S(2)}, u32[]{:S(2)}) collective-permute-start(bf16[4,3,96,128]{3,2,1,0:T(8,128)(2,1)} %get-tuple-element.27), channel_id=1, source_target_pairs={{8,0},{16,8},{24,16},{32,24},{40,32},{48,40},{56,48},{64,56},{72,6... | collective-permute-start | bytes 884744 | tf_op jit(solution)/shard_map/ppermute | solution.py:857
  9.1 0.0 copy-start.3
  9.1 1.0 %copy-done.3 = bf16[4,128,2,192]{1,3,2,0:T(8,128)(2,1)S(1)} copy-done((bf16[4,128,2,192]{1,3,2,0:T(8,128)(2,1)S(1)}, bf16[4,128,2,192]{1,3,2,0:T(8,128)(2,1)}, u32[]{:S(2)}) %copy-start.3) | copy-done | bytes 393240
  10.1 1.4 %pack.1 = bf16[32,112,128]{2,1,0:T(8,128)(2,1)} custom-call(bf16[4,2,192,128]{3,2,1,0:T(8,128)(2,1)S(1)} %bitcast.10), custom_call_target="tpu_custom_call" | custom-call | flops 1000000000 | bytes 4194304 | tf_op jit(solution)/shard_map/pack/pallas_call | solution.py:250
  11.5 0.5 combine_weights.1.weights.x_hbm
  12.0 0.0 collective-permute-done.above
  12.1 7.7 %all-to-all-start = ((bf16[32,112,128]{2,1,0:T(8,128)(2,1)}), bf16[32,112,128]{2,1,0:T(8,128)(2,1)}, u32[]{:S(2)}, u32[]{:S(2)}) async-start(bf16[32,112,128]{2,1,0:T(8,128)(2,1)} %pack.1), calls=%async_computation | async-start | bytes 1835008 | tf_op jit(solution)/shard_map/all_to_all | solution.py:871
  19.8 0.1 add_convert_fusion.flags
  19.9 0.0 collective-permute-done.1.below
  19.9 7.6 %down_early.1.own_hbm = bf16[6,6,64,128]{3,2,1,0:T(8,128)(2,1)} custom-call(bf16[3,4,4,192,128]{4,3,2,1,0:T(8,128)(2,1)S(1)} %combine_weights.1.weights.x_hbm, f32[3]{0:T(128)S(1)} %add_convert_fusion.flags, bf16[4,8,96,128]{3,2,1,0:T(8,128)(2,1)S(1)} %bitcast.8, bf16[4,3,96,128]{3,2,1,0:T(8,128)(2,1)} %copy-done.5, ...), custom_call_target="tpu_custom_call" | custom-call | flops 4026531840 | bytes 4194304 | tf_op jit(solution)/shard_map/down_early/pallas_call | solution.py:426
  27.4 1.3 %collective-permute-start.2 = (bf16[6,6,64,128]{3,2,1,0:T(8,128)(2,1)}, bf16[6,6,64,128]{3,2,1,0:T(8,128)(2,1)}, u32[]{:S(2)}, u32[]{:S(2)}) collective-permute-start(bf16[6,6,64,128]{3,2,1,0:T(8,128)(2,1)} %down_early.1.own_hbm), channel_id=1, source_target_pairs={{1,0},{2,1},{3,2},{4,3},{5,4},{6,5},{7,6},{9,8},{10,9},{11,10},{12... | collective-permute-start | bytes 1769480 | tf_op jit(solution)/shard_map/ppermute | solution.py:860
  28.7 6.6 %all-to-all-done.x_ref = bf16[32,112,128]{2,1,0:T(8,128)(2,1)} async-done(((bf16[32,112,128]{2,1,0:T(8,128)(2,1)}), bf16[32,112,128]{2,1,0:T(8,128)(2,1)}, u32[]{:S(2)}, u32[]{:S(2)}) %all-to-all-start) | async-done | bytes 917536 | tf_op jit(solution)/shard_map/all_to_all | solution.py:871
  35.3 3.3 %unpack.1 = (bf16[4,8,64,192]{3,2,1,0:T(8,128)(2,1)}, bf16[2,8,64,192]{3,2,1,0:T(8,128)(2,1)}, f32[8,2,192]{2,1,0:T(2,128)}) custom-call(bf16[32,112,128]{2,1,0:T(8,128)(2,1)} %all-to-all-done.x_ref), custom_call_target="tpu_custom_call" | custom-call | flops 1000000000 | bytes 4194304 | tf_op jit(solution)/shard_map/unpack/pallas_call | solution.py:277
  38.6 8.2 %all-to-all-start.1 = ((f32[8,2,192]{2,1,0:T(2,128)}), f32[8,2,192]{2,1,0:T(2,128)S(1)}, u32[]{:S(2)}, u32[]{:S(2)}) async-start(f32[8,2,192]{2,1,0:T(2,128)} %get-tuple-element.24), calls=%async_computation.1 | async-start | bytes 32768 | tf_op jit(solution)/shard_map/all_to_all | solution.py:871
  46.8 4.4 %down_late.1.late_hbm = f32[2,6,64,192]{3,2,1,0:T(8,128)} custom-call(bf16[3,4,4,192,128]{4,3,2,1,0:T(8,128)(2,1)S(1)} %combine_weights.1.weights.x_hbm, f32[3]{0:T(128)S(1)} %add_convert_fusion.flags, bf16[4,8,96,128]{3,2,1,0:T(8,128)(2,1)S(1)} %bitcast.9, bf16[4,3,96,128]{3,2,1,0:T(8,128)(2,1)} %copy-done.5, ...), custom_call_target="tpu_custom_call" | custom-call | flops 1207959552 | bytes 4194304 | tf_op jit(solution)/shard_map/down_late/pallas_call | solution.py:447
  51.2 2.2 %all-to-all-done.1.parts_ref = f32[8,2,192]{2,1,0:T(2,128)S(1)} async-done(((f32[8,2,192]{2,1,0:T(2,128)}), f32[8,2,192]{2,1,0:T(2,128)S(1)}, u32[]{:S(2)}, u32[]{:S(2)}) %all-to-all-start.1) | async-done | bytes 12320 | tf_op jit(solution)/shard_map/all_to_all | solution.py:871
  53.4 2.3 %collective-permute-start.3 = (bf16[2,8,64,192]{3,2,1,0:T(8,128)(2,1)}, bf16[2,8,64,192]{3,2,1,0:T(8,128)(2,1)S(1)}, u32[]{:S(2)}, u32[]{:S(2)}) collective-permute-start(bf16[2,8,64,192]{3,2,1,0:T(8,128)(2,1)} %get-tuple-element.37), channel_id=1, source_target_pairs={{0,1},{1,2},{2,3},{3,4},{4,5},{5,6},{6,7},{8,9},{9,10},{10,11},{11... | collective-permute-start | bytes 1179656 | tf_op jit(solution)/shard_map/ppermute | solution.py:860
  55.8 8.3 %back.1 = (bf16[32,64,128]{2,1,0:T(8,128)(2,1)}, f32[2,192]{1,0:T(2,128)S(1)}) custom-call(f32[8,2,192]{2,1,0:T(2,128)S(1)} %all-to-all-done.1.parts_ref, bf16[3,3,3,192,192]{4,3,2,1,0:T(8,128)(2,1)} %w_hbm.3, bf16[4,8,64,192]{3,2,1,0:T(8,128)(2,1)} %get-tuple-element.31.tile_hbm, bf16[6,6,64,128]{3,2,1,0:T(8,128)(2,1)} %down_early.1.own_hbm, ...), custom_call_target="tpu_custom_call" | custom-call | flops 2818572288 | bytes 4194304 | tf_op jit(solution)/shard_map/back/pallas_call | solution.py:546
  64.1 5.9 %all-to-all-start.2 = ((bf16[32,64,128]{2,1,0:T(8,128)(2,1)}), bf16[32,64,128]{2,1,0:T(8,128)(2,1)S(1)}, u32[]{:S(2)}, u32[]{:S(2)}) async-start(bf16[32,64,128]{2,1,0:T(8,128)(2,1)} %get-tuple-element.33), calls=%async_computation.2 | async-start | bytes 1048576 | tf_op jit(solution)/shard_map/all_to_all | solution.py:871
  70.0 0.0 collective-permute-done.3.before_ref
  70.0 8.1 %middle.1 = (bf16[4,6,64,192]{3,2,1,0:T(8,128)(2,1)S(1)}, bf16[3,6,64,128]{3,2,1,0:T(8,128)(2,1)S(1)}) custom-call(f32[3]{0:T(128)S(1)} %add_convert_fusion.flags, f32[2,192]{1,0:T(2,128)S(1)} %get-tuple-element.36.stats.stats_ref, bf16[3,3,3,192,192]{4,3,2,1,0:T(8,128)(2,1)} %w_hbm.3, bf16[4,8,64,192]{3,2,1,0:T(8,128)(2,1)} %get-tuple-element.31.tile_hbm, ...), custom_call_target="tpu_custom_call" | custom-call | flops 5435817984 | bytes 4194304 | tf_op jit(solution)/shard_map/middle/pallas_call | solution.py:746
  78.1 2.1 %collective-permute-start.4 = (bf16[3,6,64,128]{3,2,1,0:T(8,128)(2,1)S(1)}, bf16[3,6,64,128]{3,2,1,0:T(8,128)(2,1)S(1)}, u32[]{:S(2)}, u32[]{:S(2)}) collective-permute-start(bf16[3,6,64,128]{3,2,1,0:T(8,128)(2,1)S(1)} %get-tuple-element.38), channel_id=1, source_target_pairs={{0,1},{1,2},{2,3},{3,4},{4,5},{5,6},{6,7},{8,9},{9,10},{10,11},{11... | collective-permute-start | bytes 884744 | tf_op jit(solution)/shard_map/ppermute | solution.py:860
  80.3 1.3 %all-to-all-done.2.x_ref = bf16[32,64,128]{2,1,0:T(8,128)(2,1)S(1)} async-done(((bf16[32,64,128]{2,1,0:T(8,128)(2,1)}), bf16[32,64,128]{2,1,0:T(8,128)(2,1)S(1)}, u32[]{:S(2)}, u32[]{:S(2)}) %all-to-all-start.2) | async-done | bytes 524320 | tf_op jit(solution)/shard_map/all_to_all | solution.py:871
  81.6 0.8 local_sums.1
  82.4 3.3 %all-to-all-start.3 = ((f32[8,2,192]{2,1,0:T(2,128)}), f32[8,2,192]{2,1,0:T(2,128)S(1)}, u32[]{:S(2)}, u32[]{:S(2)}) async-start(f32[8,2,192]{2,1,0:T(2,128)} %local_sums.1), calls=%async_computation.3 | async-start | bytes 32768 | tf_op jit(solution)/shard_map/all_to_all | solution.py:871
  85.7 1.7 %bring.1.weights = bf16[3,4,4,192,128]{4,3,2,1,0:T(8,128)(2,1)S(1)} custom-call(bf16[3,4,4,192,128]{4,3,2,1,0:T(8,128)(2,1)} %copy-done), custom_call_target="tpu_custom_call" | custom-call | flops 1000000 | bytes 4194304 | tf_op jit(solution)/shard_map/bring/pallas_call | solution.py:770
  87.4 0.0 copy-start.4
  87.4 4.9 %decode.1 = bf16[4,8,96,128]{3,2,1,0:T(8,128)(2,1)} custom-call(bf16[3,4,4,192,128]{4,3,2,1,0:T(8,128)(2,1)S(1)} %bring.1.weights, bf16[3,6,64,128]{3,2,1,0:T(8,128)(2,1)S(1)} %collective-permute-done.4.before_ref, bf16[4,6,64,192]{3,2,1,0:T(8,128)(2,1)S(1)} %get-tuple-element.39.mid_ref), custom_call_target="tpu_custom_call" | custom-call | flops 3221225472 | bytes 4194304 | tf_op jit(solution)/shard_map/decode/pallas_call | solution.py:839
  92.3 1.6 %token_gradient.1 = bf16[4,2,192,128]{3,2,1,0:T(8,128)(2,1)} custom-call(bf16[32,64,128]{2,1,0:T(8,128)(2,1)S(1)} %all-to-all-done.2.x_ref, bf16[4,2,192,128]{3,2,1,0:T(8,128)(2,1)S(1)} %bitcast.11, f32[2,192]{1,0:T(2,128)S(1)} %get-tuple-element.36.stats.stats_ref, f32[8,2,192]{2,1,0:T(2,128)S(1)} %all-to-all-done.3.parts_ref), custom_call_target="tpu_custom_call" | custom-call | flops 1000000000 | bytes 4194304 | tf_op jit(solution)/shard_map/token_gradient/pallas_call | solution.py:620
  (11 shorter events, 0.0 us)
Async XLA Ops:
  2.4 9.1 %copy-start.2 = (bf16[3,3,3,192,96]{4,3,2,1,0:T(8,128)(2,1)S(1)}, bf16[3,3,3,192,96]{4,3,2,1,0:T(8,128)(2,1)}, u32[]{:S(2)}) copy-start(bf16[3,3,3,192,96]{4,3,2,1,0:T(8,128)(2,1)} %w_ref.1) | copy-start | bytes 2985988
  2.5 9.6 %collective-permute-start = (bf16[4,3,96,128]{3,2,1,0:T(8,128)(2,1)}, bf16[4,3,96,128]{3,2,1,0:T(8,128)(2,1)S(1)}, u32[]{:S(2)}, u32[]{:S(2)}) collective-permute-start(bf16[4,3,96,128]{3,2,1,0:T(8,128)(2,1)} %get-tuple-element.22), channel_id=1, source_target_pairs={{0,8},{8,16},{16,24},{24,32},{32,40},{40,48},{48,56},{56,64},{64,7... | collective-permute-start | bytes 884744 | tf_op jit(solution)/shard_map/ppermute | solution.py:857
  7.2 12.7 %collective-permute-start.1 = (bf16[4,3,96,128]{3,2,1,0:T(8,128)(2,1)}, bf16[4,3,96,128]{3,2,1,0:T(8,128)(2,1)}, u32[]{:S(2)}, u32[]{:S(2)}) collective-permute-start(bf16[4,3,96,128]{3,2,1,0:T(8,128)(2,1)} %get-tuple-element.27), channel_id=1, source_target_pairs={{8,0},{16,8},{24,16},{32,24},{40,32},{48,40},{56,48},{64,56},{72,6... | collective-permute-start | bytes 884744 | tf_op jit(solution)/shard_map/ppermute | solution.py:857
  9.1 1.0 %copy-start.3 = (bf16[4,128,2,192]{1,3,2,0:T(8,128)(2,1)S(1)}, bf16[4,128,2,192]{1,3,2,0:T(8,128)(2,1)}, u32[]{:S(2)}) copy-start(bf16[4,128,2,192]{1,3,2,0:T(8,128)(2,1)} %param.4) | copy-start | bytes 1179652
  11.5 8.3 %copy-start.1 = (bf16[4,8,128,96]{2,3,1,0:T(8,128)(2,1)S(1)}, bf16[4,8,128,96]{2,3,1,0:T(8,128)(2,1)}, u32[]{:S(2)}) copy-start(bf16[4,8,128,96]{2,3,1,0:T(8,128)(2,1)} %param.7) | copy-start | bytes 2359300
  12.0 34.7 %copy-start = (bf16[3,4,4,192,128]{4,3,2,1,0:T(8,128)(2,1)}, bf16[3,4,4,192,128]{4,3,2,1,0:T(8,128)(2,1)S(1)}, u32[]{:S(2)}) copy-start(bf16[3,4,4,192,128]{4,3,2,1,0:T(8,128)(2,1)S(1)} %combine_weights.1.weights.x_hbm) | copy-start | bytes 7077892
  12.1 7.8 %copy-start.5 = (bf16[4,3,96,128]{3,2,1,0:T(8,128)(2,1)}, bf16[4,3,96,128]{3,2,1,0:T(8,128)(2,1)S(1)}, u32[]{:S(2)}) copy-start(bf16[4,3,96,128]{3,2,1,0:T(8,128)(2,1)S(1)} %collective-permute-done.above) | copy-start | bytes 884740
  12.1 23.2 %all-to-all-start = ((bf16[32,112,128]{2,1,0:T(8,128)(2,1)}), bf16[32,112,128]{2,1,0:T(8,128)(2,1)}, u32[]{:S(2)}, u32[]{:S(2)}) async-start(bf16[32,112,128]{2,1,0:T(8,128)(2,1)} %pack.1), calls=%async_computation | async-start | bytes 1835008 | tf_op jit(solution)/shard_map/all_to_all | solution.py:871
  27.4 28.3 %collective-permute-start.2 = (bf16[6,6,64,128]{3,2,1,0:T(8,128)(2,1)}, bf16[6,6,64,128]{3,2,1,0:T(8,128)(2,1)}, u32[]{:S(2)}, u32[]{:S(2)}) collective-permute-start(bf16[6,6,64,128]{3,2,1,0:T(8,128)(2,1)} %down_early.1.own_hbm), channel_id=1, source_target_pairs={{1,0},{2,1},{3,2},{4,3},{5,4},{6,5},{7,6},{9,8},{10,9},{11,10},{12... | collective-permute-start | bytes 1769480 | tf_op jit(solution)/shard_map/ppermute | solution.py:860
  38.6 14.8 %all-to-all-start.1 = ((f32[8,2,192]{2,1,0:T(2,128)}), f32[8,2,192]{2,1,0:T(2,128)S(1)}, u32[]{:S(2)}, u32[]{:S(2)}) async-start(f32[8,2,192]{2,1,0:T(2,128)} %get-tuple-element.24), calls=%async_computation.1 | async-start | bytes 32768 | tf_op jit(solution)/shard_map/all_to_all | solution.py:871
  53.4 16.6 %collective-permute-start.3 = (bf16[2,8,64,192]{3,2,1,0:T(8,128)(2,1)}, bf16[2,8,64,192]{3,2,1,0:T(8,128)(2,1)S(1)}, u32[]{:S(2)}, u32[]{:S(2)}) collective-permute-start(bf16[2,8,64,192]{3,2,1,0:T(8,128)(2,1)} %get-tuple-element.37), channel_id=1, source_target_pairs={{0,1},{1,2},{2,3},{3,4},{4,5},{5,6},{6,7},{8,9},{9,10},{10,11},{11... | collective-permute-start | bytes 1179656 | tf_op jit(solution)/shard_map/ppermute | solution.py:860
  64.1 17.5 %all-to-all-start.2 = ((bf16[32,64,128]{2,1,0:T(8,128)(2,1)}), bf16[32,64,128]{2,1,0:T(8,128)(2,1)S(1)}, u32[]{:S(2)}, u32[]{:S(2)}) async-start(bf16[32,64,128]{2,1,0:T(8,128)(2,1)} %get-tuple-element.33), calls=%async_computation.2 | async-start | bytes 1048576 | tf_op jit(solution)/shard_map/all_to_all | solution.py:871
  78.1 9.3 %collective-permute-start.4 = (bf16[3,6,64,128]{3,2,1,0:T(8,128)(2,1)S(1)}, bf16[3,6,64,128]{3,2,1,0:T(8,128)(2,1)S(1)}, u32[]{:S(2)}, u32[]{:S(2)}) collective-permute-start(bf16[3,6,64,128]{3,2,1,0:T(8,128)(2,1)S(1)} %get-tuple-element.38), channel_id=1, source_target_pairs={{0,1},{1,2},{2,3},{3,4},{4,5},{5,6},{6,7},{8,9},{9,10},{10,11},{11... | collective-permute-start | bytes 884744 | tf_op jit(solution)/shard_map/ppermute | solution.py:860
  82.4 9.9 %all-to-all-start.3 = ((f32[8,2,192]{2,1,0:T(2,128)}), f32[8,2,192]{2,1,0:T(2,128)S(1)}, u32[]{:S(2)}, u32[]{:S(2)}) async-start(f32[8,2,192]{2,1,0:T(2,128)} %local_sums.1), calls=%async_computation.3 | async-start | bytes 32768 | tf_op jit(solution)/shard_map/all_to_all | solution.py:871
  87.4 4.9 %copy-start.4 = (bf16[4,128,2,192]{1,3,2,0:T(8,128)(2,1)S(1)}, bf16[4,128,2,192]{1,3,2,0:T(8,128)(2,1)}, u32[]{:S(2)}) copy-start(bf16[4,128,2,192]{1,3,2,0:T(8,128)(2,1)} %param.4) | copy-start | bytes 1179652

commit v6 on v5

--- a/solution.py
+++ b/solution.py
@@ -171,35 +171,37 @@
     return call(combine_kernel, "combine_weights", shape, vmem(1), [], 10**6)(conv_two)
 
 
-def edges_kernel(x_hbm, first_hbm, last_hbm, near_ref, sems):
+def edges_kernel(x_hbm, tokens_hbm, first_hbm, last_hbm, tokens_ref, near_ref, sems, sem):
     lines = x_hbm.shape[1]
     ends = ((0, first_hbm), (lines - 3, last_hbm))
     for k, (at, _) in enumerate(ends):
         pltpu.make_async_copy(x_hbm.at[:, pl.ds(at, 3)], near_ref.at[k], sems.at[0, k]).start()
-    copies = []
+    copies = [pltpu.make_async_copy(tokens_hbm, tokens_ref, sem)]
+    copies[0].start()
     for k, (at, ref) in enumerate(ends):
         pltpu.make_async_copy(x_hbm.at[:, pl.ds(at, 3)], near_ref.at[k], sems.at[0, k]).wait()
         copies.append(pltpu.make_async_copy(near_ref.at[k], ref, sems.at[1, k]))
-        copies[k].start()
+        copies[k + 1].start()
     for copy in copies:
         copy.wait()
 
 
-def edges(pixels):
+def edges(pixels, tokens):
     frames, _, outs, wide = pixels.shape
     shape = pltpu.HBM((frames, 3, outs, wide), BF16)
     return pl.pallas_call(
         edges_kernel,
         name="edges",
-        out_shape=(shape, shape),
-        in_specs=[anywhere()],
-        out_specs=(anywhere(), anywhere()),
+        out_shape=(shape, shape, kept(tokens.shape)),
+        in_specs=[anywhere(), anywhere()],
+        out_specs=(anywhere(), anywhere(), *vmem(1)),
         scratch_shapes=[
             pltpu.VMEM((2, *shape.shape), BF16),
             pltpu.SemaphoreType.DMA((2, 2)),
+            pltpu.SemaphoreType.DMA,
         ],
         cost_estimate=pl.CostEstimate(flops=10**6, bytes_accessed=10**6, transcendentals=0),
-    )(far(pixels))
+    )(far(pixels), far(tokens))
 
 
 def own_moments(x_ref):
@@ -882,9 +884,9 @@
     pixels = pixel_grad.transpose(0, 1, 3, 2)
     held = float(frames * height * stripe)
 
-    first, last = edges(pixels)
+    first, last, near_tokens = edges(pixels, tokens)
     above, below = moved(last, 0, 1), moved(first, 0, -1)
-    packed = pack(tokens, seqs)
+    packed = pack(near(near_tokens), seqs)
     both = combined_weights(conv_two)
     above, both, packed = lax.optimization_barrier((above, both, packed))
 

time: 94.6 us -> 94.3 us (level)
  local copies, waits for them, and re-layouts: 1.02 us -> 0.02 us
    unnamed x12 -> x10, local copies, waits for them, and re-layouts: 1.02 us -> 0.02 us
  transfers between devices with their start and end apart: 9 -> 9, of which waited for: 3 -> 4; matrix products, arithmetic and copies ran while one was open for 0% -> 0% of each run, Pallas kernels for 43% -> 44%
where the time goes in v6:
time: 94.3 us; the launch traced here: 93.6 us
  Pallas kernels  44.3 us (47%)
  starting transfers between devices  38.2 us (41%)
  waiting for transfers between devices  10.3 us (11%)
    all_to_all x4, starting transfers between devices, exchanged(): return lax.all_to_all(blocks, axis, 0, 0, tiled=True)  25.7 us
    all_to_all x4, waiting for transfers between devices, exchanged(): return lax.all_to_all(blocks, axis, 0, 0, tiled=True)  10.1 us
    pallas_call x1, Pallas kernels, back(): call(functools.partial(back_kernel, held), 'back', (pltpu.HBM((seqs, 12 *...  8.34 us
    pallas_call x1, Pallas kernels, middle(): call(mid_kernel, 'middle', (kept((frames, rows, cols, chans)), array((3,...  8.09 us
    pallas_call x1, Pallas kernels, down_early(): pl.pallas_call(functools.partial(early_kernel, plan), name='down_early',...  7.54 us
    ppermute x2, starting transfers between devices, moved(): return lax.ppermute(block, 'seq', route)  6.65 us
    ppermute x3, starting transfers between devices, moved(): return lax.ppermute(block, 'clip', route)  5.78 us
    pallas_call x1, Pallas kernels, decode(): call(decode_kernel, 'decode', array((frames, 2 * rows, outs, 2 * cols)),...  4.87 us
  transfers between devices with their start and end apart: 9, of which 4 were waited for; matrix products, arithmetic and copies ran while one was open for 0% of the time, Pallas kernels for 44%

profile of v6, /device:TPU:1, one launch (start us, length us, event | category | flops | bytes accessed | tf_op | source)
XLA Modules:
  0.0 93.6 jit_solution(7975803871884978339)
XLA Ops:
  0.6 1.8 %edges.1 = (bf16[4,3,96,128]{3,2,1,0:T(8,128)(2,1)}, bf16[4,3,96,128]{3,2,1,0:T(8,128)(2,1)}, bf16[4,2,192,128]{3,2,1,0:T(8,128)(2,1)S(1)}) custom-call(bf16[4,8,96,128]{3,2,1,0:T(8,128)(2,1)} %bitcast.7, bf16[4,2,192,128]{3,2,1,0:T(8,128)(2,1)} %bitcast.10), custom_call_target="tpu_custom_call" | custom-call | flops 1000000 | bytes 1000000 | tf_op jit(solution)/shard_map/edges/pallas_call | solution.py:192
  2.5 0.0 copy-start.2
  2.5 4.7 %collective-permute-start = (bf16[4,3,96,128]{3,2,1,0:T(8,128)(2,1)}, bf16[4,3,96,128]{3,2,1,0:T(8,128)(2,1)S(1)}, u32[]{:S(2)}, u32[]{:S(2)}) collective-permute-start(bf16[4,3,96,128]{3,2,1,0:T(8,128)(2,1)} %get-tuple-element.23), channel_id=1, source_target_pairs={{0,8},{8,16},{16,24},{24,32},{32,40},{40,48},{48,56},{56,64},{64,7... | collective-permute-start | bytes 884744 | tf_op jit(solution)/shard_map/ppermute | solution.py:859
  7.2 1.9 %collective-permute-start.1 = (bf16[4,3,96,128]{3,2,1,0:T(8,128)(2,1)}, bf16[4,3,96,128]{3,2,1,0:T(8,128)(2,1)}, u32[]{:S(2)}, u32[]{:S(2)}) collective-permute-start(bf16[4,3,96,128]{3,2,1,0:T(8,128)(2,1)} %get-tuple-element.29), channel_id=1, source_target_pairs={{8,0},{16,8},{24,16},{32,24},{40,32},{48,40},{56,48},{64,56},{72,6... | collective-permute-start | bytes 884744 | tf_op jit(solution)/shard_map/ppermute | solution.py:859
  9.1 1.4 %pack.1 = bf16[32,112,128]{2,1,0:T(8,128)(2,1)} custom-call(bf16[4,2,192,128]{3,2,1,0:T(8,128)(2,1)S(1)} %get-tuple-element.24.x_ref), custom_call_target="tpu_custom_call" | custom-call | flops 1000000000 | bytes 4194304 | tf_op jit(solution)/shard_map/pack/pallas_call | solution.py:252
  10.6 0.5 combine_weights.1.weights.x_hbm
  11.1 0.1 collective-permute-done.above
  11.2 8.3 %all-to-all-start = ((bf16[32,112,128]{2,1,0:T(8,128)(2,1)}), bf16[32,112,128]{2,1,0:T(8,128)(2,1)}, u32[]{:S(2)}, u32[]{:S(2)}) async-start(bf16[32,112,128]{2,1,0:T(8,128)(2,1)} %pack.1), calls=%async_computation | async-start | bytes 1835008 | tf_op jit(solution)/shard_map/all_to_all | solution.py:873
  19.5 0.1 add_convert_fusion.flags
  19.6 0.0 collective-permute-done.1.below
  19.6 7.5 %down_early.1.own_hbm = bf16[6,6,64,128]{3,2,1,0:T(8,128)(2,1)} custom-call(bf16[3,4,4,192,128]{4,3,2,1,0:T(8,128)(2,1)S(1)} %combine_weights.1.weights.x_hbm, f32[3]{0:T(128)S(1)} %add_convert_fusion.flags, bf16[4,8,96,128]{3,2,1,0:T(8,128)(2,1)S(1)} %bitcast.8, bf16[4,3,96,128]{3,2,1,0:T(8,128)(2,1)} %copy-done.4, ...), custom_call_target="tpu_custom_call" | custom-call | flops 4026531840 | bytes 4194304 | tf_op jit(solution)/shard_map/down_early/pallas_call | solution.py:428
  27.1 1.3 %collective-permute-start.2 = (bf16[6,6,64,128]{3,2,1,0:T(8,128)(2,1)}, bf16[6,6,64,128]{3,2,1,0:T(8,128)(2,1)}, u32[]{:S(2)}, u32[]{:S(2)}) collective-permute-start(bf16[6,6,64,128]{3,2,1,0:T(8,128)(2,1)} %down_early.1.own_hbm), channel_id=1, source_target_pairs={{1,0},{2,1},{3,2},{4,3},{5,4},{6,5},{7,6},{9,8},{10,9},{11,10},{12... | collective-permute-start | bytes 1769480 | tf_op jit(solution)/shard_map/ppermute | solution.py:862
  28.4 6.6 %all-to-all-done.x_ref = bf16[32,112,128]{2,1,0:T(8,128)(2,1)} async-done(((bf16[32,112,128]{2,1,0:T(8,128)(2,1)}), bf16[32,112,128]{2,1,0:T(8,128)(2,1)}, u32[]{:S(2)}, u32[]{:S(2)}) %all-to-all-start) | async-done | bytes 917536 | tf_op jit(solution)/shard_map/all_to_all | solution.py:873
  35.0 3.3 %unpack.1 = (bf16[4,8,64,192]{3,2,1,0:T(8,128)(2,1)}, bf16[2,8,64,192]{3,2,1,0:T(8,128)(2,1)}, f32[8,2,192]{2,1,0:T(2,128)}) custom-call(bf16[32,112,128]{2,1,0:T(8,128)(2,1)} %all-to-all-done.x_ref), custom_call_target="tpu_custom_call" | custom-call | flops 1000000000 | bytes 4194304 | tf_op jit(solution)/shard_map/unpack/pallas_call | solution.py:279
  38.3 8.2 %all-to-all-start.1 = ((f32[8,2,192]{2,1,0:T(2,128)}), f32[8,2,192]{2,1,0:T(2,128)S(1)}, u32[]{:S(2)}, u32[]{:S(2)}) async-start(f32[8,2,192]{2,1,0:T(2,128)} %get-tuple-element.26), calls=%async_computation.1 | async-start | bytes 32768 | tf_op jit(solution)/shard_map/all_to_all | solution.py:873
  46.5 4.4 %down_late.1.late_hbm = f32[2,6,64,192]{3,2,1,0:T(8,128)} custom-call(bf16[3,4,4,192,128]{4,3,2,1,0:T(8,128)(2,1)S(1)} %combine_weights.1.weights.x_hbm, f32[3]{0:T(128)S(1)} %add_convert_fusion.flags, bf16[4,8,96,128]{3,2,1,0:T(8,128)(2,1)S(1)} %bitcast.9, bf16[4,3,96,128]{3,2,1,0:T(8,128)(2,1)} %copy-done.4, ...), custom_call_target="tpu_custom_call" | custom-call | flops 1207959552 | bytes 4194304 | tf_op jit(solution)/shard_map/down_late/pallas_call | solution.py:449
  50.9 2.2 %all-to-all-done.1.parts_ref = f32[8,2,192]{2,1,0:T(2,128)S(1)} async-done(((f32[8,2,192]{2,1,0:T(2,128)}), f32[8,2,192]{2,1,0:T(2,128)S(1)}, u32[]{:S(2)}, u32[]{:S(2)}) %all-to-all-start.1) | async-done | bytes 12320 | tf_op jit(solution)/shard_map/all_to_all | solution.py:873
  53.1 2.3 %collective-permute-start.3 = (bf16[2,8,64,192]{3,2,1,0:T(8,128)(2,1)}, bf16[2,8,64,192]{3,2,1,0:T(8,128)(2,1)S(1)}, u32[]{:S(2)}, u32[]{:S(2)}) collective-permute-start(bf16[2,8,64,192]{3,2,1,0:T(8,128)(2,1)} %get-tuple-element.39), channel_id=1, source_target_pairs={{0,1},{1,2},{2,3},{3,4},{4,5},{5,6},{6,7},{8,9},{9,10},{10,11},{11... | collective-permute-start | bytes 1179656 | tf_op jit(solution)/shard_map/ppermute | solution.py:862
  55.5 0.0 collective-permute-done.2.next_hbm
  55.5 8.3 %back.1 = (bf16[32,64,128]{2,1,0:T(8,128)(2,1)}, f32[2,192]{1,0:T(2,128)S(1)}) custom-call(f32[8,2,192]{2,1,0:T(2,128)S(1)} %all-to-all-done.1.parts_ref, bf16[3,3,3,192,192]{4,3,2,1,0:T(8,128)(2,1)} %w_hbm.3, bf16[4,8,64,192]{3,2,1,0:T(8,128)(2,1)} %get-tuple-element.33.tile_hbm, bf16[6,6,64,128]{3,2,1,0:T(8,128)(2,1)} %down_early.1.own_hbm, ...), custom_call_target="tpu_custom_call" | custom-call | flops 2818572288 | bytes 4194304 | tf_op jit(solution)/shard_map/back/pallas_call | solution.py:548
  63.8 5.9 %all-to-all-start.2 = ((bf16[32,64,128]{2,1,0:T(8,128)(2,1)}), bf16[32,64,128]{2,1,0:T(8,128)(2,1)S(1)}, u32[]{:S(2)}, u32[]{:S(2)}) async-start(bf16[32,64,128]{2,1,0:T(8,128)(2,1)} %get-tuple-element.35), calls=%async_computation.2 | async-start | bytes 1048576 | tf_op jit(solution)/shard_map/all_to_all | solution.py:873
  69.7 0.0 collective-permute-done.3.before_ref
  69.7 8.1 %middle.1 = (bf16[4,6,64,192]{3,2,1,0:T(8,128)(2,1)S(1)}, bf16[3,6,64,128]{3,2,1,0:T(8,128)(2,1)S(1)}) custom-call(f32[3]{0:T(128)S(1)} %add_convert_fusion.flags, f32[2,192]{1,0:T(2,128)S(1)} %get-tuple-element.38.stats.stats_ref, bf16[3,3,3,192,192]{4,3,2,1,0:T(8,128)(2,1)} %w_hbm.3, bf16[4,8,64,192]{3,2,1,0:T(8,128)(2,1)} %get-tuple-element.33.tile_hbm, ...), custom_call_target="tpu_custom_call" | custom-call | flops 5435817984 | bytes 4194304 | tf_op jit(solution)/shard_map/middle/pallas_call | solution.py:748
  77.8 2.2 %collective-permute-start.4 = (bf16[3,6,64,128]{3,2,1,0:T(8,128)(2,1)S(1)}, bf16[3,6,64,128]{3,2,1,0:T(8,128)(2,1)S(1)}, u32[]{:S(2)}, u32[]{:S(2)}) collective-permute-start(bf16[3,6,64,128]{3,2,1,0:T(8,128)(2,1)S(1)} %get-tuple-element.40), channel_id=1, source_target_pairs={{0,1},{1,2},{2,3},{3,4},{4,5},{5,6},{6,7},{8,9},{9,10},{10,11},{11... | collective-permute-start | bytes 884744 | tf_op jit(solution)/shard_map/ppermute | solution.py:862
  80.0 1.3 %all-to-all-done.2.x_ref = bf16[32,64,128]{2,1,0:T(8,128)(2,1)S(1)} async-done(((bf16[32,64,128]{2,1,0:T(8,128)(2,1)}), bf16[32,64,128]{2,1,0:T(8,128)(2,1)S(1)}, u32[]{:S(2)}, u32[]{:S(2)}) %all-to-all-start.2) | async-done | bytes 524320 | tf_op jit(solution)/shard_map/all_to_all | solution.py:873
  81.3 0.8 local_sums.1
  82.1 3.3 %all-to-all-start.3 = ((f32[8,2,192]{2,1,0:T(2,128)}), f32[8,2,192]{2,1,0:T(2,128)S(1)}, u32[]{:S(2)}, u32[]{:S(2)}) async-start(f32[8,2,192]{2,1,0:T(2,128)} %local_sums.1), calls=%async_computation.3 | async-start | bytes 32768 | tf_op jit(solution)/shard_map/all_to_all | solution.py:873
  85.4 1.7 %bring.1.weights = bf16[3,4,4,192,128]{4,3,2,1,0:T(8,128)(2,1)S(1)} custom-call(bf16[3,4,4,192,128]{4,3,2,1,0:T(8,128)(2,1)} %copy-done), custom_call_target="tpu_custom_call" | custom-call | flops 1000000 | bytes 4194304 | tf_op jit(solution)/shard_map/bring/pallas_call | solution.py:772
  87.1 0.0 copy-start.3
  87.2 4.9 %decode.1 = bf16[4,8,96,128]{3,2,1,0:T(8,128)(2,1)} custom-call(bf16[3,4,4,192,128]{4,3,2,1,0:T(8,128)(2,1)S(1)} %bring.1.weights, bf16[3,6,64,128]{3,2,1,0:T(8,128)(2,1)S(1)} %collective-permute-done.4.before_ref, bf16[4,6,64,192]{3,2,1,0:T(8,128)(2,1)S(1)} %get-tuple-element.41.mid_ref), custom_call_target="tpu_custom_call" | custom-call | flops 3221225472 | bytes 4194304 | tf_op jit(solution)/shard_map/decode/pallas_call | solution.py:841
  92.0 0.0 all-to-all-done.3.parts_ref
  92.0 1.6 %token_gradient.1 = bf16[4,2,192,128]{3,2,1,0:T(8,128)(2,1)} custom-call(bf16[32,64,128]{2,1,0:T(8,128)(2,1)S(1)} %all-to-all-done.2.x_ref, bf16[4,2,192,128]{3,2,1,0:T(8,128)(2,1)S(1)} %bitcast.11, f32[2,192]{1,0:T(2,128)S(1)} %get-tuple-element.38.stats.stats_ref, f32[8,2,192]{2,1,0:T(2,128)S(1)} %all-to-all-done.3.parts_ref), custom_call_target="tpu_custom_call" | custom-call | flops 1000000000 | bytes 4194304 | tf_op jit(solution)/shard_map/token_gradient/pallas_call | solution.py:622
  (9 shorter events, 0.0 us)
Async XLA Ops:
  2.5 8.1 %copy-start.2 = (bf16[3,3,3,192,96]{4,3,2,1,0:T(8,128)(2,1)S(1)}, bf16[3,3,3,192,96]{4,3,2,1,0:T(8,128)(2,1)}, u32[]{:S(2)}) copy-start(bf16[3,3,3,192,96]{4,3,2,1,0:T(8,128)(2,1)} %w_ref.1) | copy-start | bytes 2985988
  2.5 8.7 %collective-permute-start = (bf16[4,3,96,128]{3,2,1,0:T(8,128)(2,1)}, bf16[4,3,96,128]{3,2,1,0:T(8,128)(2,1)S(1)}, u32[]{:S(2)}, u32[]{:S(2)}) collective-permute-start(bf16[4,3,96,128]{3,2,1,0:T(8,128)(2,1)} %get-tuple-element.23), channel_id=1, source_target_pairs={{0,8},{8,16},{16,24},{24,32},{32,40},{40,48},{48,56},{56,64},{64,7... | collective-permute-start | bytes 884744 | tf_op jit(solution)/shard_map/ppermute | solution.py:859
  7.2 12.4 %collective-permute-start.1 = (bf16[4,3,96,128]{3,2,1,0:T(8,128)(2,1)}, bf16[4,3,96,128]{3,2,1,0:T(8,128)(2,1)}, u32[]{:S(2)}, u32[]{:S(2)}) collective-permute-start(bf16[4,3,96,128]{3,2,1,0:T(8,128)(2,1)} %get-tuple-element.29), channel_id=1, source_target_pairs={{8,0},{16,8},{24,16},{32,24},{40,32},{48,40},{56,48},{64,56},{72,6... | collective-permute-start | bytes 884744 | tf_op jit(solution)/shard_map/ppermute | solution.py:859
  10.6 9.0 %copy-start.1 = (bf16[4,8,128,96]{2,3,1,0:T(8,128)(2,1)S(1)}, bf16[4,8,128,96]{2,3,1,0:T(8,128)(2,1)}, u32[]{:S(2)}) copy-start(bf16[4,8,128,96]{2,3,1,0:T(8,128)(2,1)} %param.7) | copy-start | bytes 2359300
  11.1 35.5 %copy-start = (bf16[3,4,4,192,128]{4,3,2,1,0:T(8,128)(2,1)}, bf16[3,4,4,192,128]{4,3,2,1,0:T(8,128)(2,1)S(1)}, u32[]{:S(2)}) copy-start(bf16[3,4,4,192,128]{4,3,2,1,0:T(8,128)(2,1)S(1)} %combine_weights.1.weights.x_hbm) | copy-start | bytes 7077892
  11.2 8.4 %copy-start.4 = (bf16[4,3,96,128]{3,2,1,0:T(8,128)(2,1)}, bf16[4,3,96,128]{3,2,1,0:T(8,128)(2,1)S(1)}, u32[]{:S(2)}) copy-start(bf16[4,3,96,128]{3,2,1,0:T(8,128)(2,1)S(1)} %collective-permute-done.above) | copy-start | bytes 884740
  11.2 23.9 %all-to-all-start = ((bf16[32,112,128]{2,1,0:T(8,128)(2,1)}), bf16[32,112,128]{2,1,0:T(8,128)(2,1)}, u32[]{:S(2)}, u32[]{:S(2)}) async-start(bf16[32,112,128]{2,1,0:T(8,128)(2,1)} %pack.1), calls=%async_computation | async-start | bytes 1835008 | tf_op jit(solution)/shard_map/all_to_all | solution.py:873
  27.1 28.4 %collective-permute-start.2 = (bf16[6,6,64,128]{3,2,1,0:T(8,128)(2,1)}, bf16[6,6,64,128]{3,2,1,0:T(8,128)(2,1)}, u32[]{:S(2)}, u32[]{:S(2)}) collective-permute-start(bf16[6,6,64,128]{3,2,1,0:T(8,128)(2,1)} %down_early.1.own_hbm), channel_id=1, source_target_pairs={{1,0},{2,1},{3,2},{4,3},{5,4},{6,5},{7,6},{9,8},{10,9},{11,10},{12... | collective-permute-start | bytes 1769480 | tf_op jit(solution)/shard_map/ppermute | solution.py:862
  38.3 14.8 %all-to-all-start.1 = ((f32[8,2,192]{2,1,0:T(2,128)}), f32[8,2,192]{2,1,0:T(2,128)S(1)}, u32[]{:S(2)}, u32[]{:S(2)}) async-start(f32[8,2,192]{2,1,0:T(2,128)} %get-tuple-element.26), calls=%async_computation.1 | async-start | bytes 32768 | tf_op jit(solution)/shard_map/all_to_all | solution.py:873
  53.1 16.6 %collective-permute-start.3 = (bf16[2,8,64,192]{3,2,1,0:T(8,128)(2,1)}, bf16[2,8,64,192]{3,2,1,0:T(8,128)(2,1)S(1)}, u32[]{:S(2)}, u32[]{:S(2)}) collective-permute-start(bf16[2,8,64,192]{3,2,1,0:T(8,128)(2,1)} %get-tuple-element.39), channel_id=1, source_target_pairs={{0,1},{1,2},{2,3},{3,4},{4,5},{5,6},{6,7},{8,9},{9,10},{10,11},{11... | collective-permute-start | bytes 1179656 | tf_op jit(solution)/shard_map/ppermute | solution.py:862
  63.8 17.5 %all-to-all-start.2 = ((bf16[32,64,128]{2,1,0:T(8,128)(2,1)}), bf16[32,64,128]{2,1,0:T(8,128)(2,1)S(1)}, u32[]{:S(2)}, u32[]{:S(2)}) async-start(bf16[32,64,128]{2,1,0:T(8,128)(2,1)} %get-tuple-element.35), calls=%async_computation.2 | async-start | bytes 1048576 | tf_op jit(solution)/shard_map/all_to_all | solution.py:873
  77.8 9.3 %collective-permute-start.4 = (bf16[3,6,64,128]{3,2,1,0:T(8,128)(2,1)S(1)}, bf16[3,6,64,128]{3,2,1,0:T(8,128)(2,1)S(1)}, u32[]{:S(2)}, u32[]{:S(2)}) collective-permute-start(bf16[3,6,64,128]{3,2,1,0:T(8,128)(2,1)S(1)} %get-tuple-element.40), channel_id=1, source_target_pairs={{0,1},{1,2},{2,3},{3,4},{4,5},{5,6},{6,7},{8,9},{9,10},{10,11},{11... | collective-permute-start | bytes 884744 | tf_op jit(solution)/shard_map/ppermute | solution.py:862
  82.1 9.9 %all-to-all-start.3 = ((f32[8,2,192]{2,1,0:T(2,128)}), f32[8,2,192]{2,1,0:T(2,128)S(1)}, u32[]{:S(2)}, u32[]{:S(2)}) async-start(f32[8,2,192]{2,1,0:T(2,128)} %local_sums.1), calls=%async_computation.3 | async-start | bytes 32768 | tf_op jit(solution)/shard_map/all_to_all | solution.py:873
  87.1 4.9 %copy-start.3 = (bf16[4,128,2,192]{1,3,2,0:T(8,128)(2,1)S(1)}, bf16[4,128,2,192]{1,3,2,0:T(8,128)(2,1)}, u32[]{:S(2)}) copy-start(bf16[4,128,2,192]{1,3,2,0:T(8,128)(2,1)} %param.4) | copy-start | bytes 1179652
